TPU v7x, 32 devices: a whole 2x2x4 slice. The times are simulated.
32 devices in a mesh: dom: 8 (over z, x), sub: 4 (over y, core).
Axes of the slice: x: 2, y: 2, z: 4, core: 2. Of those that a mesh axis runs over, the one named last changes fastest.
Arguments:
- adjoint_field: float32 [4096, 5, 512], P(('dom', 'sub')), may hold values from -6 to 6
- metric: float32 [4096, 3, 512], P(('dom', 'sub')), may hold values from 0.5 to 4
- velocity: float32 [4096, 3, 512], P(('dom', 'sub')), may hold values from -2 to 2
- mortar_route: int32 [4096, 1], P(('dom', 'sub')), may hold values from 0 to 7, as said below
- mortar_element: int32 [4096, 1], P(('dom', 'sub')), may hold values from 0 to 127
- face_code: int32 [4096, 1], P(('dom', 'sub')), may hold values from 0 to 7
- hanging: int32 [4096, 1], P(('dom', 'sub')), may hold values 0 or 1
Outputs:
- result: float32 [4096, 5, 512], P(('dom', 'sub'))
Inputs may be any that keep to these rules, and one draw needn't show every extreme that they name: `mortar_route`: each element's value is its own device's dom index d or one of d - 2, d - 1, d + 1, d + 2 taken modulo 8. In each aligned block of 128 rows (the elements of one device) no value is named by more than 96 rows, and some value by exactly 96.
All inputs are finite; a program needn't handle non-finite values. No bound on the sum of `hanging` on one device may be relied on, other than what follows from the above.
Results may differ from a plain program's by a relative error of at most 0.00088.
Values may be sent and summed in bfloat16 or wider, within the bound.
No kernel may reach another device: no remote copies, remote signals or barrier semaphores. Data moves between devices by JAX's collectives and lax.ppermute only.
A program may use at most 64 MiB of HBM per device.

v0:
```python
import jax
import jax.numpy as jnp
import ml_dtypes
import numpy as np
from jax import lax
from jax.experimental import pallas as pl
from jax.experimental.pallas import tpu as pltpu
from jax.sharding import PartitionSpec as P

gll_nodes = np.array(
    [
        -1.0,
        -0.8717401485096066,
        -0.5917001814331423,
        -0.2092992179024789,
        0.2092992179024789,
        0.5917001814331423,
        0.8717401485096066,
        1.0,
    ]
)
viscosity = 0.005
F32, BF16 = jnp.float32, jnp.bfloat16
E = 128
HBM = pl.BlockSpec(memory_space=pltpu.HBM)
VM = pl.BlockSpec(memory_space=pltpu.VMEM)
LIMIT = 32 * 1024 * 1024
WHOLE = 64 * 1024 * 1024


def legendre_seven(points):
    prev = np.ones(points.shape)
    curr = np.array(points)
    for order in range(1, 7):
        nxt = ((2 * order + 1) * points * curr - order * prev) / (order + 1)
        prev, curr = (curr, nxt)
    return curr


def diff_matrix():
    values = legendre_seven(gll_nodes)
    result_mat = np.zeros((8, 8))
    for row in range(8):
        for col in range(8):
            if row != col:
                result_mat[row, col] = values[row] / (
                    values[col] * (gll_nodes[row] - gll_nodes[col])
                )
    result_mat[0, 0] = -14.0
    result_mat[7, 7] = 14.0
    return result_mat


def lagrange_at(points):
    basis = np.ones((8, 8))
    for row in range(8):
        for col in range(8):
            for other in range(8):
                if other != col:
                    basis[row, col] *= (points[row] - gll_nodes[other]) / (
                        gll_nodes[col] - gll_nodes[other]
                    )
    return basis


def face_tables():
    halves = [lagrange_at((gll_nodes - 1.0) / 2.0), lagrange_at((gll_nodes + 1.0) / 2.0)]
    perm_mat = np.zeros((64, 64))
    for col in range(64):
        perm_mat[col % 8 * 8 + col // 8, col] = 1.0
    tables = []
    for code in range(8):
        mat = np.kron(halves[code % 2], halves[code // 2 % 2])
        if code >= 4:
            mat = mat @ perm_mat
        tables.append(mat)
    return np.stack(tables)


def two_parts(mat):
    high = mat.astype(ml_dtypes.bfloat16)
    low = (mat - high.astype(np.float64)).astype(ml_dtypes.bfloat16)
    return high, low


def constants():
    dmat = diff_matrix()
    eye = np.eye(8)
    along_j = np.kron(np.eye(2), np.kron(dmat, eye))
    along_k = np.kron(np.eye(16), dmat)

    def forward(first, second):
        fh, fl = two_parts(viscosity * first.T)
        sh, sl = two_parts(viscosity * second.T)
        top = np.concatenate([fh, sh], 1)
        return np.concatenate([top, top], 0), np.concatenate([fl, sl], 1)

    def backward(first, second):
        fh, fl = two_parts(first)
        sh, sl = two_parts(second)
        return (
            np.concatenate([np.concatenate([fh, fl], 1), np.concatenate([sh, sl], 1)], 0),
            np.concatenate([fh, sh], 0),
        )

    def split_parity(mat):
        vectors = []
        for sign in (1.0, -1.0):
            small = (mat[:4, :4] + sign * mat[:4, ::-1][:, :4]) / 2
            for c in range(2):
                for other in range(2):
                    for swap in (0, 1):
                        vectors.append(
                            np.concatenate(
                                [
                                    np.full(64, small[2 * c + h, 2 * other + (h ^ swap)])
                                    for h in range(2)
                                ]
                            )
                        )
        return np.stack(vectors)

    coef = np.concatenate([split_parity(viscosity * dmat), split_parity(dmat.T)], 0)
    column = np.tile(np.repeat(viscosity * dmat[:, 0], 8), 2)[None]
    ends = [
        np.repeat(viscosity * dmat[2 * c : 2 * c + 2, end], 64)[None]
        for end in (0, 7)
        for c in range(4)
    ]
    coef = np.concatenate([coef, column, *ends, np.zeros((7, 128))], 0).astype(np.float32)

    tables = face_tables()
    fold = np.zeros((256, 512), ml_dtypes.bfloat16)
    for code in range(8):
        high, low = two_parts(tables[code])
        for i in range(8):
            for k in range(8):
                c, h = i // 2, i % 2
                spot = (56 + 64 * h + 16 * c + k) % 128
                cols = slice(64 * code, 64 * code + 64)
                fold[spot, cols] = high[8 * i + k]
                fold[(spot + 8) % 128, cols] = high[8 * i + k]
                fold[128 + spot, cols] = low[8 * i + k]

    spread = np.zeros((64, 512))
    place = np.zeros((64, 512))
    for i in range(8):
        for k in range(8):
            place[8 * i + k, 64 * i + k] = 1.0
            for j in range(8):
                spread[8 * i + k, 64 * i + 8 * j + k] = 1.0
    zero = np.zeros((64, 512))

    def pair(mat):
        one = np.concatenate(
            [np.concatenate([mat, zero], 1), np.concatenate([zero, mat], 1)], 0
        )
        return np.concatenate([one, one], 0).astype(ml_dtypes.bfloat16)

    return {
        "fold": fold,
        "forward": forward(along_j, along_k),
        "backward": backward(along_j, along_k),
        "spread": pair(spread),
        "place": pair(place),
        "coef": coef,
    }


def iota(dim, shape=(E, 128)):
    return lax.broadcasted_iota(jnp.int32, shape, dim)


def down(row):
    spots = jnp.where(iota(0) == iota(1), row, 0).astype(F32).astype(BF16)
    return jnp.dot(spots, jnp.ones((E, 128), BF16), preferred_element_type=F32)


def dot(a, b):
    return jnp.dot(a, b, preferred_element_type=F32)


def parts_of(x):
    high = x.astype(BF16)
    return high, (x - high.astype(F32)).astype(BF16)


def fetch(pairs, sems):
    copies = [
        pltpu.make_async_copy(src, dst, sems.at[n]) for n, (src, dst) in enumerate(pairs)
    ]
    for copy in copies:
        copy.start()
    return copies


def fold_kernel(
    route_hbm, target_hbm, code_hbm, hang_hbm, adj_hbm, fold_hbm, *refs
):
    outs, edges_out, marks_out, ints, x, fold, wide, sems = refs[:5], *refs[5:]
    peers = lax.axis_size("dom")
    copies = fetch(
        [(ref, ints.at[n]) for n, ref in enumerate((route_hbm, target_hbm, code_hbm, hang_hbm))]
        + [(adj_hbm, x), (fold_hbm, fold)],
        sems,
    )
    for copy in copies:
        copy.wait()
    route, target, code, hang = (ints[n] for n in range(4))
    lane = iota(1)
    left = lane < 64
    slot = lax.rem(route - lax.axis_index("dom") + 2 + peers, peers)
    hit = (iota(0, (5 * E, E)) == slot * E + target).astype(F32).astype(BF16)
    marked = down(jnp.where(hang == 1, code, -2)) - (lane // 64).astype(F32)
    odd = lane % 16 >= 8
    group = (lane // 16 + 1) % 4
    for f in range(5):
        packed = jnp.zeros((E, 128), F32)
        for c in range(4):
            moved = x[f, :, 128 * c : 128 * c + 128]
            if c:
                moved = pltpu.roll(moved, 16 * c, 1)
            packed = jnp.where(odd & (group == c), moved, packed)
        high = packed.astype(BF16)
        high_f = high.astype(F32)
        both = jnp.where(odd, high_f, pltpu.roll(packed - high_f, 8, 1)).astype(BF16)
        wide[E * f : E * f + E, 0:128] = both
        wide[E * f : E * f + E, 128:256] = high
    mapped = dot(wide[...], fold[...])
    faces = []
    for f in range(5):
        total = jnp.zeros((E, 128), F32)
        for q in range(4):
            total = total + jnp.where(
                marked == 2.0 * q, mapped[E * f : E * f + E, 128 * q : 128 * q + 128], 0.0
            )
        faces.append(total + pltpu.roll(total, 64, 1))
    f01 = jnp.where(left, faces[0], faces[1]).astype(BF16)
    f23 = jnp.where(left, faces[2], faces[3]).astype(BF16)
    sums = dot(hit, jnp.concatenate([f01, f23, faces[4].astype(BF16)], 1))
    for o in range(5):
        ref = outs[o]
        mine = sums[o * E : o * E + E]
        last = jnp.where(left[:64], mine[:64, 256:384], mine[64:, 256:384])
        ref[0:128] = mine[:, 0:128].astype(ref.dtype)
        ref[128:256] = mine[:, 128:256].astype(ref.dtype)
        ref[256:320] = last.astype(ref.dtype)

    marks_out[...] = jnp.broadcast_to(1.0 - hang.astype(F32), (8, E))
    lane = iota(1, (1, 128))
    own = marked[0:1], marked[E - 1 : E]
    edges_out[...] = jnp.zeros((16, 128), F32)
    for n in range(3):
        first, second = 2 * n, min(2 * n + 1, 4)
        for end, (at, chunk) in enumerate(((0, 0), (E - 1, 3))):
            a = x[first, at : at + 1, 128 * chunk : 128 * chunk + 128]
            b = x[second, at : at + 1, 128 * chunk : 128 * chunk + 128]
            if end == 0:
                b = pltpu.roll(b, 64, 1)
            else:
                a = pltpu.roll(a, 64, 1)
            keep = jnp.where((lane % 64 >= 56) & (own[end] >= -1.5), 0.0, 1.0)
            spot = 8 * end + n
            edges_out[spot : spot + 1] = jnp.where(lane < 64, a, b) * keep


def folded_of(route, target, code, hang, adjoint, fold):
    return pl.pallas_call(
        fold_kernel,
        out_shape=[
            jax.ShapeDtypeStruct((320, 128), F32 if o == 2 else BF16) for o in range(5)
        ]
        + [jax.ShapeDtypeStruct((16, 128), F32), jax.ShapeDtypeStruct((8, 128), F32)],
        in_specs=[HBM] * 6,
        out_specs=[VM] * 7,
        scratch_shapes=[
            pltpu.VMEM((4, 1, E), jnp.int32),
            pltpu.VMEM((5, E, 512), F32),
            pltpu.VMEM((256, 512), BF16),
            pltpu.VMEM((5 * E, 256), BF16),
            pltpu.SemaphoreType.DMA((6,)),
        ],
        compiler_params=pltpu.CompilerParams(vmem_limit_bytes=WHOLE),
        name="fold",
    )(route, target, code, hang, adjoint, fold)


def swap(x):
    return pltpu.roll(x, 64, 1)


def along_first(x, coef, base):
    r3, r2 = swap(x[3]), swap(x[2])
    parity = ((x[0] + r3, x[1] + r2), (x[0] - r3, x[1] - r2))
    sums = []
    for s in range(2):
        kept = (parity[s][0], swap(parity[s][0]), parity[s][1], swap(parity[s][1]))
        for c in range(2):
            at = base + 8 * s + 4 * c
            total = coef[at : at + 1] * kept[0]
            for n in range(1, 4):
                total = total + coef[at + n : at + n + 1] * kept[n]
            sums.append(total)
    p0, p1, q0, q1 = sums
    return [p0 + q0, p1 + q1, swap(q1 - p1), swap(q0 - p0)]


def main_kernel(
    adj_hbm, met_hbm, vel_hbm, keep_ref, wf1, wf2, wb1, wb2, coef,
    out, q_out, plane_out, end_q, end_mv, x_ref, met, vel, sems,
):
    order = (1, 0, 2)
    pairs = [(adj_hbm.at[0], x_ref.at[0])]
    for d in order:
        pairs += [(met_hbm.at[d], met.at[d]), (vel_hbm.at[d], vel.at[d])]
    pairs += [(adj_hbm.at[f], x_ref.at[f]) for f in range(1, 5)]
    copies = fetch(pairs, sems)
    lane, row = iota(1), iota(0)
    keep = keep_ref[...]
    left = lane < 64
    for copy in copies[:3]:
        copy.wait()

    for c in range(4):
        at = slice(128 * c, 128 * c + 128)
        w = met[1, :, at] * coef[32:33] + jnp.where(lane % 64 < 8, vel[1, :, at], 0.0)
        high, low = parts_of(w)
        wide = dot(high, wb1[0:128])
        q_out[:, at] = wide[:, :128] + wide[:, 128:] + dot(low, wb2[0:128])

    for copy in copies[3:]:
        copy.wait()
    for n, (ref, d) in enumerate(((met, 0), (met, 2), (vel, 0), (vel, 2))):
        packed = jnp.zeros((E, 128), F32)
        for c in range(4):
            moved = ref[d, :, 128 * c : 128 * c + 128]
            if c:
                moved = pltpu.roll(moved, 16 * c, 1)
            packed = jnp.where((lane // 16) % 4 == c, moved, packed)
        even = jnp.where(left, packed, swap(packed))
        other = jnp.where(left, swap(packed), packed)
        plane_out[n] = jnp.where(lane % 16 < 8, even, pltpu.roll(other, 8, 1))

    small_left = iota(1, (8, 128)) < 64
    for end in range(2):
        rows = slice((E - 8) * end, (E - 8) * end + 8)
        w = []
        for c in range(4):
            at = slice(128 * c, 128 * c + 128)
            spot = 33 + 4 * end + c
            term = met[0, rows, at] * coef[spot : spot + 1]
            if c == 3 * end:
                term = term + jnp.where(small_left != (end == 1), vel[0, rows, at], 0.0)
            w.append(term)
        back = along_first(w, coef, 16)
        for c in range(4):
            end_q[end, c] = back[c]
        at = slice(384 * end, 384 * end + 128)
        for n, (ref, d) in enumerate(((met, 1), (met, 2), (vel, 1), (vel, 2))):
            end_mv[end, n] = ref[d, rows, at]

    def field(f, carry):
        x = [x_ref[f, :, 128 * c : 128 * c + 128] * keep for c in range(4)]
        low_faces = pltpu.roll(swap(x[0]), E - 1, 0)
        high_faces = pltpu.roll(swap(x[3]), 1, 0)
        x[0] = x[0] + jnp.where(left & (row > 0), high_faces, 0.0)
        x[3] = x[3] + jnp.where(left | (row == E - 1), 0.0, low_faces)
        g0 = along_first(x, coef, 0)
        inner0 = []
        totals = []
        for c in range(4):
            at = slice(128 * c, 128 * c + 128)
            high, low = parts_of(x[c])
            g = dot(jnp.concatenate([high, low], 1), wf1[...]) + dot(high, wf2[...])
            inner0.append(met[0, :, at] * g0[c] + vel[0, :, at] * x[c])
            in1 = met[1, :, at] * g[:, :128] + vel[1, :, at] * x[c]
            in2 = met[2, :, at] * g[:, 128:] + vel[2, :, at] * x[c]
            high1, low1 = parts_of(in1)
            high2, low2 = parts_of(in2)
            wide = dot(jnp.concatenate([high1, high2], 1), wb1[...])
            totals.append(
                wide[:, :128]
                + wide[:, 128:]
                + dot(jnp.concatenate([low1, low2], 1), wb2[...])
            )
        back = along_first(inner0, coef, 16)
        for c in range(4):
            out[f, :, 128 * c : 128 * c + 128] = totals[c] + back[c]
        return carry

    lax.fori_loop(0, 5, field, 0)


def keep_kernel(marks, out):
    kept = jnp.where(iota(0) == iota(1), marks[0:1], 0.0).astype(BF16)
    column = dot(kept, jnp.ones((E, 128), BF16))
    out[...] = jnp.where(iota(1) % 64 >= 56, column, 1.0)


def kept_of(marks):
    return pl.pallas_call(
        keep_kernel,
        out_shape=jax.ShapeDtypeStruct((E, 128), F32),
        in_specs=[VM],
        out_specs=VM,
        compiler_params=pltpu.CompilerParams(vmem_limit_bytes=16 * 1024 * 1024),
        cost_estimate=pl.CostEstimate(
            flops=8_000_000_000, bytes_accessed=30_000_000, transcendentals=0
        ),
        name="keep",
    )(marks)


def main_of(adjoint, metric, velocity, keep, tables):
    return pl.pallas_call(
        main_kernel,
        out_shape=[
            jax.ShapeDtypeStruct((5, E, 512), F32),
            jax.ShapeDtypeStruct((E, 512), F32),
            jax.ShapeDtypeStruct((4, E, 128), F32),
            jax.ShapeDtypeStruct((2, 4, 8, 128), F32),
            jax.ShapeDtypeStruct((2, 4, 8, 128), F32),
        ],
        in_specs=[HBM] * 3 + [VM] * 6,
        out_specs=[VM] * 5,
        scratch_shapes=[
            pltpu.VMEM((5, E, 512), F32),
            pltpu.VMEM((3, E, 512), F32),
            pltpu.VMEM((3, E, 512), F32),
            pltpu.SemaphoreType.DMA((11,)),
        ],
        compiler_params=pltpu.CompilerParams(vmem_limit_bytes=LIMIT),
        cost_estimate=pl.CostEstimate(
            flops=4_000_000_000, bytes_accessed=6_000_000, transcendentals=0
        ),
        name="inner",
    )(
        adjoint, metric, velocity, keep,
        *tables["forward"], *tables["backward"], tables["coef"],
    )


def odd_device():
    index = lax.axis_index("dom") * lax.axis_size("sub") + lax.axis_index("sub")
    return lax.rem(index, 2) == 1


def line_kernel(a, b, own, c, d, edges, across, inside):
    def rows(start):
        return sum(ref[start : start + 16].astype(F32) for ref in (a, b, own, c, d))

    low = [edges[0:3]]
    high = [edges[8:11]]
    for n, (first, last) in enumerate(((0, 112), (128, 240), (256, 304))):
        low.append(pltpu.roll(rows(first)[0:1], 56, 1))
        line = rows(last)[15:16]
        high.append(pltpu.roll(swap(line) if n == 2 else line, 72, 1))
    zero = jnp.zeros((2, 128), F32)
    low = jnp.concatenate(low + [zero], 0)
    high = jnp.concatenate(high + [zero], 0)
    odd = odd_device()
    across[...] = jnp.where(odd, high, low)
    inside[...] = jnp.where(odd, low, high)


def lines_of(parts, edges):
    return pl.pallas_call(
        line_kernel,
        out_shape=[jax.ShapeDtypeStruct((8, 128), F32)] * 2,
        in_specs=[VM] * 6,
        out_specs=[VM] * 2,
        compiler_params=pltpu.CompilerParams(vmem_limit_bytes=LIMIT),
        name="lines",
    )(*parts, edges)


def post_kernel(
    a, b, own, c2, d, across, inside, base, q_ref, plane, end_q, end_mv,
    wf1, wf2, wb1, wb2, spread, place, out_hbm, out, out_sems,
):
    out_copies = [
        pltpu.make_async_copy(out.at[f], out_hbm.at[f], out_sems.at[f]) for f in range(5)
    ]
    lane, row = iota(1), iota(0)
    left = lane < 64

    small_left = iota(1, (1, 128)) < 64
    halo = []
    odd = odd_device()
    before = jnp.where(odd, inside[...], across[...])
    after = jnp.where(odd, across[...], inside[...])
    for got in (before, after):
        rows = []
        for n in range(3):
            pair = got[n : n + 1]
            turned = pltpu.roll(pair, 64, 1)
            rows.append(jnp.where(small_left, pair, turned))
            rows.append(jnp.where(small_left, turned, pair))
        halo.append(jnp.concatenate(rows + [jnp.zeros((2, 128), F32)], 0))
    u = jnp.concatenate(halo, 0)
    mv = [
        jnp.concatenate(
            [
                jnp.broadcast_to(end_mv[0, n, 0:1], (8, 128)),
                jnp.broadcast_to(end_mv[1, n, 7:8], (8, 128)),
            ],
            0,
        )
        for n in range(4)
    ]

    def two_dims(y, m_first, m_second, v_first, v_second):
        high, low = parts_of(y)
        g = dot(jnp.concatenate([high, low], 1), wf1[...]) + dot(high, wf2[...])
        first = m_first * g[:, :128] + v_first * y
        second = m_second * g[:, 128:] + v_second * y
        high1, low1 = parts_of(first)
        high2, low2 = parts_of(second)
        wide = dot(jnp.concatenate([high1, high2], 1), wb1[...])
        return (
            wide[:, :128]
            + wide[:, 128:]
            + dot(jnp.concatenate([low1, low2], 1), wb2[...])
        )

    ends = two_dims(u, *mv)

    for n in range(3):
        rows = slice(128 * n, min(128 * n + 128, 320))
        m = sum(ref[rows].astype(F32) for ref in (a, b, own, c2, d))
        if n == 2:
            m = jnp.concatenate([m, swap(m)], 0)
        low_lines = pltpu.roll(pltpu.roll(m, 56, 1), E - 1, 0)
        high_lines = pltpu.roll(pltpu.roll(m, 72, 1), 1, 0)
        low_lines = jnp.where(row == E - 1, after[3 + n : 4 + n], low_lines)
        high_lines = jnp.where(row == 0, before[3 + n : 4 + n], high_lines)
        y = m + jnp.where(lane % 64 < 8, high_lines, 0.0)
        y = y + jnp.where(lane % 64 >= 56, low_lines, 0.0)
        y_parts = jnp.concatenate(parts_of(y), 1)
        r = two_dims(y, plane[0], plane[1], plane[2], plane[3])
        r_parts = jnp.concatenate(parts_of(r), 1)
        for f in range(2 * n, min(2 * n + 2, 5)):
            for c in range(4):
                at = slice(128 * c, 128 * c + 128)
                start = 512 * (f - 2 * n) + 128 * c
                cols = slice(start, start + 128)
                out[f, :, at] = (
                    base[f, :, at]
                    + q_ref[:, at] * dot(y_parts, spread[:, cols])
                    + dot(r_parts, place[:, cols])
                )
                first = end_q[0, c, 0:1] * halo[0][f : f + 1]
                final = end_q[1, c, 7:8] * halo[1][f : f + 1]
                if c == 0:
                    first = first + jnp.where(small_left, ends[f : f + 1], 0.0)
                if c == 3:
                    final = final + jnp.where(small_left, 0.0, ends[8 + f : 9 + f])
                out[f, 0:1, at] += first
                out[f, E - 1 : E, at] += final
            out_copies[f].start()
    for copy in out_copies:
        copy.wait()


def post_of(parts, across, inside, local, tables):
    return pl.pallas_call(
        post_kernel,
        out_shape=jax.ShapeDtypeStruct((5, E, 512), F32),
        in_specs=[VM] * 18,
        out_specs=HBM,
        scratch_shapes=[pltpu.VMEM((5, E, 512), F32), pltpu.SemaphoreType.DMA((5,))],
        compiler_params=pltpu.CompilerParams(vmem_limit_bytes=LIMIT),
        name="outer",
    )(
        *parts, across, inside, *local, *tables["forward"], *tables["backward"],
        tables["spread"], tables["place"],
    )


def shards(adjoint_field, metric, velocity, mortar_route, mortar_element, face_code, hanging):
    tables = constants()
    peers = lax.axis_size("dom")
    adjoint = jnp.transpose(adjoint_field, (1, 0, 2))
    met = jnp.transpose(metric, (1, 0, 2))
    vel = jnp.transpose(velocity, (1, 0, 2))
    route, target, code, hang = (
        x.reshape(1, E) for x in (mortar_route, mortar_element, face_code, hanging)
    )
    *parts, edges, marks = folded_of(route, target, code, hang, adjoint, tables["fold"])
    for o in (0, 4, 1, 3):
        pairs = [(i, (i + o - 2) % peers) for i in range(peers)]
        parts[o] = lax.ppermute(parts[o], "dom", pairs)
    local = main_of(adjoint, met, vel, kept_of(marks), tables)
    parts, local = lax.optimization_barrier((parts, local))
    out_a, out_b = lines_of(parts, edges)
    axes = ("dom", "sub")
    count = lax.axis_size(axes)
    inside = [(i, i ^ 1) for i in range(count)]
    across = [(i, i + 1 if i % 2 else i - 1) for i in range(1, count - 1)]
    outward = lax.ppermute(out_a, axes, across)
    inward = lax.ppermute(out_b, axes, inside)
    result = post_of(parts, outward, inward, local, tables)
    return jnp.transpose(result, (1, 0, 2))


def solution(mesh):
    block = P(("dom", "sub"), None, None)
    flat = P(("dom", "sub"), None)
    return jax.shard_map(
        shards,
        mesh=mesh,
        in_specs=(block, block, block, flat, flat, flat, flat),
        out_specs=block,
        check_vma=False,
    )
```

profile of v0, /device:TPU:0, one launch (start us, length us, event | category | flops | bytes accessed | tf_op | source)
XLA Modules:
  0.0 25.9 jit_solution(6484634818930049140)
XLA Ops:
  0.0 3.2 %fold.1 = (bf16[320,128]{1,0:T(8,128)(2,1)}, bf16[320,128]{1,0:T(8,128)(2,1)}, f32[320,128]{1,0:T(8,128)}, bf16[320,128]{1,0:T(8,128)(2,1)}, bf16[320,128]{1,0:T...) custom-call(s32[1,128]{1,0:T(1,128)} %bitcast.12, s32[1,128]{1,0:T(1,128)} %bitcast.13, s32[1,128]{1,0:T(1,128)} %bitcast.14, ...), custom_call_target="tpu_custom_call" | custom-call | tf_op jit(solution)/shard_map/fold/pallas_call | solution.py:268
  3.2 5.1 %collective-permute-start = (bf16[320,128]{1,0:T(8,128)(2,1)}, bf16[320,128]{1,0:T(8,128)(2,1)S(1)}, u32[]{:S(2)}, u32[]{:S(2)}) collective-permute-start(bf16[320,128]{1,0:T(8,128)(2,1)} %get-tuple-element.29), channel_id=1, source_target_pairs={{0,24},{4,28},{8,0},{12,4},{16,8},{20,12},{24,16},{28,20},{1,25},{... | collective-permute-start | bytes 245768 | tf_op jit(solution)/shard_map/ppermute | solution.py:592
  8.3 1.4 %collective-permute-start.1 = (bf16[320,128]{1,0:T(8,128)(2,1)}, bf16[320,128]{1,0:T(8,128)(2,1)S(1)}, u32[]{:S(2)}, u32[]{:S(2)}) collective-permute-start(bf16[320,128]{1,0:T(8,128)(2,1)} %get-tuple-element.30), channel_id=1, source_target_pairs={{0,28},{4,0},{8,4},{12,8},{16,12},{20,16},{24,20},{28,24},{1,29},{... | collective-permute-start | bytes 245768 | tf_op jit(solution)/shard_map/ppermute | solution.py:592
  9.7 0.6 %collective-permute-start.2 = (bf16[320,128]{1,0:T(8,128)(2,1)}, bf16[320,128]{1,0:T(8,128)(2,1)S(1)}, u32[]{:S(2)}, u32[]{:S(2)}) collective-permute-start(bf16[320,128]{1,0:T(8,128)(2,1)} %get-tuple-element.32), channel_id=1, source_target_pairs={{0,4},{4,8},{8,12},{12,16},{16,20},{20,24},{24,28},{28,0},{1,5},{5... | collective-permute-start | bytes 245768 | tf_op jit(solution)/shard_map/ppermute | solution.py:592
  10.3 0.9 %collective-permute-start.3 = (bf16[320,128]{1,0:T(8,128)(2,1)}, bf16[320,128]{1,0:T(8,128)(2,1)S(1)}, u32[]{:S(2)}, u32[]{:S(2)}) collective-permute-start(bf16[320,128]{1,0:T(8,128)(2,1)} %get-tuple-element.33), channel_id=1, source_target_pairs={{0,8},{4,12},{8,16},{12,20},{16,24},{20,28},{24,0},{28,4},{1,9},{5... | collective-permute-start | bytes 245768 | tf_op jit(solution)/shard_map/ppermute | solution.py:592
  11.3 0.0 copy-start.11
  11.3 0.7 %copy-done.11 = f32[8,128]{1,0:T(8,128)S(1)} copy-done((f32[8,128]{1,0:T(8,128)S(1)}, f32[8,128]{1,0:T(8,128)}, u32[]{:S(2)}) %copy-start.11) | copy-done | bytes 4120
  11.9 0.0 copy-start
  11.9 0.0 copy-start.4
  11.9 0.0 copy-start.5
  12.0 0.0 copy-start.6
  12.0 0.0 copy-start.7
  12.0 0.0 copy-start.9
  12.0 0.0 copy-start.10
  12.0 0.0 copy-start.12
  12.0 0.1 keep.1.keep_ref
  12.1 1.1 %copy-done = f32[128,5,512]{2,0,1:T(8,128)S(1)} copy-done((f32[128,5,512]{2,0,1:T(8,128)S(1)}, f32[128,5,512]{2,0,1:T(8,128)}, u32[]{:S(2)}) %copy-start) | copy-done | bytes 1310744
  13.3 0.0 copy-done.4
  13.3 0.0 copy-done.5
  13.3 0.0 copy-done.6
  13.3 0.0 copy-done.7
  13.3 0.3 %copy-done.9 = f32[128,3,512]{2,0,1:T(8,128)S(1)} copy-done((f32[128,3,512]{2,0,1:T(8,128)S(1)}, f32[128,3,512]{2,0,1:T(8,128)}, u32[]{:S(2)}) %copy-start.9) | copy-done | bytes 786456
  13.6 0.2 copy-done.10
  13.8 0.0 copy-done.12
  13.8 0.0 copy-start.1
  13.8 0.0 copy-start.8
  13.8 0.0 copy-start.2
  13.8 0.0 copy-start.3
  13.9 5.0 %inner.1 = (f32[5,128,512]{2,1,0:T(8,128)S(1)}, f32[128,512]{1,0:T(8,128)S(1)}, f32[4,128,128]{2,1,0:T(8,128)S(1)}, f32[2,4,8,128]{3,2,1,0:T(8,128)S(1)}, f32[2,4,8,128]{3,2,1,0:T(8,128)S(1)}) custom-call(f32[5,128,512]{2,1,0:T(8,128)S(1)} %bitcast.9, f32[3,128,512]{2,1,0:T(8,128)S(1)} %bitcast.10, f32[3,128,512]{2,1,0:T(8,128)S(1)} %bitcast.11, ...), custom_call_target="tpu_custom_call" | custom-call | flops 4000000000 | bytes 6000000 | tf_op jit(solution)/shard_map/inner/pallas_call | solution.py:415
  18.9 0.0 collective-permute-done.a
  18.9 0.0 collective-permute-done.1.b
  18.9 0.0 collective-permute-done.2.c.c2
  18.9 0.0 collective-permute-done.3.d
  18.9 0.0 copy-done.1
  18.9 0.0 copy-done.8
  18.9 0.1 lines.1
  19.1 0.7 %collective-permute-start.4 = (f32[8,128]{1,0:T(8,128)S(1)}, f32[8,128]{1,0:T(8,128)S(1)}, u32[]{:S(2)}, u32[]{:S(2)}) collective-permute-start(f32[8,128]{1,0:T(8,128)S(1)} %get-tuple-element.46), channel_id=1, source_target_pairs={{1,2},{2,1},{3,4},{4,3},{5,6},{6,5},{7,8},{8,7},{9,10},{10,9},{11,... | collective-permute-start | bytes 12296 | tf_op jit(solution)/shard_map/ppermute | solution.py:600
  19.7 2.9 %collective-permute-start.5 = (f32[8,128]{1,0:T(8,128)S(1)}, f32[8,128]{1,0:T(8,128)S(1)}, u32[]{:S(2)}, u32[]{:S(2)}) collective-permute-start(f32[8,128]{1,0:T(8,128)S(1)} %get-tuple-element.47), channel_id=1, source_target_pairs={{0,1},{1,0},{2,3},{3,2},{4,5},{5,4},{6,7},{7,6},{8,9},{9,8},{10,11... | collective-permute-start | bytes 12296 | tf_op jit(solution)/shard_map/ppermute | solution.py:601
  22.7 0.0 collective-permute-done.4.across
  22.7 0.8 %collective-permute-done.5.inside = f32[8,128]{1,0:T(8,128)S(1)} collective-permute-done((f32[8,128]{1,0:T(8,128)S(1)}, f32[8,128]{1,0:T(8,128)S(1)}, u32[]{:S(2)}, u32[]{:S(2)}) %collective-permute-start.5) | collective-permute-done | bytes 4128 | tf_op jit(solution)/shard_map/ppermute | solution.py:601
  23.5 0.0 copy-done.2
  23.5 0.0 copy-done.3
  23.5 2.4 %outer.1 = f32[5,128,512]{2,1,0:T(8,128)} custom-call(bf16[320,128]{1,0:T(8,128)(2,1)S(1)} %collective-permute-done.a, bf16[320,128]{1,0:T(8,128)(2,1)S(1)} %collective-permute-done.1.b, f32[320,128]{1,0:T(8,128)S(1)} %copy-done.1, bf16[320,128]{1,0:T(8,128)(2,1)S(1)} %collective-permute-done.2.c.c2, bf16[320,128]{1,0:T(8,128)(2,1)S(1)} %collective-permute-done.3.d, ...), custom_call_target="tpu_custom_call" | custom-call | tf_op jit(solution)/shard_map/outer/pallas_call | solution.py:566
Async XLA Ops:
  3.2 15.7 %collective-permute-start = (bf16[320,128]{1,0:T(8,128)(2,1)}, bf16[320,128]{1,0:T(8,128)(2,1)S(1)}, u32[]{:S(2)}, u32[]{:S(2)}) collective-permute-start(bf16[320,128]{1,0:T(8,128)(2,1)} %get-tuple-element.29), channel_id=1, source_target_pairs={{0,24},{4,28},{8,0},{12,4},{16,8},{20,12},{24,16},{28,20},{1,25},{... | collective-permute-start | bytes 245768 | tf_op jit(solution)/shard_map/ppermute | solution.py:592
  8.3 10.6 %collective-permute-start.1 = (bf16[320,128]{1,0:T(8,128)(2,1)}, bf16[320,128]{1,0:T(8,128)(2,1)S(1)}, u32[]{:S(2)}, u32[]{:S(2)}) collective-permute-start(bf16[320,128]{1,0:T(8,128)(2,1)} %get-tuple-element.30), channel_id=1, source_target_pairs={{0,28},{4,0},{8,4},{12,8},{16,12},{20,16},{24,20},{28,24},{1,29},{... | collective-permute-start | bytes 245768 | tf_op jit(solution)/shard_map/ppermute | solution.py:592
  9.7 9.2 %collective-permute-start.2 = (bf16[320,128]{1,0:T(8,128)(2,1)}, bf16[320,128]{1,0:T(8,128)(2,1)S(1)}, u32[]{:S(2)}, u32[]{:S(2)}) collective-permute-start(bf16[320,128]{1,0:T(8,128)(2,1)} %get-tuple-element.32), channel_id=1, source_target_pairs={{0,4},{4,8},{8,12},{12,16},{16,20},{20,24},{24,28},{28,0},{1,5},{5... | collective-permute-start | bytes 245768 | tf_op jit(solution)/shard_map/ppermute | solution.py:592
  10.3 8.6 %collective-permute-start.3 = (bf16[320,128]{1,0:T(8,128)(2,1)}, bf16[320,128]{1,0:T(8,128)(2,1)S(1)}, u32[]{:S(2)}, u32[]{:S(2)}) collective-permute-start(bf16[320,128]{1,0:T(8,128)(2,1)} %get-tuple-element.33), channel_id=1, source_target_pairs={{0,8},{4,12},{8,16},{12,20},{16,24},{20,28},{24,0},{28,4},{1,9},{5... | collective-permute-start | bytes 245768 | tf_op jit(solution)/shard_map/ppermute | solution.py:592
  11.3 0.7 %copy-start.11 = (f32[8,128]{1,0:T(8,128)S(1)}, f32[8,128]{1,0:T(8,128)}, u32[]{:S(2)}) copy-start(f32[8,128]{1,0:T(8,128)} %get-tuple-element.34.marks) | copy-start | bytes 12292
  11.9 1.3 %copy-start = (f32[128,5,512]{2,0,1:T(8,128)S(1)}, f32[128,5,512]{2,0,1:T(8,128)}, u32[]{:S(2)}) copy-start(f32[128,5,512]{2,0,1:T(8,128)} %param.15) | copy-start | bytes 3932164
  11.9 1.3 %copy-start.4 = (bf16[256,256]{1,0:T(8,128)(2,1)S(1)}, bf16[256,256]{1,0:T(8,128)(2,1)}, u32[]{:S(2)}) copy-start(bf16[256,256]{1,0:T(8,128)(2,1)} %constant.19.clone.wb1) | copy-start | bytes 393220
  11.9 1.3 %copy-start.5 = (bf16[256,256]{1,0:T(8,128)(2,1)S(1)}, bf16[256,256]{1,0:T(8,128)(2,1)}, u32[]{:S(2)}) copy-start(bf16[256,256]{1,0:T(8,128)(2,1)} %constant.17.clone.wf1) | copy-start | bytes 393220
  12.0 1.3 %copy-start.6 = (bf16[256,128]{1,0:T(8,128)(2,1)S(1)}, bf16[256,128]{1,0:T(8,128)(2,1)}, u32[]{:S(2)}) copy-start(bf16[256,128]{1,0:T(8,128)(2,1)} %constant.20.clone.wb2) | copy-start | bytes 196612
  12.0 1.3 %copy-start.7 = (bf16[128,256]{1,0:T(8,128)(2,1)S(1)}, bf16[128,256]{1,0:T(8,128)(2,1)}, u32[]{:S(2)}) copy-start(bf16[128,256]{1,0:T(8,128)(2,1)} %constant.18.clone.wf2) | copy-start | bytes 196612
  12.0 1.6 %copy-start.9 = (f32[128,3,512]{2,0,1:T(8,128)S(1)}, f32[128,3,512]{2,0,1:T(8,128)}, u32[]{:S(2)}) copy-start(f32[128,3,512]{2,0,1:T(8,128)} %param.16) | copy-start | bytes 2359300
  12.0 1.8 %copy-start.10 = (f32[128,3,512]{2,0,1:T(8,128)S(1)}, f32[128,3,512]{2,0,1:T(8,128)}, u32[]{:S(2)}) copy-start(f32[128,3,512]{2,0,1:T(8,128)} %param.17) | copy-start | bytes 2359300
  12.0 1.8 %copy-start.12 = (f32[48,128]{1,0:T(8,128)S(1)}, f32[48,128]{1,0:T(8,128)}, u32[]{:S(2)}) copy-start(f32[48,128]{1,0:T(8,128)} %constant.21.clone.coef) | copy-start | bytes 73732
  13.8 5.1 %copy-start.1 = (f32[320,128]{1,0:T(8,128)S(1)}, f32[320,128]{1,0:T(8,128)}, u32[]{:S(2)}) copy-start(f32[320,128]{1,0:T(8,128)} %get-tuple-element.42.own) | copy-start | bytes 491524
  13.8 5.1 %copy-start.8 = (f32[16,128]{1,0:T(8,128)S(1)}, f32[16,128]{1,0:T(8,128)}, u32[]{:S(2)}) copy-start(f32[16,128]{1,0:T(8,128)} %get-tuple-element.45.edges) | copy-start | bytes 24580
  13.8 9.7 %copy-start.2 = (bf16[256,1024]{1,0:T(8,128)(2,1)S(1)}, bf16[256,1024]{1,0:T(8,128)(2,1)}, u32[]{:S(2)}) copy-start(bf16[256,1024]{1,0:T(8,128)(2,1)} %constant.23.clone.place) | copy-start | bytes 1572868
  13.8 9.7 %copy-start.3 = (bf16[256,1024]{1,0:T(8,128)(2,1)S(1)}, bf16[256,1024]{1,0:T(8,128)(2,1)}, u32[]{:S(2)}) copy-start(bf16[256,1024]{1,0:T(8,128)(2,1)} %constant.22.clone.spread) | copy-start | bytes 1572868
  19.1 3.6 %collective-permute-start.4 = (f32[8,128]{1,0:T(8,128)S(1)}, f32[8,128]{1,0:T(8,128)S(1)}, u32[]{:S(2)}, u32[]{:S(2)}) collective-permute-start(f32[8,128]{1,0:T(8,128)S(1)} %get-tuple-element.46), channel_id=1, source_target_pairs={{1,2},{2,1},{3,4},{4,3},{5,6},{6,5},{7,8},{8,7},{9,10},{10,9},{11,... | collective-permute-start | bytes 12296 | tf_op jit(solution)/shard_map/ppermute | solution.py:600
  19.7 3.8 %collective-permute-start.5 = (f32[8,128]{1,0:T(8,128)S(1)}, f32[8,128]{1,0:T(8,128)S(1)}, u32[]{:S(2)}, u32[]{:S(2)}) collective-permute-start(f32[8,128]{1,0:T(8,128)S(1)} %get-tuple-element.47), channel_id=1, source_target_pairs={{0,1},{1,0},{2,3},{3,2},{4,5},{5,4},{6,7},{7,6},{8,9},{9,8},{10,11... | collective-permute-start | bytes 12296 | tf_op jit(solution)/shard_map/ppermute | solution.py:601
where the time goes:
time: 26.3 us; the launch traced here: 25.9 us
  starting transfers between devices  11.7 us (44%)
  Pallas kernels  10.9 us (41%)
  local copies, waits for them, and re-layouts  2.42 us (9%)
  waiting for transfers between devices  0.83 us (3%)
    ppermute x4, starting transfers between devices, shards(): parts[o] = lax.ppermute(parts[o], 'dom', pairs)  8.06 us
    pallas_call x1, Pallas kernels, main_of(): pl.pallas_call(main_kernel, out_shape=[jax.ShapeDtypeStruct((5, E, 512),...  5.02 us
    pallas_call x1, Pallas kernels, folded_of(): pl.pallas_call(fold_kernel, out_shape=[jax.ShapeDtypeStruct((320, 128), F...  3.19 us
    ppermute x1, starting transfers between devices, shards(): inward = lax.ppermute(out_b, axes, inside)  2.95 us
    unnamed x26, local copies, waits for them, and re-layouts  2.42 us
    pallas_call x1, Pallas kernels, post_of(): pl.pallas_call(post_kernel, out_shape=jax.ShapeDtypeStruct((5, E, 512), F...  2.4 us
    ppermute x1, waiting for transfers between devices, shards(): inward = lax.ppermute(out_b, axes, inside)  0.82 us
    ppermute x1, starting transfers between devices, shards(): outward = lax.ppermute(out_a, axes, across)  0.65 us
  transfers between devices with their start and end apart: 6, of which 1 were waited for; matrix products, arithmetic and copies ran while one was open for 0% of the time, Pallas kernels for 20%

commit v1 on v0

--- a/solution.py
+++ b/solution.py
@@ -201,10 +201,11 @@
     peers = lax.axis_size("dom")
     copies = fetch(
         [(ref, ints.at[n]) for n, ref in enumerate((route_hbm, target_hbm, code_hbm, hang_hbm))]
-        + [(adj_hbm, x), (fold_hbm, fold)],
+        + [(adj_hbm.at[f], x.at[f]) for f in range(5)]
+        + [(fold_hbm, fold)],
         sems,
     )
-    for copy in copies:
+    for copy in copies[:4]:
         copy.wait()
     route, target, code, hang = (ints[n] for n in range(4))
     lane = iota(1)
@@ -215,6 +216,7 @@
     odd = lane % 16 >= 8
     group = (lane // 16 + 1) % 4
     for f in range(5):
+        copies[4 + f].wait()
         packed = jnp.zeros((E, 128), F32)
         for c in range(4):
             moved = x[f, :, 128 * c : 128 * c + 128]
@@ -226,6 +228,7 @@
         both = jnp.where(odd, high_f, pltpu.roll(packed - high_f, 8, 1)).astype(BF16)
         wide[E * f : E * f + E, 0:128] = both
         wide[E * f : E * f + E, 128:256] = high
+    copies[9].wait()
     mapped = dot(wide[...], fold[...])
     faces = []
     for f in range(5):
@@ -278,7 +281,7 @@
             pltpu.VMEM((5, E, 512), F32),
             pltpu.VMEM((256, 512), BF16),
             pltpu.VMEM((5 * E, 256), BF16),
-            pltpu.SemaphoreType.DMA((6,)),
+            pltpu.SemaphoreType.DMA((10,)),
         ],
         compiler_params=pltpu.CompilerParams(vmem_limit_bytes=WHOLE),
         name="fold",
@@ -305,21 +308,26 @@
     return [p0 + q0, p1 + q1, swap(q1 - p1), swap(q0 - p0)]
 
 
+def chunks_of(ref, d):
+    return jnp.concatenate([ref[d, :, 128 * c : 128 * c + 128] for c in range(4)], 0)
+
+
+def two_dims(y, m_first, m_second, v_first, v_second, wf1, wf2, wb1, wb2):
+    high, low = parts_of(y)
+    g = dot(jnp.concatenate([high, low], 1), wf1[...]) + dot(high, wf2[...])
+    high1, low1 = parts_of(m_first * g[:, :128] + v_first * y)
+    high2, low2 = parts_of(m_second * g[:, 128:] + v_second * y)
+    wide = dot(jnp.concatenate([high1, high2], 1), wb1[...])
+    low = dot(jnp.concatenate([low1, low2], 1), wb2[...])
+    return wide[:, :128] + wide[:, 128:] + low
+
+
 def main_kernel(
-    adj_hbm, met_hbm, vel_hbm, keep_ref, wf1, wf2, wb1, wb2, coef,
-    out, q_out, plane_out, end_q, end_mv, x_ref, met, vel, sems,
+    x_ref, met, vel, keep_ref, wf1, wf2, wb1, wb2, coef, out, q_out, plane_out, end_q, end_mv,
 ):
-    order = (1, 0, 2)
-    pairs = [(adj_hbm.at[0], x_ref.at[0])]
-    for d in order:
-        pairs += [(met_hbm.at[d], met.at[d]), (vel_hbm.at[d], vel.at[d])]
-    pairs += [(adj_hbm.at[f], x_ref.at[f]) for f in range(1, 5)]
-    copies = fetch(pairs, sems)
     lane, row = iota(1), iota(0)
     keep = keep_ref[...]
     left = lane < 64
-    for copy in copies[:3]:
-        copy.wait()
 
     for c in range(4):
         at = slice(128 * c, 128 * c + 128)
@@ -328,8 +336,6 @@
         wide = dot(high, wb1[0:128])
         q_out[:, at] = wide[:, :128] + wide[:, 128:] + dot(low, wb2[0:128])
 
-    for copy in copies[3:]:
-        copy.wait()
     for n, (ref, d) in enumerate(((met, 0), (met, 2), (vel, 0), (vel, 2))):
         packed = jnp.zeros((E, 128), F32)
         for c in range(4):
@@ -365,27 +371,19 @@
         high_faces = pltpu.roll(swap(x[3]), 1, 0)
         x[0] = x[0] + jnp.where(left & (row > 0), high_faces, 0.0)
         x[3] = x[3] + jnp.where(left | (row == E - 1), 0.0, low_faces)
+        stacked = jnp.concatenate(x, 0)
+        rest = two_dims(
+            stacked, chunks_of(met, 1), chunks_of(met, 2), chunks_of(vel, 1), chunks_of(vel, 2),
+            wf1, wf2, wb1, wb2,
+        )
         g0 = along_first(x, coef, 0)
         inner0 = []
-        totals = []
         for c in range(4):
             at = slice(128 * c, 128 * c + 128)
-            high, low = parts_of(x[c])
-            g = dot(jnp.concatenate([high, low], 1), wf1[...]) + dot(high, wf2[...])
             inner0.append(met[0, :, at] * g0[c] + vel[0, :, at] * x[c])
-            in1 = met[1, :, at] * g[:, :128] + vel[1, :, at] * x[c]
-            in2 = met[2, :, at] * g[:, 128:] + vel[2, :, at] * x[c]
-            high1, low1 = parts_of(in1)
-            high2, low2 = parts_of(in2)
-            wide = dot(jnp.concatenate([high1, high2], 1), wb1[...])
-            totals.append(
-                wide[:, :128]
-                + wide[:, 128:]
-                + dot(jnp.concatenate([low1, low2], 1), wb2[...])
-            )
         back = along_first(inner0, coef, 16)
         for c in range(4):
-            out[f, :, 128 * c : 128 * c + 128] = totals[c] + back[c]
+            out[f, :, 128 * c : 128 * c + 128] = rest[E * c : E * c + E] + back[c]
         return carry
 
     lax.fori_loop(0, 5, field, 0)
@@ -405,7 +403,7 @@
         out_specs=VM,
         compiler_params=pltpu.CompilerParams(vmem_limit_bytes=16 * 1024 * 1024),
         cost_estimate=pl.CostEstimate(
-            flops=8_000_000_000, bytes_accessed=30_000_000, transcendentals=0
+            flops=1_200_000_000, bytes_accessed=1_000_000, transcendentals=0
         ),
         name="keep",
     )(marks)
@@ -421,14 +419,8 @@
             jax.ShapeDtypeStruct((2, 4, 8, 128), F32),
             jax.ShapeDtypeStruct((2, 4, 8, 128), F32),
         ],
-        in_specs=[HBM] * 3 + [VM] * 6,
+        in_specs=[VM] * 9,
         out_specs=[VM] * 5,
-        scratch_shapes=[
-            pltpu.VMEM((5, E, 512), F32),
-            pltpu.VMEM((3, E, 512), F32),
-            pltpu.VMEM((3, E, 512), F32),
-            pltpu.SemaphoreType.DMA((11,)),
-        ],
         compiler_params=pltpu.CompilerParams(vmem_limit_bytes=LIMIT),
         cost_estimate=pl.CostEstimate(
             flops=4_000_000_000, bytes_accessed=6_000_000, transcendentals=0
@@ -498,33 +490,7 @@
             rows.append(jnp.where(small_left, turned, pair))
         halo.append(jnp.concatenate(rows + [jnp.zeros((2, 128), F32)], 0))
     u = jnp.concatenate(halo, 0)
-    mv = [
-        jnp.concatenate(
-            [
-                jnp.broadcast_to(end_mv[0, n, 0:1], (8, 128)),
-                jnp.broadcast_to(end_mv[1, n, 7:8], (8, 128)),
-            ],
-            0,
-        )
-        for n in range(4)
-    ]
-
-    def two_dims(y, m_first, m_second, v_first, v_second):
-        high, low = parts_of(y)
-        g = dot(jnp.concatenate([high, low], 1), wf1[...]) + dot(high, wf2[...])
-        first = m_first * g[:, :128] + v_first * y
-        second = m_second * g[:, 128:] + v_second * y
-        high1, low1 = parts_of(first)
-        high2, low2 = parts_of(second)
-        wide = dot(jnp.concatenate([high1, high2], 1), wb1[...])
-        return (
-            wide[:, :128]
-            + wide[:, 128:]
-            + dot(jnp.concatenate([low1, low2], 1), wb2[...])
-        )
-
-    ends = two_dims(u, *mv)
-
+    faces = []
     for n in range(3):
         rows = slice(128 * n, min(128 * n + 128, 320))
         m = sum(ref[rows].astype(F32) for ref in (a, b, own, c2, d))
@@ -536,19 +502,34 @@
         high_lines = jnp.where(row == 0, before[3 + n : 4 + n], high_lines)
         y = m + jnp.where(lane % 64 < 8, high_lines, 0.0)
         y = y + jnp.where(lane % 64 >= 56, low_lines, 0.0)
-        y_parts = jnp.concatenate(parts_of(y), 1)
-        r = two_dims(y, plane[0], plane[1], plane[2], plane[3])
-        r_parts = jnp.concatenate(parts_of(r), 1)
+        faces.append(y)
+    stacked = jnp.concatenate(faces + [u], 0)
+    factors = [
+        jnp.concatenate(
+            [plane[at]] * 3
+            + [
+                jnp.broadcast_to(end_mv[0, n, 0:1], (8, 128)),
+                jnp.broadcast_to(end_mv[1, n, 7:8], (8, 128)),
+            ],
+            0,
+        )
+        for n, at in enumerate((0, 1, 2, 3))
+    ]
+    r = two_dims(stacked, *factors, wf1, wf2, wb1, wb2)
+    ends = r[3 * E :]
+    y_parts = jnp.concatenate(parts_of(stacked[: 3 * E]), 1)
+    r_parts = jnp.concatenate(parts_of(r[: 3 * E]), 1)
+    for n in range(3):
+        rows = slice(E * n, E * n + E)
         for f in range(2 * n, min(2 * n + 2, 5)):
+            cols = slice(512 * (f - 2 * n), 512 * (f - 2 * n) + 512)
+            out[f] = (
+                base[f]
+                + q_ref[...] * dot(y_parts[rows], spread[:, cols])
+                + dot(r_parts[rows], place[:, cols])
+            )
             for c in range(4):
                 at = slice(128 * c, 128 * c + 128)
-                start = 512 * (f - 2 * n) + 128 * c
-                cols = slice(start, start + 128)
-                out[f, :, at] = (
-                    base[f, :, at]
-                    + q_ref[:, at] * dot(y_parts, spread[:, cols])
-                    + dot(r_parts, place[:, cols])
-                )
                 first = end_q[0, c, 0:1] * halo[0][f : f + 1]
                 final = end_q[1, c, 7:8] * halo[1][f : f + 1]
                 if c == 0:

time: 26.3 us -> 25.7 us (0.977)
  Pallas kernels: 10.9 us -> 10.3 us
    pallas_call x1, Pallas kernels: 2.4 us -> 1.87 us  [post_of(): pl.pallas_call(post_kernel, out_shape=jax.ShapeDtypeStruct((5, E, 512), F...]
    pallas_call x1, Pallas kernels: 5.02 us -> 4.74 us  [main_of(): pl.pallas_call(main_kernel, out_shape=[jax.ShapeDtypeStruct((5, E, 512),...]
  transfers between devices with their start and end apart: 6 -> 6, of which waited for: 1 -> 1; matrix products, arithmetic and copies ran while one was open for 0% -> 0% of each run, Pallas kernels for 20% -> 19%
where the time goes in v1:
time: 25.7 us; the launch traced here: 25.3 us
  starting transfers between devices  11.7 us (46%)
  Pallas kernels  10.3 us (40%)
  local copies, waits for them, and re-layouts  2.42 us (9%)
  waiting for transfers between devices  0.83 us (3%)
    ppermute x4, starting transfers between devices, shards(): parts[o] = lax.ppermute(parts[o], 'dom', pairs)  8.05 us
    pallas_call x1, Pallas kernels, main_of(): pl.pallas_call(main_kernel, out_shape=[jax.ShapeDtypeStruct((5, E, 512),...  4.74 us
    pallas_call x1, Pallas kernels, folded_of(): pl.pallas_call(fold_kernel, out_shape=[jax.ShapeDtypeStruct((320, 128), F...  3.43 us
    ppermute x1, starting transfers between devices, shards(): inward = lax.ppermute(out_b, axes, inside)  2.95 us
    unnamed x26, local copies, waits for them, and re-layouts  2.42 us
    pallas_call x1, Pallas kernels, post_of(): pl.pallas_call(post_kernel, out_shape=jax.ShapeDtypeStruct((5, E, 512), F...  1.87 us
    ppermute x1, waiting for transfers between devices, shards(): inward = lax.ppermute(out_b, axes, inside)  0.82 us
    ppermute x1, starting transfers between devices, shards(): outward = lax.ppermute(out_a, axes, across)  0.65 us
  transfers between devices with their start and end apart: 6, of which 1 were waited for; matrix products, arithmetic and copies ran while one was open for 0% of the time, Pallas kernels for 19%

profile of v1, /device:TPU:0, one launch (start us, length us, event | category | flops | bytes accessed | tf_op | source)
XLA Modules:
  0.0 25.3 jit_solution(9863467469601480895)
XLA Ops:
  0.0 3.4 %fold.1 = (bf16[320,128]{1,0:T(8,128)(2,1)}, bf16[320,128]{1,0:T(8,128)(2,1)}, f32[320,128]{1,0:T(8,128)}, bf16[320,128]{1,0:T(8,128)(2,1)}, bf16[320,128]{1,0:T...) custom-call(s32[1,128]{1,0:T(1,128)} %bitcast.12, s32[1,128]{1,0:T(1,128)} %bitcast.13, s32[1,128]{1,0:T(1,128)} %bitcast.14, ...), custom_call_target="tpu_custom_call" | custom-call | tf_op jit(solution)/shard_map/fold/pallas_call | solution.py:271
  3.4 5.1 %collective-permute-start = (bf16[320,128]{1,0:T(8,128)(2,1)}, bf16[320,128]{1,0:T(8,128)(2,1)S(1)}, u32[]{:S(2)}, u32[]{:S(2)}) collective-permute-start(bf16[320,128]{1,0:T(8,128)(2,1)} %get-tuple-element.29), channel_id=1, source_target_pairs={{0,24},{4,28},{8,0},{12,4},{16,8},{20,12},{24,16},{28,20},{1,25},{... | collective-permute-start | bytes 245768 | tf_op jit(solution)/shard_map/ppermute | solution.py:573
  8.5 1.4 %collective-permute-start.1 = (bf16[320,128]{1,0:T(8,128)(2,1)}, bf16[320,128]{1,0:T(8,128)(2,1)S(1)}, u32[]{:S(2)}, u32[]{:S(2)}) collective-permute-start(bf16[320,128]{1,0:T(8,128)(2,1)} %get-tuple-element.30), channel_id=1, source_target_pairs={{0,28},{4,0},{8,4},{12,8},{16,12},{20,16},{24,20},{28,24},{1,29},{... | collective-permute-start | bytes 245768 | tf_op jit(solution)/shard_map/ppermute | solution.py:573
  9.9 0.7 %collective-permute-start.2 = (bf16[320,128]{1,0:T(8,128)(2,1)}, bf16[320,128]{1,0:T(8,128)(2,1)S(1)}, u32[]{:S(2)}, u32[]{:S(2)}) collective-permute-start(bf16[320,128]{1,0:T(8,128)(2,1)} %get-tuple-element.32), channel_id=1, source_target_pairs={{0,4},{4,8},{8,12},{12,16},{16,20},{20,24},{24,28},{28,0},{1,5},{5... | collective-permute-start | bytes 245768 | tf_op jit(solution)/shard_map/ppermute | solution.py:573
  10.6 0.9 %collective-permute-start.3 = (bf16[320,128]{1,0:T(8,128)(2,1)}, bf16[320,128]{1,0:T(8,128)(2,1)S(1)}, u32[]{:S(2)}, u32[]{:S(2)}) collective-permute-start(bf16[320,128]{1,0:T(8,128)(2,1)} %get-tuple-element.33), channel_id=1, source_target_pairs={{0,8},{4,12},{8,16},{12,20},{16,24},{20,28},{24,0},{28,4},{1,9},{5... | collective-permute-start | bytes 245768 | tf_op jit(solution)/shard_map/ppermute | solution.py:573
  11.5 0.0 copy-start.11
  11.5 0.7 %copy-done.11 = f32[8,128]{1,0:T(8,128)S(1)} copy-done((f32[8,128]{1,0:T(8,128)S(1)}, f32[8,128]{1,0:T(8,128)}, u32[]{:S(2)}) %copy-start.11) | copy-done | bytes 4120
  12.2 0.0 copy-start
  12.2 0.0 copy-start.4
  12.2 0.0 copy-start.5
  12.2 0.0 copy-start.6
  12.2 0.0 copy-start.7
  12.2 0.0 copy-start.9
  12.2 0.0 copy-start.10
  12.2 0.0 copy-start.12
  12.2 0.1 keep.1.keep_ref
  12.4 1.1 %copy-done = f32[128,5,512]{2,0,1:T(8,128)S(1)} copy-done((f32[128,5,512]{2,0,1:T(8,128)S(1)}, f32[128,5,512]{2,0,1:T(8,128)}, u32[]{:S(2)}) %copy-start) | copy-done | bytes 1310744
  13.5 0.0 copy-done.4
  13.5 0.0 copy-done.5
  13.5 0.0 copy-done.6
  13.5 0.0 copy-done.7
  13.5 0.3 %copy-done.9 = f32[128,3,512]{2,0,1:T(8,128)S(1)} copy-done((f32[128,3,512]{2,0,1:T(8,128)S(1)}, f32[128,3,512]{2,0,1:T(8,128)}, u32[]{:S(2)}) %copy-start.9) | copy-done | bytes 786456
  13.8 0.2 copy-done.10
  14.1 0.0 copy-done.12
  14.1 0.0 copy-start.1
  14.1 0.0 copy-start.8
  14.1 0.0 copy-start.2
  14.1 0.0 copy-start.3
  14.1 4.7 %inner.1 = (f32[5,128,512]{2,1,0:T(8,128)S(1)}, f32[128,512]{1,0:T(8,128)S(1)}, f32[4,128,128]{2,1,0:T(8,128)S(1)}, f32[2,4,8,128]{3,2,1,0:T(8,128)S(1)}, f32[2,4,8,128]{3,2,1,0:T(8,128)S(1)}) custom-call(f32[5,128,512]{2,1,0:T(8,128)S(1)} %bitcast.9, f32[3,128,512]{2,1,0:T(8,128)S(1)} %bitcast.10, f32[3,128,512]{2,1,0:T(8,128)S(1)} %bitcast.11, ...), custom_call_target="tpu_custom_call" | custom-call | flops 4000000000 | bytes 6000000 | tf_op jit(solution)/shard_map/inner/pallas_call | solution.py:413
  18.8 0.0 collective-permute-done.a
  18.8 0.0 collective-permute-done.1.b
  18.8 0.0 collective-permute-done.2.c.c2
  18.9 0.0 collective-permute-done.3.d
  18.9 0.0 copy-done.1
  18.9 0.0 copy-done.8
  18.9 0.1 lines.1
  19.0 0.7 %collective-permute-start.4 = (f32[8,128]{1,0:T(8,128)S(1)}, f32[8,128]{1,0:T(8,128)S(1)}, u32[]{:S(2)}, u32[]{:S(2)}) collective-permute-start(f32[8,128]{1,0:T(8,128)S(1)} %get-tuple-element.46), channel_id=1, source_target_pairs={{1,2},{2,1},{3,4},{4,3},{5,6},{6,5},{7,8},{8,7},{9,10},{10,9},{11,... | collective-permute-start | bytes 12296 | tf_op jit(solution)/shard_map/ppermute | solution.py:581
  19.7 2.9 %collective-permute-start.5 = (f32[8,128]{1,0:T(8,128)S(1)}, f32[8,128]{1,0:T(8,128)S(1)}, u32[]{:S(2)}, u32[]{:S(2)}) collective-permute-start(f32[8,128]{1,0:T(8,128)S(1)} %get-tuple-element.47), channel_id=1, source_target_pairs={{0,1},{1,0},{2,3},{3,2},{4,5},{5,4},{6,7},{7,6},{8,9},{9,8},{10,11... | collective-permute-start | bytes 12296 | tf_op jit(solution)/shard_map/ppermute | solution.py:582
  22.6 0.0 collective-permute-done.4.across
  22.6 0.8 %collective-permute-done.5.inside = f32[8,128]{1,0:T(8,128)S(1)} collective-permute-done((f32[8,128]{1,0:T(8,128)S(1)}, f32[8,128]{1,0:T(8,128)S(1)}, u32[]{:S(2)}, u32[]{:S(2)}) %collective-permute-start.5) | collective-permute-done | bytes 4128 | tf_op jit(solution)/shard_map/ppermute | solution.py:582
  23.5 0.0 copy-done.2
  23.5 0.0 copy-done.3
  23.5 1.9 %outer.1 = f32[5,128,512]{2,1,0:T(8,128)} custom-call(bf16[320,128]{1,0:T(8,128)(2,1)S(1)} %collective-permute-done.a, bf16[320,128]{1,0:T(8,128)(2,1)S(1)} %collective-permute-done.1.b, f32[320,128]{1,0:T(8,128)S(1)} %copy-done.1, bf16[320,128]{1,0:T(8,128)(2,1)S(1)} %collective-permute-done.2.c.c2, bf16[320,128]{1,0:T(8,128)(2,1)S(1)} %collective-permute-done.3.d, ...), custom_call_target="tpu_custom_call" | custom-call | tf_op jit(solution)/shard_map/outer/pallas_call | solution.py:547
Async XLA Ops:
  3.4 15.4 %collective-permute-start = (bf16[320,128]{1,0:T(8,128)(2,1)}, bf16[320,128]{1,0:T(8,128)(2,1)S(1)}, u32[]{:S(2)}, u32[]{:S(2)}) collective-permute-start(bf16[320,128]{1,0:T(8,128)(2,1)} %get-tuple-element.29), channel_id=1, source_target_pairs={{0,24},{4,28},{8,0},{12,4},{16,8},{20,12},{24,16},{28,20},{1,25},{... | collective-permute-start | bytes 245768 | tf_op jit(solution)/shard_map/ppermute | solution.py:573
  8.5 10.3 %collective-permute-start.1 = (bf16[320,128]{1,0:T(8,128)(2,1)}, bf16[320,128]{1,0:T(8,128)(2,1)S(1)}, u32[]{:S(2)}, u32[]{:S(2)}) collective-permute-start(bf16[320,128]{1,0:T(8,128)(2,1)} %get-tuple-element.30), channel_id=1, source_target_pairs={{0,28},{4,0},{8,4},{12,8},{16,12},{20,16},{24,20},{28,24},{1,29},{... | collective-permute-start | bytes 245768 | tf_op jit(solution)/shard_map/ppermute | solution.py:573
  9.9 8.9 %collective-permute-start.2 = (bf16[320,128]{1,0:T(8,128)(2,1)}, bf16[320,128]{1,0:T(8,128)(2,1)S(1)}, u32[]{:S(2)}, u32[]{:S(2)}) collective-permute-start(bf16[320,128]{1,0:T(8,128)(2,1)} %get-tuple-element.32), channel_id=1, source_target_pairs={{0,4},{4,8},{8,12},{12,16},{16,20},{20,24},{24,28},{28,0},{1,5},{5... | collective-permute-start | bytes 245768 | tf_op jit(solution)/shard_map/ppermute | solution.py:573
  10.6 8.3 %collective-permute-start.3 = (bf16[320,128]{1,0:T(8,128)(2,1)}, bf16[320,128]{1,0:T(8,128)(2,1)S(1)}, u32[]{:S(2)}, u32[]{:S(2)}) collective-permute-start(bf16[320,128]{1,0:T(8,128)(2,1)} %get-tuple-element.33), channel_id=1, source_target_pairs={{0,8},{4,12},{8,16},{12,20},{16,24},{20,28},{24,0},{28,4},{1,9},{5... | collective-permute-start | bytes 245768 | tf_op jit(solution)/shard_map/ppermute | solution.py:573
  11.5 0.7 %copy-start.11 = (f32[8,128]{1,0:T(8,128)S(1)}, f32[8,128]{1,0:T(8,128)}, u32[]{:S(2)}) copy-start(f32[8,128]{1,0:T(8,128)} %get-tuple-element.34.marks) | copy-start | bytes 12292
  12.2 1.3 %copy-start = (f32[128,5,512]{2,0,1:T(8,128)S(1)}, f32[128,5,512]{2,0,1:T(8,128)}, u32[]{:S(2)}) copy-start(f32[128,5,512]{2,0,1:T(8,128)} %param.15) | copy-start | bytes 3932164
  12.2 1.3 %copy-start.4 = (bf16[256,256]{1,0:T(8,128)(2,1)S(1)}, bf16[256,256]{1,0:T(8,128)(2,1)}, u32[]{:S(2)}) copy-start(bf16[256,256]{1,0:T(8,128)(2,1)} %constant.19.clone.wb1) | copy-start | bytes 393220
  12.2 1.3 %copy-start.5 = (bf16[256,256]{1,0:T(8,128)(2,1)S(1)}, bf16[256,256]{1,0:T(8,128)(2,1)}, u32[]{:S(2)}) copy-start(bf16[256,256]{1,0:T(8,128)(2,1)} %constant.17.clone.wf1) | copy-start | bytes 393220
  12.2 1.3 %copy-start.6 = (bf16[256,128]{1,0:T(8,128)(2,1)S(1)}, bf16[256,128]{1,0:T(8,128)(2,1)}, u32[]{:S(2)}) copy-start(bf16[256,128]{1,0:T(8,128)(2,1)} %constant.20.clone.wb2) | copy-start | bytes 196612
  12.2 1.3 %copy-start.7 = (bf16[128,256]{1,0:T(8,128)(2,1)S(1)}, bf16[128,256]{1,0:T(8,128)(2,1)}, u32[]{:S(2)}) copy-start(bf16[128,256]{1,0:T(8,128)(2,1)} %constant.18.clone.wf2) | copy-start | bytes 196612
  12.2 1.6 %copy-start.9 = (f32[128,3,512]{2,0,1:T(8,128)S(1)}, f32[128,3,512]{2,0,1:T(8,128)}, u32[]{:S(2)}) copy-start(f32[128,3,512]{2,0,1:T(8,128)} %param.16) | copy-start | bytes 2359300
  12.2 1.8 %copy-start.10 = (f32[128,3,512]{2,0,1:T(8,128)S(1)}, f32[128,3,512]{2,0,1:T(8,128)}, u32[]{:S(2)}) copy-start(f32[128,3,512]{2,0,1:T(8,128)} %param.17) | copy-start | bytes 2359300
  12.2 1.8 %copy-start.12 = (f32[48,128]{1,0:T(8,128)S(1)}, f32[48,128]{1,0:T(8,128)}, u32[]{:S(2)}) copy-start(f32[48,128]{1,0:T(8,128)} %constant.21.clone.coef) | copy-start | bytes 73732
  14.1 4.8 %copy-start.1 = (f32[320,128]{1,0:T(8,128)S(1)}, f32[320,128]{1,0:T(8,128)}, u32[]{:S(2)}) copy-start(f32[320,128]{1,0:T(8,128)} %get-tuple-element.42.own) | copy-start | bytes 491524
  14.1 4.8 %copy-start.8 = (f32[16,128]{1,0:T(8,128)S(1)}, f32[16,128]{1,0:T(8,128)}, u32[]{:S(2)}) copy-start(f32[16,128]{1,0:T(8,128)} %get-tuple-element.45.edges) | copy-start | bytes 24580
  14.1 9.4 %copy-start.2 = (bf16[256,1024]{1,0:T(8,128)(2,1)S(1)}, bf16[256,1024]{1,0:T(8,128)(2,1)}, u32[]{:S(2)}) copy-start(bf16[256,1024]{1,0:T(8,128)(2,1)} %constant.23.clone.place) | copy-start | bytes 1572868
  14.1 9.4 %copy-start.3 = (bf16[256,1024]{1,0:T(8,128)(2,1)S(1)}, bf16[256,1024]{1,0:T(8,128)(2,1)}, u32[]{:S(2)}) copy-start(bf16[256,1024]{1,0:T(8,128)(2,1)} %constant.22.clone.spread) | copy-start | bytes 1572868
  19.0 3.6 %collective-permute-start.4 = (f32[8,128]{1,0:T(8,128)S(1)}, f32[8,128]{1,0:T(8,128)S(1)}, u32[]{:S(2)}, u32[]{:S(2)}) collective-permute-start(f32[8,128]{1,0:T(8,128)S(1)} %get-tuple-element.46), channel_id=1, source_target_pairs={{1,2},{2,1},{3,4},{4,3},{5,6},{6,5},{7,8},{8,7},{9,10},{10,9},{11,... | collective-permute-start | bytes 12296 | tf_op jit(solution)/shard_map/ppermute | solution.py:581
  19.7 3.8 %collective-permute-start.5 = (f32[8,128]{1,0:T(8,128)S(1)}, f32[8,128]{1,0:T(8,128)S(1)}, u32[]{:S(2)}, u32[]{:S(2)}) collective-permute-start(f32[8,128]{1,0:T(8,128)S(1)} %get-tuple-element.47), channel_id=1, source_target_pairs={{0,1},{1,0},{2,3},{3,2},{4,5},{5,4},{6,7},{7,6},{8,9},{9,8},{10,11... | collective-permute-start | bytes 12296 | tf_op jit(solution)/shard_map/ppermute | solution.py:582

commit v2 on v1

--- a/solution.py
+++ b/solution.py
@@ -322,13 +322,9 @@
     return wide[:, :128] + wide[:, 128:] + low
 
 
-def main_kernel(
-    x_ref, met, vel, keep_ref, wf1, wf2, wb1, wb2, coef, out, q_out, plane_out, end_q, end_mv,
-):
-    lane, row = iota(1), iota(0)
-    keep = keep_ref[...]
+def factors_of(met, vel, wb1, wb2, coef, q_out, plane_out, end_q, end_mv):
+    lane = iota(1)
     left = lane < 64
-
     for c in range(4):
         at = slice(128 * c, 128 * c + 128)
         w = met[1, :, at] * coef[32:33] + jnp.where(lane % 64 < 8, vel[1, :, at], 0.0)
@@ -365,7 +361,16 @@
         for n, (ref, d) in enumerate(((met, 1), (met, 2), (vel, 1), (vel, 2))):
             end_mv[end, n] = ref[d, rows, at]
 
-    def field(f, carry):
+
+def main_kernel(fields, x_ref, met, vel, keep_ref, wf1, wf2, wb1, wb2, coef, out, *factors):
+    lane, row = iota(1), iota(0)
+    keep = keep_ref[...]
+    left = lane < 64
+    if factors:
+        factors_of(met, vel, wb1, wb2, coef, *factors)
+
+    def field(n, carry):
+        f = n + fields[0]
         x = [x_ref[f, :, 128 * c : 128 * c + 128] * keep for c in range(4)]
         low_faces = pltpu.roll(swap(x[0]), E - 1, 0)
         high_faces = pltpu.roll(swap(x[3]), 1, 0)
@@ -383,10 +388,10 @@
             inner0.append(met[0, :, at] * g0[c] + vel[0, :, at] * x[c])
         back = along_first(inner0, coef, 16)
         for c in range(4):
-            out[f, :, 128 * c : 128 * c + 128] = rest[E * c : E * c + E] + back[c]
+            out[n, :, 128 * c : 128 * c + 128] = rest[E * c : E * c + E] + back[c]
         return carry
 
-    lax.fori_loop(0, 5, field, 0)
+    lax.fori_loop(0, len(fields), field, 0)
 
 
 def keep_kernel(marks, out):
@@ -409,21 +414,22 @@
     )(marks)
 
 
-def main_of(adjoint, metric, velocity, keep, tables):
+def main_of(adjoint, metric, velocity, keep, tables, fields, factors):
+    def body(*refs):
+        main_kernel(fields, *refs)
+
     return pl.pallas_call(
-        main_kernel,
+        body,
         out_shape=[
-            jax.ShapeDtypeStruct((5, E, 512), F32),
-            jax.ShapeDtypeStruct((E, 512), F32),
-            jax.ShapeDtypeStruct((4, E, 128), F32),
-            jax.ShapeDtypeStruct((2, 4, 8, 128), F32),
-            jax.ShapeDtypeStruct((2, 4, 8, 128), F32),
+            jax.ShapeDtypeStruct(shape, F32)
+            for shape in [(len(fields), E, 512)]
+            + [(E, 512), (4, E, 128), (2, 4, 8, 128), (2, 4, 8, 128)] * factors
         ],
         in_specs=[VM] * 9,
-        out_specs=[VM] * 5,
+        out_specs=[VM] * (5 if factors else 1),
         compiler_params=pltpu.CompilerParams(vmem_limit_bytes=LIMIT),
         cost_estimate=pl.CostEstimate(
-            flops=4_000_000_000, bytes_accessed=6_000_000, transcendentals=0
+            flops=800_000_000 * len(fields), bytes_accessed=5_000_000, transcendentals=0
         ),
         name="inner",
     )(
@@ -467,7 +473,7 @@
 
 
 def post_kernel(
-    a, b, own, c2, d, across, inside, base, q_ref, plane, end_q, end_mv,
+    a, b, own, c2, d, across, inside, base_a, base_b, q_ref, plane, end_q, end_mv,
     wf1, wf2, wb1, wb2, spread, place, out_hbm, out, out_sems,
 ):
     out_copies = [
@@ -524,7 +530,7 @@
         for f in range(2 * n, min(2 * n + 2, 5)):
             cols = slice(512 * (f - 2 * n), 512 * (f - 2 * n) + 512)
             out[f] = (
-                base[f]
+                (base_a[f] if f < 2 else base_b[f - 2])
                 + q_ref[...] * dot(y_parts[rows], spread[:, cols])
                 + dot(r_parts[rows], place[:, cols])
             )
@@ -547,7 +553,7 @@
     return pl.pallas_call(
         post_kernel,
         out_shape=jax.ShapeDtypeStruct((5, E, 512), F32),
-        in_specs=[VM] * 18,
+        in_specs=[VM] * 19,
         out_specs=HBM,
         scratch_shapes=[pltpu.VMEM((5, E, 512), F32), pltpu.SemaphoreType.DMA((5,))],
         compiler_params=pltpu.CompilerParams(vmem_limit_bytes=LIMIT),
@@ -571,16 +577,19 @@
     for o in (0, 4, 1, 3):
         pairs = [(i, (i + o - 2) % peers) for i in range(peers)]
         parts[o] = lax.ppermute(parts[o], "dom", pairs)
-    local = main_of(adjoint, met, vel, kept_of(marks), tables)
-    parts, local = lax.optimization_barrier((parts, local))
-    out_a, out_b = lines_of(parts, edges)
+    kept = kept_of(marks)
+    early, *factors = main_of(adjoint, met, vel, kept, tables, (0, 1), True)
+    parts, early = lax.optimization_barrier((parts, early))
+    lines = lines_of(parts, edges)
+    (out_a, out_b), kept = lax.optimization_barrier((lines, kept))
     axes = ("dom", "sub")
     count = lax.axis_size(axes)
     inside = [(i, i ^ 1) for i in range(count)]
     across = [(i, i + 1 if i % 2 else i - 1) for i in range(1, count - 1)]
     outward = lax.ppermute(out_a, axes, across)
     inward = lax.ppermute(out_b, axes, inside)
-    result = post_of(parts, outward, inward, local, tables)
+    (late,) = main_of(adjoint, met, vel, kept, tables, (2, 3, 4), False)
+    result = post_of(parts, outward, inward, (early, late, *factors), tables)
     return jnp.transpose(result, (1, 0, 2))
 
 

time: 25.7 us -> 26.2 us (1.019)
  waiting for transfers between devices: 0.83 us -> 1.3 us
    ppermute x4, waiting for transfers between devices: 0.01 us -> 1.29 us  [shards(): parts[o] = lax.ppermute(parts[o], 'dom', pairs)]
    ppermute x1, waiting for transfers between devices: 0.82 us -> 0.01 us  [shards(): inward = lax.ppermute(out_b, axes, inside)]
    pallas_call x1 -> x2, Pallas kernels: 4.74 us -> 4.76 us  [main_of(): pl.pallas_call(body, out_shape=[jax.ShapeDtypeStruct(shape, F32) for shap...]
where the time goes in v2:
time: 26.2 us; the launch traced here: 26 us
  starting transfers between devices  11.8 us (45%)
  Pallas kernels  10.4 us (40%)
  local copies, waits for them, and re-layouts  2.41 us (9%)
  waiting for transfers between devices  1.3 us (5%)
    ppermute x4, starting transfers between devices, shards(): parts[o] = lax.ppermute(parts[o], 'dom', pairs)  8.05 us
    pallas_call x2, Pallas kernels, main_of(): pl.pallas_call(body, out_shape=[jax.ShapeDtypeStruct(shape, F32) for shap...  4.76 us
    pallas_call x1, Pallas kernels, folded_of(): pl.pallas_call(fold_kernel, out_shape=[jax.ShapeDtypeStruct((320, 128), F...  3.43 us
    ppermute x1, starting transfers between devices, shards(): inward = lax.ppermute(out_b, axes, inside)  2.94 us
    unnamed x26, local copies, waits for them, and re-layouts  2.41 us
    pallas_call x1, Pallas kernels, post_of(): pl.pallas_call(post_kernel, out_shape=jax.ShapeDtypeStruct((5, E, 512), F...  1.92 us
    ppermute x4, waiting for transfers between devices, shards(): parts[o] = lax.ppermute(parts[o], 'dom', pairs)  1.29 us
    ppermute x1, starting transfers between devices, shards(): outward = lax.ppermute(out_a, axes, across)  0.78 us
  transfers between devices with their start and end apart: 6, of which 1 were waited for; matrix products, arithmetic and copies ran while one was open for 0% of the time, Pallas kernels for 19%

profile of v2, /device:TPU:0, one launch (start us, length us, event | category | flops | bytes accessed | tf_op | source)
XLA Modules:
  0.0 26.0 jit_solution(7248126582548861253)
XLA Ops:
  0.0 3.4 %fold.1 = (bf16[320,128]{1,0:T(8,128)(2,1)}, bf16[320,128]{1,0:T(8,128)(2,1)}, f32[320,128]{1,0:T(8,128)}, bf16[320,128]{1,0:T(8,128)(2,1)}, bf16[320,128]{1,0:T...) custom-call(s32[1,128]{1,0:T(1,128)} %bitcast.15, s32[1,128]{1,0:T(1,128)} %bitcast.16, s32[1,128]{1,0:T(1,128)} %bitcast.17, ...), custom_call_target="tpu_custom_call" | custom-call | tf_op jit(solution)/shard_map/fold/pallas_call | solution.py:271
  3.4 5.1 %collective-permute-start = (bf16[320,128]{1,0:T(8,128)(2,1)}, bf16[320,128]{1,0:T(8,128)(2,1)S(1)}, u32[]{:S(2)}, u32[]{:S(2)}) collective-permute-start(bf16[320,128]{1,0:T(8,128)(2,1)} %get-tuple-element.28), channel_id=1, source_target_pairs={{0,24},{4,28},{8,0},{12,4},{16,8},{20,12},{24,16},{28,20},{1,25},{... | collective-permute-start | bytes 245768 | tf_op jit(solution)/shard_map/ppermute | solution.py:579
  8.5 1.4 %collective-permute-start.1 = (bf16[320,128]{1,0:T(8,128)(2,1)}, bf16[320,128]{1,0:T(8,128)(2,1)S(1)}, u32[]{:S(2)}, u32[]{:S(2)}) collective-permute-start(bf16[320,128]{1,0:T(8,128)(2,1)} %get-tuple-element.29), channel_id=1, source_target_pairs={{0,28},{4,0},{8,4},{12,8},{16,12},{20,16},{24,20},{28,24},{1,29},{... | collective-permute-start | bytes 245768 | tf_op jit(solution)/shard_map/ppermute | solution.py:579
  9.9 0.7 %collective-permute-start.2 = (bf16[320,128]{1,0:T(8,128)(2,1)}, bf16[320,128]{1,0:T(8,128)(2,1)S(1)}, u32[]{:S(2)}, u32[]{:S(2)}) collective-permute-start(bf16[320,128]{1,0:T(8,128)(2,1)} %get-tuple-element.31), channel_id=1, source_target_pairs={{0,4},{4,8},{8,12},{12,16},{16,20},{20,24},{24,28},{28,0},{1,5},{5... | collective-permute-start | bytes 245768 | tf_op jit(solution)/shard_map/ppermute | solution.py:579
  10.6 0.9 %collective-permute-start.3 = (bf16[320,128]{1,0:T(8,128)(2,1)}, bf16[320,128]{1,0:T(8,128)(2,1)S(1)}, u32[]{:S(2)}, u32[]{:S(2)}) collective-permute-start(bf16[320,128]{1,0:T(8,128)(2,1)} %get-tuple-element.32), channel_id=1, source_target_pairs={{0,8},{4,12},{8,16},{12,20},{16,24},{20,28},{24,0},{28,4},{1,9},{5... | collective-permute-start | bytes 245768 | tf_op jit(solution)/shard_map/ppermute | solution.py:579
  11.5 0.0 copy-start.11
  11.5 0.7 %copy-done.11 = f32[8,128]{1,0:T(8,128)S(1)} copy-done((f32[8,128]{1,0:T(8,128)S(1)}, f32[8,128]{1,0:T(8,128)}, u32[]{:S(2)}) %copy-start.11) | copy-done | bytes 4120
  12.2 0.0 copy-start
  12.2 0.0 copy-start.4
  12.2 0.0 copy-start.5
  12.2 0.0 copy-start.6
  12.2 0.0 copy-start.7
  12.2 0.0 copy-start.9
  12.2 0.0 copy-start.10
  12.2 0.0 copy-start.12
  12.2 0.1 keep.1.refs_3_
  12.4 1.1 %copy-done = f32[128,5,512]{2,0,1:T(8,128)S(1)} copy-done((f32[128,5,512]{2,0,1:T(8,128)S(1)}, f32[128,5,512]{2,0,1:T(8,128)}, u32[]{:S(2)}) %copy-start) | copy-done | bytes 1310744
  13.5 0.0 copy-done.4
  13.5 0.0 copy-done.5
  13.5 0.0 copy-done.6
  13.5 0.0 copy-done.7
  13.5 0.3 %copy-done.9 = f32[128,3,512]{2,0,1:T(8,128)S(1)} copy-done((f32[128,3,512]{2,0,1:T(8,128)S(1)}, f32[128,3,512]{2,0,1:T(8,128)}, u32[]{:S(2)}) %copy-start.9) | copy-done | bytes 786456
  13.8 0.2 copy-done.10
  14.1 0.0 copy-done.12
  14.1 0.0 copy-start.1
  14.1 0.0 copy-start.8
  14.1 2.4 %inner.2 = (f32[2,128,512]{2,1,0:T(8,128)S(1)}, f32[128,512]{1,0:T(8,128)S(1)}, f32[4,128,128]{2,1,0:T(8,128)S(1)}, f32[2,4,8,128]{3,2,1,0:T(8,128)S(1)}, f32[2,4,8,128]{3,2,1,0:T(8,128)S(1)}) custom-call(f32[5,128,512]{2,1,0:T(8,128)S(1)} %bitcast.9, f32[3,128,512]{2,1,0:T(8,128)S(1)} %bitcast.11, f32[3,128,512]{2,1,0:T(8,128)S(1)} %bitcast.13, ...), custom_call_target="tpu_custom_call" | custom-call | flops 1600000000 | bytes 5000000 | tf_op jit(solution)/shard_map/inner/pallas_call | solution.py:421
  16.4 0.0 collective-permute-done.a
  16.4 0.0 collective-permute-done.1.b
  16.5 1.3 %collective-permute-done.2.c.c2 = bf16[320,128]{1,0:T(8,128)(2,1)S(1)} collective-permute-done((bf16[320,128]{1,0:T(8,128)(2,1)}, bf16[320,128]{1,0:T(8,128)(2,1)S(1)}, u32[]{:S(2)}, u32[]{:S(2)}) %collective-permute-start.2) | collective-permute-done | bytes 81952 | tf_op jit(solution)/shard_map/ppermute | solution.py:579
  17.7 0.0 collective-permute-done.3.d
  17.7 0.0 copy-done.1
  17.7 0.0 copy-done.8
  17.8 0.1 lines.1
  17.9 0.0 copy-start.2
  17.9 0.0 copy-start.3
  17.9 0.8 %collective-permute-start.4 = (f32[8,128]{1,0:T(8,128)S(1)}, f32[8,128]{1,0:T(8,128)S(1)}, u32[]{:S(2)}, u32[]{:S(2)}) collective-permute-start(f32[8,128]{1,0:T(8,128)S(1)} %get-tuple-element.43), channel_id=1, source_target_pairs={{1,2},{2,1},{3,4},{4,3},{5,6},{6,5},{7,8},{8,7},{9,10},{10,9},{11,... | collective-permute-start | bytes 12296 | tf_op jit(solution)/shard_map/ppermute | solution.py:589
  18.7 2.9 %collective-permute-start.5 = (f32[8,128]{1,0:T(8,128)S(1)}, f32[8,128]{1,0:T(8,128)S(1)}, u32[]{:S(2)}, u32[]{:S(2)}) collective-permute-start(f32[8,128]{1,0:T(8,128)S(1)} %get-tuple-element.44), channel_id=1, source_target_pairs={{0,1},{1,0},{2,3},{3,2},{4,5},{5,4},{6,7},{7,6},{8,9},{9,8},{10,11... | collective-permute-start | bytes 12296 | tf_op jit(solution)/shard_map/ppermute | solution.py:590
  21.6 2.4 %inner.3.base_b = f32[3,128,512]{2,1,0:T(8,128)S(1)} custom-call(f32[5,128,512]{2,1,0:T(8,128)S(1)} %bitcast.10, f32[3,128,512]{2,1,0:T(8,128)S(1)} %bitcast.12, f32[3,128,512]{2,1,0:T(8,128)S(1)} %bitcast.14, f32[128,128]{1,0:T(8,128)S(1)} %keep.1.refs_3_, bf16[256,256]{1,0:T(8,128)(2,1)S(1)} %copy-done.5, bf16[128,256]{1,0:T(8,128)(2,1)S(1)} %copy-done.7, ...), custom_call_target="tpu_custom_call" | custom-call | flops 2400000000 | bytes 5000000 | tf_op jit(solution)/shard_map/inner/pallas_call | solution.py:421
  24.0 0.0 collective-permute-done.4.across
  24.1 0.0 collective-permute-done.5.inside
  24.1 0.0 copy-done.2
  24.1 0.0 copy-done.3
  24.1 1.9 %outer.1 = f32[5,128,512]{2,1,0:T(8,128)} custom-call(bf16[320,128]{1,0:T(8,128)(2,1)S(1)} %collective-permute-done.a, bf16[320,128]{1,0:T(8,128)(2,1)S(1)} %collective-permute-done.1.b, f32[320,128]{1,0:T(8,128)S(1)} %copy-done.1, bf16[320,128]{1,0:T(8,128)(2,1)S(1)} %collective-permute-done.2.c.c2, bf16[320,128]{1,0:T(8,128)(2,1)S(1)} %collective-permute-done.3.d, ...), custom_call_target="tpu_custom_call" | custom-call | tf_op jit(solution)/shard_map/outer/pallas_call | solution.py:553
Async XLA Ops:
  3.4 13.0 %collective-permute-start = (bf16[320,128]{1,0:T(8,128)(2,1)}, bf16[320,128]{1,0:T(8,128)(2,1)S(1)}, u32[]{:S(2)}, u32[]{:S(2)}) collective-permute-start(bf16[320,128]{1,0:T(8,128)(2,1)} %get-tuple-element.28), channel_id=1, source_target_pairs={{0,24},{4,28},{8,0},{12,4},{16,8},{20,12},{24,16},{28,20},{1,25},{... | collective-permute-start | bytes 245768 | tf_op jit(solution)/shard_map/ppermute | solution.py:579
  8.5 7.9 %collective-permute-start.1 = (bf16[320,128]{1,0:T(8,128)(2,1)}, bf16[320,128]{1,0:T(8,128)(2,1)S(1)}, u32[]{:S(2)}, u32[]{:S(2)}) collective-permute-start(bf16[320,128]{1,0:T(8,128)(2,1)} %get-tuple-element.29), channel_id=1, source_target_pairs={{0,28},{4,0},{8,4},{12,8},{16,12},{20,16},{24,20},{28,24},{1,29},{... | collective-permute-start | bytes 245768 | tf_op jit(solution)/shard_map/ppermute | solution.py:579
  9.9 7.8 %collective-permute-start.2 = (bf16[320,128]{1,0:T(8,128)(2,1)}, bf16[320,128]{1,0:T(8,128)(2,1)S(1)}, u32[]{:S(2)}, u32[]{:S(2)}) collective-permute-start(bf16[320,128]{1,0:T(8,128)(2,1)} %get-tuple-element.31), channel_id=1, source_target_pairs={{0,4},{4,8},{8,12},{12,16},{16,20},{20,24},{24,28},{28,0},{1,5},{5... | collective-permute-start | bytes 245768 | tf_op jit(solution)/shard_map/ppermute | solution.py:579
  10.6 7.2 %collective-permute-start.3 = (bf16[320,128]{1,0:T(8,128)(2,1)}, bf16[320,128]{1,0:T(8,128)(2,1)S(1)}, u32[]{:S(2)}, u32[]{:S(2)}) collective-permute-start(bf16[320,128]{1,0:T(8,128)(2,1)} %get-tuple-element.32), channel_id=1, source_target_pairs={{0,8},{4,12},{8,16},{12,20},{16,24},{20,28},{24,0},{28,4},{1,9},{5... | collective-permute-start | bytes 245768 | tf_op jit(solution)/shard_map/ppermute | solution.py:579
  11.5 0.7 %copy-start.11 = (f32[8,128]{1,0:T(8,128)S(1)}, f32[8,128]{1,0:T(8,128)}, u32[]{:S(2)}) copy-start(f32[8,128]{1,0:T(8,128)} %get-tuple-element.33.marks) | copy-start | bytes 12292
  12.2 1.3 %copy-start = (f32[128,5,512]{2,0,1:T(8,128)S(1)}, f32[128,5,512]{2,0,1:T(8,128)}, u32[]{:S(2)}) copy-start(f32[128,5,512]{2,0,1:T(8,128)} %param.15) | copy-start | bytes 3932164
  12.2 1.3 %copy-start.4 = (bf16[256,256]{1,0:T(8,128)(2,1)S(1)}, bf16[256,256]{1,0:T(8,128)(2,1)}, u32[]{:S(2)}) copy-start(bf16[256,256]{1,0:T(8,128)(2,1)} %constant.19.clone.refs_6_.wb1) | copy-start | bytes 393220
  12.2 1.3 %copy-start.5 = (bf16[256,256]{1,0:T(8,128)(2,1)S(1)}, bf16[256,256]{1,0:T(8,128)(2,1)}, u32[]{:S(2)}) copy-start(bf16[256,256]{1,0:T(8,128)(2,1)} %constant.17.clone.refs_4_.wf1) | copy-start | bytes 393220
  12.2 1.3 %copy-start.6 = (bf16[256,128]{1,0:T(8,128)(2,1)S(1)}, bf16[256,128]{1,0:T(8,128)(2,1)}, u32[]{:S(2)}) copy-start(bf16[256,128]{1,0:T(8,128)(2,1)} %constant.20.clone.refs_7_.wb2) | copy-start | bytes 196612
  12.2 1.3 %copy-start.7 = (bf16[128,256]{1,0:T(8,128)(2,1)S(1)}, bf16[128,256]{1,0:T(8,128)(2,1)}, u32[]{:S(2)}) copy-start(bf16[128,256]{1,0:T(8,128)(2,1)} %constant.18.clone.refs_5_.wf2) | copy-start | bytes 196612
  12.2 1.6 %copy-start.9 = (f32[128,3,512]{2,0,1:T(8,128)S(1)}, f32[128,3,512]{2,0,1:T(8,128)}, u32[]{:S(2)}) copy-start(f32[128,3,512]{2,0,1:T(8,128)} %param.16) | copy-start | bytes 2359300
  12.2 1.8 %copy-start.10 = (f32[128,3,512]{2,0,1:T(8,128)S(1)}, f32[128,3,512]{2,0,1:T(8,128)}, u32[]{:S(2)}) copy-start(f32[128,3,512]{2,0,1:T(8,128)} %param.17) | copy-start | bytes 2359300
  12.2 1.8 %copy-start.12 = (f32[48,128]{1,0:T(8,128)S(1)}, f32[48,128]{1,0:T(8,128)}, u32[]{:S(2)}) copy-start(f32[48,128]{1,0:T(8,128)} %constant.21.clone.refs_8_) | copy-start | bytes 73732
  14.1 3.7 %copy-start.1 = (f32[320,128]{1,0:T(8,128)S(1)}, f32[320,128]{1,0:T(8,128)}, u32[]{:S(2)}) copy-start(f32[320,128]{1,0:T(8,128)} %get-tuple-element.37.own) | copy-start | bytes 491524
  14.1 3.7 %copy-start.8 = (f32[16,128]{1,0:T(8,128)S(1)}, f32[16,128]{1,0:T(8,128)}, u32[]{:S(2)}) copy-start(f32[16,128]{1,0:T(8,128)} %get-tuple-element.40.edges) | copy-start | bytes 24580
  17.9 6.2 %copy-start.2 = (bf16[256,1024]{1,0:T(8,128)(2,1)S(1)}, bf16[256,1024]{1,0:T(8,128)(2,1)}, u32[]{:S(2)}) copy-start(bf16[256,1024]{1,0:T(8,128)(2,1)} %constant.23.clone.place) | copy-start | bytes 1572868
  17.9 6.2 %copy-start.3 = (bf16[256,1024]{1,0:T(8,128)(2,1)S(1)}, bf16[256,1024]{1,0:T(8,128)(2,1)}, u32[]{:S(2)}) copy-start(bf16[256,1024]{1,0:T(8,128)(2,1)} %constant.22.clone.spread) | copy-start | bytes 1572868
  17.9 6.1 %collective-permute-start.4 = (f32[8,128]{1,0:T(8,128)S(1)}, f32[8,128]{1,0:T(8,128)S(1)}, u32[]{:S(2)}, u32[]{:S(2)}) collective-permute-start(f32[8,128]{1,0:T(8,128)S(1)} %get-tuple-element.43), channel_id=1, source_target_pairs={{1,2},{2,1},{3,4},{4,3},{5,6},{6,5},{7,8},{8,7},{9,10},{10,9},{11,... | collective-permute-start | bytes 12296 | tf_op jit(solution)/shard_map/ppermute | solution.py:589
  18.7 5.4 %collective-permute-start.5 = (f32[8,128]{1,0:T(8,128)S(1)}, f32[8,128]{1,0:T(8,128)S(1)}, u32[]{:S(2)}, u32[]{:S(2)}) collective-permute-start(f32[8,128]{1,0:T(8,128)S(1)} %get-tuple-element.44), channel_id=1, source_target_pairs={{0,1},{1,0},{2,3},{3,2},{4,5},{5,4},{6,7},{7,6},{8,9},{9,8},{10,11... | collective-permute-start | bytes 12296 | tf_op jit(solution)/shard_map/ppermute | solution.py:590

commit v3 on v2

--- a/solution.py
+++ b/solution.py
@@ -197,7 +197,8 @@
 def fold_kernel(
     route_hbm, target_hbm, code_hbm, hang_hbm, adj_hbm, fold_hbm, *refs
 ):
-    outs, edges_out, marks_out, ints, x, fold, wide, sems = refs[:5], *refs[5:]
+    out, ints, x, fold, wide, sems = refs
+    faces_out, edges_out = out.at[0:E], out.at[E : E + 32, 0:128]
     peers = lax.axis_size("dom")
     copies = fetch(
         [(ref, ints.at[n]) for n, ref in enumerate((route_hbm, target_hbm, code_hbm, hang_hbm))]
@@ -211,7 +212,6 @@
     lane = iota(1)
     left = lane < 64
     slot = lax.rem(route - lax.axis_index("dom") + 2 + peers, peers)
-    hit = (iota(0, (5 * E, E)) == slot * E + target).astype(F32).astype(BF16)
     marked = down(jnp.where(hang == 1, code, -2)) - (lane // 64).astype(F32)
     odd = lane % 16 >= 8
     group = (lane // 16 + 1) % 4
@@ -238,21 +238,15 @@
                 marked == 2.0 * q, mapped[E * f : E * f + E, 128 * q : 128 * q + 128], 0.0
             )
         faces.append(total + pltpu.roll(total, 64, 1))
-    f01 = jnp.where(left, faces[0], faces[1]).astype(BF16)
-    f23 = jnp.where(left, faces[2], faces[3]).astype(BF16)
-    sums = dot(hit, jnp.concatenate([f01, f23, faces[4].astype(BF16)], 1))
-    for o in range(5):
-        ref = outs[o]
-        mine = sums[o * E : o * E + E]
-        last = jnp.where(left[:64], mine[:64, 256:384], mine[64:, 256:384])
-        ref[0:128] = mine[:, 0:128].astype(ref.dtype)
-        ref[128:256] = mine[:, 128:256].astype(ref.dtype)
-        ref[256:320] = last.astype(ref.dtype)
-
-    marks_out[...] = jnp.broadcast_to(1.0 - hang.astype(F32), (8, E))
+    faces_out[:, 0:128] = jnp.where(left, faces[0], faces[1])
+    faces_out[:, 128:256] = jnp.where(left, faces[2], faces[3])
+    faces_out[:, 256:384] = faces[4]
+
+    edges_out[...] = jnp.zeros((32, 128), F32)
+    edges_out[16:17] = (slot * E + target).astype(F32)
+    edges_out[17:18] = 1.0 - hang.astype(F32)
     lane = iota(1, (1, 128))
     own = marked[0:1], marked[E - 1 : E]
-    edges_out[...] = jnp.zeros((16, 128), F32)
     for n in range(3):
         first, second = 2 * n, min(2 * n + 1, 4)
         for end, (at, chunk) in enumerate(((0, 0), (E - 1, 3))):
@@ -270,12 +264,9 @@
 def folded_of(route, target, code, hang, adjoint, fold):
     return pl.pallas_call(
         fold_kernel,
-        out_shape=[
-            jax.ShapeDtypeStruct((320, 128), F32 if o == 2 else BF16) for o in range(5)
-        ]
-        + [jax.ShapeDtypeStruct((16, 128), F32), jax.ShapeDtypeStruct((8, 128), F32)],
+        out_shape=jax.ShapeDtypeStruct((E + 32, 384), F32),
         in_specs=[HBM] * 6,
-        out_specs=[VM] * 7,
+        out_specs=VM,
         scratch_shapes=[
             pltpu.VMEM((4, 1, E), jnp.int32),
             pltpu.VMEM((5, E, 512), F32),
@@ -394,24 +385,38 @@
     lax.fori_loop(0, len(fields), field, 0)
 
 
-def keep_kernel(marks, out):
-    kept = jnp.where(iota(0) == iota(1), marks[0:1], 0.0).astype(BF16)
-    column = dot(kept, jnp.ones((E, 128), BF16))
-    out[...] = jnp.where(iota(1) % 64 >= 56, column, 1.0)
-
-
-def kept_of(marks):
+def sum_kernel(both, *outs):
+    faces, edges = both.at[0:E], both.at[E : E + 32, 0:128]
+    column = jnp.where(iota(0) == iota(1), edges[17:18], 0.0).astype(BF16)
+    column = dot(column, jnp.ones((E, 128), BF16))
+    outs[5][...] = jnp.where(iota(1) % 64 >= 56, column, 1.0)
+    spot = edges[16:17].astype(jnp.int32)
+    hit = (iota(0, (5 * E, E)) == spot).astype(F32).astype(BF16)
+    sums = dot(hit, faces[...].astype(BF16))
+    left = iota(1, (64, 128)) < 64
+    for o in range(5):
+        ref = outs[o]
+        mine = sums[o * E : o * E + E]
+        ref[0:128] = mine[:, 0:128].astype(ref.dtype)
+        ref[128:256] = mine[:, 128:256].astype(ref.dtype)
+        ref[256:320] = jnp.where(left, mine[:64, 256:384], mine[64:, 256:384]).astype(ref.dtype)
+
+
+def sums_of(both):
     return pl.pallas_call(
-        keep_kernel,
-        out_shape=jax.ShapeDtypeStruct((E, 128), F32),
+        sum_kernel,
+        out_shape=[
+            jax.ShapeDtypeStruct((320, 128), F32 if o == 2 else BF16) for o in range(5)
+        ]
+        + [jax.ShapeDtypeStruct((E, 128), F32)],
         in_specs=[VM],
-        out_specs=VM,
+        out_specs=[VM] * 6,
         compiler_params=pltpu.CompilerParams(vmem_limit_bytes=16 * 1024 * 1024),
         cost_estimate=pl.CostEstimate(
-            flops=1_200_000_000, bytes_accessed=1_000_000, transcendentals=0
+            flops=8_000_000_000, bytes_accessed=30_000_000, transcendentals=0
         ),
-        name="keep",
-    )(marks)
+        name="sums",
+    )(both)
 
 
 def main_of(adjoint, metric, velocity, keep, tables, fields, factors):
@@ -443,7 +448,8 @@
     return lax.rem(index, 2) == 1
 
 
-def line_kernel(a, b, own, c, d, edges, across, inside):
+def line_kernel(a, b, own, c, d, both, across, inside):
+    edges = both.at[E : E + 32, 0:128]
     def rows(start):
         return sum(ref[start : start + 16].astype(F32) for ref in (a, b, own, c, d))
 
@@ -461,7 +467,7 @@
     inside[...] = jnp.where(odd, low, high)
 
 
-def lines_of(parts, edges):
+def lines_of(parts, both):
     return pl.pallas_call(
         line_kernel,
         out_shape=[jax.ShapeDtypeStruct((8, 128), F32)] * 2,
@@ -469,7 +475,7 @@
         out_specs=[VM] * 2,
         compiler_params=pltpu.CompilerParams(vmem_limit_bytes=LIMIT),
         name="lines",
-    )(*parts, edges)
+    )(*parts, both)
 
 
 def post_kernel(
@@ -573,14 +579,14 @@
     route, target, code, hang = (
         x.reshape(1, E) for x in (mortar_route, mortar_element, face_code, hanging)
     )
-    *parts, edges, marks = folded_of(route, target, code, hang, adjoint, tables["fold"])
-    for o in (0, 4, 1, 3):
+    both = folded_of(route, target, code, hang, adjoint, tables["fold"])
+    *parts, kept = sums_of(both)
+    for o in (0, 4, 3, 1):
         pairs = [(i, (i + o - 2) % peers) for i in range(peers)]
         parts[o] = lax.ppermute(parts[o], "dom", pairs)
-    kept = kept_of(marks)
     early, *factors = main_of(adjoint, met, vel, kept, tables, (0, 1), True)
     parts, early = lax.optimization_barrier((parts, early))
-    lines = lines_of(parts, edges)
+    lines = lines_of(parts, both)
     (out_a, out_b), kept = lax.optimization_barrier((lines, kept))
     axes = ("dom", "sub")
     count = lax.axis_size(axes)

time: 26.2 us -> 27 us (1.031)
  waiting for transfers between devices: 1.3 us -> 3.59 us
  local copies, waits for them, and re-layouts: 2.41 us -> 0.99 us
    ppermute x4, waiting for transfers between devices: 1.29 us -> 3.58 us  [shards(): parts[o] = lax.ppermute(parts[o], 'dom', pairs)]
    unnamed x26 -> x24, local copies, waits for them, and re-layouts: 2.41 us -> 0.99 us
  transfers between devices with their start and end apart: 6 -> 6, of which waited for: 1 -> 1; matrix products, arithmetic and copies ran while one was open for 0% -> 0% of each run, Pallas kernels for 19% -> 18%
where the time goes in v3:
time: 27 us; the launch traced here: 26.8 us
  starting transfers between devices  11.8 us (44%)
  Pallas kernels  10.3 us (38%)
  waiting for transfers between devices  3.59 us (13%)
  local copies, waits for them, and re-layouts  0.99 us (4%)
    ppermute x4, starting transfers between devices, shards(): parts[o] = lax.ppermute(parts[o], 'dom', pairs)  8.05 us
    pallas_call x2, Pallas kernels, main_of(): pl.pallas_call(body, out_shape=[jax.ShapeDtypeStruct(shape, F32) for shap...  4.77 us
    ppermute x4, waiting for transfers between devices, shards(): parts[o] = lax.ppermute(parts[o], 'dom', pairs)  3.58 us
    pallas_call x1, Pallas kernels, folded_of(): pl.pallas_call(fold_kernel, out_shape=jax.ShapeDtypeStruct((E + 32, 384),...  3.17 us
    ppermute x1, starting transfers between devices, shards(): inward = lax.ppermute(out_b, axes, inside)  2.95 us
    pallas_call x1, Pallas kernels, post_of(): pl.pallas_call(post_kernel, out_shape=jax.ShapeDtypeStruct((5, E, 512), F...  1.92 us
    unnamed x24, local copies, waits for them, and re-layouts  0.99 us
    ppermute x1, starting transfers between devices, shards(): outward = lax.ppermute(out_a, axes, across)  0.78 us
  transfers between devices with their start and end apart: 6, of which 1 were waited for; matrix products, arithmetic and copies ran while one was open for 0% of the time, Pallas kernels for 18%

profile of v3, /device:TPU:0, one launch (start us, length us, event | category | flops | bytes accessed | tf_op | source)
XLA Modules:
  0.0 26.8 jit_solution(9173976161662955273)
XLA Ops:
  0.0 3.2 %fold.1.both = f32[160,384]{1,0:T(8,128)} custom-call(s32[1,128]{1,0:T(1,128)} %bitcast.15, s32[1,128]{1,0:T(1,128)} %bitcast.16, s32[1,128]{1,0:T(1,128)} %bitcast.17, s32[1,128]{1,0:T(1,128)} %bitcast.18, f32[5,128,512]{2,1,0:T(8,128)} %bitcast.8, bf16[256,512]{1,0:T(8,128)(2,1)} %constant.16.clone.fold_hbm), custom_call_target="tpu_custom_call" | custom-call | tf_op jit(solution)/shard_map/fold/pallas_call | solution.py:265
  3.2 0.0 copy-start.1
  3.2 0.9 %copy-done.1 = f32[160,384]{1,0:T(8,128)S(1)} copy-done((f32[160,384]{1,0:T(8,128)S(1)}, f32[160,384]{1,0:T(8,128)}, u32[]{:S(2)}) %copy-start.1) | copy-done | bytes 245784
  4.1 0.0 copy-start
  4.1 0.0 copy-start.5
  4.1 0.0 copy-start.6
  4.1 0.0 copy-start.7
  4.1 0.0 copy-start.8
  4.2 0.0 copy-start.9
  4.2 0.0 copy-start.10
  4.2 0.0 copy-start.11
  4.2 0.3 %sums.1 = (bf16[320,128]{1,0:T(8,128)(2,1)S(1)}, bf16[320,128]{1,0:T(8,128)(2,1)S(1)}, f32[320,128]{1,0:T(8,128)S(1)}, bf16[320,128]{1,0:T(8,128)(2,1)S(1)}, bf1...) custom-call(f32[160,384]{1,0:T(8,128)S(1)} %copy-done.1), custom_call_target="tpu_custom_call" | custom-call | flops 8000000000 | bytes 30000000 | tf_op jit(solution)/shard_map/sums/pallas_call | solution.py:406
  4.5 5.1 %collective-permute-start = (bf16[320,128]{1,0:T(8,128)(2,1)S(1)}, bf16[320,128]{1,0:T(8,128)(2,1)S(1)}, u32[]{:S(2)}, u32[]{:S(2)}) collective-permute-start(bf16[320,128]{1,0:T(8,128)(2,1)S(1)} %get-tuple-element.27), channel_id=1, source_target_pairs={{0,24},{4,28},{8,0},{12,4},{16,8},{20,12},{24,16},{28,20},{1,25},{... | collective-permute-start | bytes 245768 | tf_op jit(solution)/shard_map/ppermute | solution.py:586
  9.6 1.4 %collective-permute-start.1 = (bf16[320,128]{1,0:T(8,128)(2,1)S(1)}, bf16[320,128]{1,0:T(8,128)(2,1)S(1)}, u32[]{:S(2)}, u32[]{:S(2)}) collective-permute-start(bf16[320,128]{1,0:T(8,128)(2,1)S(1)} %get-tuple-element.28), channel_id=1, source_target_pairs={{0,28},{4,0},{8,4},{12,8},{16,12},{20,16},{24,20},{28,24},{1,29},{... | collective-permute-start | bytes 245768 | tf_op jit(solution)/shard_map/ppermute | solution.py:586
  11.0 0.6 %collective-permute-start.2 = (bf16[320,128]{1,0:T(8,128)(2,1)S(1)}, bf16[320,128]{1,0:T(8,128)(2,1)S(1)}, u32[]{:S(2)}, u32[]{:S(2)}) collective-permute-start(bf16[320,128]{1,0:T(8,128)(2,1)S(1)} %get-tuple-element.30), channel_id=1, source_target_pairs={{0,4},{4,8},{8,12},{12,16},{16,20},{20,24},{24,28},{28,0},{1,5},{5... | collective-permute-start | bytes 245768 | tf_op jit(solution)/shard_map/ppermute | solution.py:586
  11.6 0.9 %collective-permute-start.3 = (bf16[320,128]{1,0:T(8,128)(2,1)S(1)}, bf16[320,128]{1,0:T(8,128)(2,1)S(1)}, u32[]{:S(2)}, u32[]{:S(2)}) collective-permute-start(bf16[320,128]{1,0:T(8,128)(2,1)S(1)} %get-tuple-element.31), channel_id=1, source_target_pairs={{0,8},{4,12},{8,16},{12,20},{16,24},{20,28},{24,0},{28,4},{1,9},{5... | collective-permute-start | bytes 245768 | tf_op jit(solution)/shard_map/ppermute | solution.py:586
  12.5 0.0 copy-done
  12.5 0.0 copy-done.5
  12.5 0.0 copy-done.6
  12.5 0.0 copy-done.7
  12.5 0.0 copy-done.8
  12.6 0.0 copy-done.9
  12.6 0.0 copy-done.10
  12.6 0.0 copy-done.11
  12.6 0.0 copy-start.2
  12.6 2.4 %inner.2 = (f32[2,128,512]{2,1,0:T(8,128)S(1)}, f32[128,512]{1,0:T(8,128)S(1)}, f32[4,128,128]{2,1,0:T(8,128)S(1)}, f32[2,4,8,128]{3,2,1,0:T(8,128)S(1)}, f32[2,4,8,128]{3,2,1,0:T(8,128)S(1)}) custom-call(f32[5,128,512]{2,1,0:T(8,128)S(1)} %bitcast.9, f32[3,128,512]{2,1,0:T(8,128)S(1)} %bitcast.11, f32[3,128,512]{2,1,0:T(8,128)S(1)} %bitcast.13, ...), custom_call_target="tpu_custom_call" | custom-call | flops 1600000000 | bytes 5000000 | tf_op jit(solution)/shard_map/inner/pallas_call | solution.py:426
  15.0 0.0 collective-permute-done.a
  15.0 0.0 collective-permute-done.1.b
  15.0 3.6 %collective-permute-done.2.c.c2 = bf16[320,128]{1,0:T(8,128)(2,1)S(1)} collective-permute-done((bf16[320,128]{1,0:T(8,128)(2,1)S(1)}, bf16[320,128]{1,0:T(8,128)(2,1)S(1)}, u32[]{:S(2)}, u32[]{:S(2)}) %collective-permute-start.2) | collective-permute-done | bytes 81952 | tf_op jit(solution)/shard_map/ppermute | solution.py:586
  18.6 0.0 collective-permute-done.3.d
  18.6 0.0 copy-done.2
  18.6 0.1 lines.1
  18.7 0.0 copy-start.3
  18.7 0.0 copy-start.4
  18.7 0.8 %collective-permute-start.4 = (f32[8,128]{1,0:T(8,128)S(1)}, f32[8,128]{1,0:T(8,128)S(1)}, u32[]{:S(2)}, u32[]{:S(2)}) collective-permute-start(f32[8,128]{1,0:T(8,128)S(1)} %get-tuple-element.41), channel_id=1, source_target_pairs={{1,2},{2,1},{3,4},{4,3},{5,6},{6,5},{7,8},{8,7},{9,10},{10,9},{11,... | collective-permute-start | bytes 12296 | tf_op jit(solution)/shard_map/ppermute | solution.py:595
  19.5 2.9 %collective-permute-start.5 = (f32[8,128]{1,0:T(8,128)S(1)}, f32[8,128]{1,0:T(8,128)S(1)}, u32[]{:S(2)}, u32[]{:S(2)}) collective-permute-start(f32[8,128]{1,0:T(8,128)S(1)} %get-tuple-element.42), channel_id=1, source_target_pairs={{0,1},{1,0},{2,3},{3,2},{4,5},{5,4},{6,7},{7,6},{8,9},{9,8},{10,11... | collective-permute-start | bytes 12296 | tf_op jit(solution)/shard_map/ppermute | solution.py:596
  22.5 2.4 %inner.3.base_b = f32[3,128,512]{2,1,0:T(8,128)S(1)} custom-call(f32[5,128,512]{2,1,0:T(8,128)S(1)} %bitcast.10, f32[3,128,512]{2,1,0:T(8,128)S(1)} %bitcast.12, f32[3,128,512]{2,1,0:T(8,128)S(1)} %bitcast.14, f32[128,128]{1,0:T(8,128)S(1)} %get-tuple-element.44.refs_3_, bf16[256,256]{1,0:T(8,128)(2,1)S(1)} %copy-done.6, bf16[128,256]{1,0:T(8,128)(2,1)S(1)} %copy-done.8, ...), custom_call_target="tpu_custom_call" | custom-call | flops 2400000000 | bytes 5000000 | tf_op jit(solution)/shard_map/inner/pallas_call | solution.py:426
  24.9 0.0 collective-permute-done.4.across
  24.9 0.0 collective-permute-done.5.inside
  24.9 0.0 copy-done.3
  24.9 0.0 copy-done.4
  24.9 1.9 %outer.1 = f32[5,128,512]{2,1,0:T(8,128)} custom-call(bf16[320,128]{1,0:T(8,128)(2,1)S(1)} %collective-permute-done.a, bf16[320,128]{1,0:T(8,128)(2,1)S(1)} %collective-permute-done.1.b, f32[320,128]{1,0:T(8,128)S(1)} %get-tuple-element.36.own, bf16[320,128]{1,0:T(8,128)(2,1)S(1)} %collective-permute-done.2.c.c2, ...), custom_call_target="tpu_custom_call" | custom-call | tf_op jit(solution)/shard_map/outer/pallas_call | solution.py:559
Async XLA Ops:
  3.2 0.9 %copy-start.1 = (f32[160,384]{1,0:T(8,128)S(1)}, f32[160,384]{1,0:T(8,128)}, u32[]{:S(2)}) copy-start(f32[160,384]{1,0:T(8,128)} %fold.1.both) | copy-start | bytes 737284
  4.1 8.4 %copy-start = (f32[128,5,512]{2,0,1:T(8,128)S(1)}, f32[128,5,512]{2,0,1:T(8,128)}, u32[]{:S(2)}) copy-start(f32[128,5,512]{2,0,1:T(8,128)} %param.15) | copy-start | bytes 3932164
  4.1 8.4 %copy-start.5 = (bf16[256,256]{1,0:T(8,128)(2,1)S(1)}, bf16[256,256]{1,0:T(8,128)(2,1)}, u32[]{:S(2)}) copy-start(bf16[256,256]{1,0:T(8,128)(2,1)} %constant.19.clone.refs_6_.wb1) | copy-start | bytes 393220
  4.1 8.4 %copy-start.6 = (bf16[256,256]{1,0:T(8,128)(2,1)S(1)}, bf16[256,256]{1,0:T(8,128)(2,1)}, u32[]{:S(2)}) copy-start(bf16[256,256]{1,0:T(8,128)(2,1)} %constant.17.clone.refs_4_.wf1) | copy-start | bytes 393220
  4.1 8.4 %copy-start.7 = (bf16[256,128]{1,0:T(8,128)(2,1)S(1)}, bf16[256,128]{1,0:T(8,128)(2,1)}, u32[]{:S(2)}) copy-start(bf16[256,128]{1,0:T(8,128)(2,1)} %constant.20.clone.refs_7_.wb2) | copy-start | bytes 196612
  4.1 8.4 %copy-start.8 = (bf16[128,256]{1,0:T(8,128)(2,1)S(1)}, bf16[128,256]{1,0:T(8,128)(2,1)}, u32[]{:S(2)}) copy-start(bf16[128,256]{1,0:T(8,128)(2,1)} %constant.18.clone.refs_5_.wf2) | copy-start | bytes 196612
  4.2 8.4 %copy-start.9 = (f32[128,3,512]{2,0,1:T(8,128)S(1)}, f32[128,3,512]{2,0,1:T(8,128)}, u32[]{:S(2)}) copy-start(f32[128,3,512]{2,0,1:T(8,128)} %param.16) | copy-start | bytes 2359300
  4.2 8.4 %copy-start.10 = (f32[128,3,512]{2,0,1:T(8,128)S(1)}, f32[128,3,512]{2,0,1:T(8,128)}, u32[]{:S(2)}) copy-start(f32[128,3,512]{2,0,1:T(8,128)} %param.17) | copy-start | bytes 2359300
  4.2 8.4 %copy-start.11 = (f32[48,128]{1,0:T(8,128)S(1)}, f32[48,128]{1,0:T(8,128)}, u32[]{:S(2)}) copy-start(f32[48,128]{1,0:T(8,128)} %constant.21.clone.refs_8_) | copy-start | bytes 73732
  4.5 10.5 %collective-permute-start = (bf16[320,128]{1,0:T(8,128)(2,1)S(1)}, bf16[320,128]{1,0:T(8,128)(2,1)S(1)}, u32[]{:S(2)}, u32[]{:S(2)}) collective-permute-start(bf16[320,128]{1,0:T(8,128)(2,1)S(1)} %get-tuple-element.27), channel_id=1, source_target_pairs={{0,24},{4,28},{8,0},{12,4},{16,8},{20,12},{24,16},{28,20},{1,25},{... | collective-permute-start | bytes 245768 | tf_op jit(solution)/shard_map/ppermute | solution.py:586
  9.6 5.4 %collective-permute-start.1 = (bf16[320,128]{1,0:T(8,128)(2,1)S(1)}, bf16[320,128]{1,0:T(8,128)(2,1)S(1)}, u32[]{:S(2)}, u32[]{:S(2)}) collective-permute-start(bf16[320,128]{1,0:T(8,128)(2,1)S(1)} %get-tuple-element.28), channel_id=1, source_target_pairs={{0,28},{4,0},{8,4},{12,8},{16,12},{20,16},{24,20},{28,24},{1,29},{... | collective-permute-start | bytes 245768 | tf_op jit(solution)/shard_map/ppermute | solution.py:586
  11.0 7.6 %collective-permute-start.2 = (bf16[320,128]{1,0:T(8,128)(2,1)S(1)}, bf16[320,128]{1,0:T(8,128)(2,1)S(1)}, u32[]{:S(2)}, u32[]{:S(2)}) collective-permute-start(bf16[320,128]{1,0:T(8,128)(2,1)S(1)} %get-tuple-element.30), channel_id=1, source_target_pairs={{0,4},{4,8},{8,12},{12,16},{16,20},{20,24},{24,28},{28,0},{1,5},{5... | collective-permute-start | bytes 245768 | tf_op jit(solution)/shard_map/ppermute | solution.py:586
  11.6 7.0 %collective-permute-start.3 = (bf16[320,128]{1,0:T(8,128)(2,1)S(1)}, bf16[320,128]{1,0:T(8,128)(2,1)S(1)}, u32[]{:S(2)}, u32[]{:S(2)}) collective-permute-start(bf16[320,128]{1,0:T(8,128)(2,1)S(1)} %get-tuple-element.31), channel_id=1, source_target_pairs={{0,8},{4,12},{8,16},{12,20},{16,24},{20,28},{24,0},{28,4},{1,9},{5... | collective-permute-start | bytes 245768 | tf_op jit(solution)/shard_map/ppermute | solution.py:586
  12.6 6.0 %copy-start.2 = (f32[160,384]{1,0:T(8,128)S(1)}, f32[160,384]{1,0:T(8,128)}, u32[]{:S(2)}) copy-start(f32[160,384]{1,0:T(8,128)} %fold.1.both) | copy-start | bytes 737284
  18.7 6.2 %copy-start.3 = (bf16[256,1024]{1,0:T(8,128)(2,1)S(1)}, bf16[256,1024]{1,0:T(8,128)(2,1)}, u32[]{:S(2)}) copy-start(bf16[256,1024]{1,0:T(8,128)(2,1)} %constant.23.clone.place) | copy-start | bytes 1572868
  18.7 6.2 %copy-start.4 = (bf16[256,1024]{1,0:T(8,128)(2,1)S(1)}, bf16[256,1024]{1,0:T(8,128)(2,1)}, u32[]{:S(2)}) copy-start(bf16[256,1024]{1,0:T(8,128)(2,1)} %constant.22.clone.spread) | copy-start | bytes 1572868
  18.7 6.1 %collective-permute-start.4 = (f32[8,128]{1,0:T(8,128)S(1)}, f32[8,128]{1,0:T(8,128)S(1)}, u32[]{:S(2)}, u32[]{:S(2)}) collective-permute-start(f32[8,128]{1,0:T(8,128)S(1)} %get-tuple-element.41), channel_id=1, source_target_pairs={{1,2},{2,1},{3,4},{4,3},{5,6},{6,5},{7,8},{8,7},{9,10},{10,9},{11,... | collective-permute-start | bytes 12296 | tf_op jit(solution)/shard_map/ppermute | solution.py:595
  19.5 5.4 %collective-permute-start.5 = (f32[8,128]{1,0:T(8,128)S(1)}, f32[8,128]{1,0:T(8,128)S(1)}, u32[]{:S(2)}, u32[]{:S(2)}) collective-permute-start(f32[8,128]{1,0:T(8,128)S(1)} %get-tuple-element.42), channel_id=1, source_target_pairs={{0,1},{1,0},{2,3},{3,2},{4,5},{5,4},{6,7},{7,6},{8,9},{9,8},{10,11... | collective-permute-start | bytes 12296 | tf_op jit(solution)/shard_map/ppermute | solution.py:596

commit v4 on v3

--- a/solution.py
+++ b/solution.py
@@ -25,6 +25,7 @@
 HBM = pl.BlockSpec(memory_space=pltpu.HBM)
 VM = pl.BlockSpec(memory_space=pltpu.VMEM)
 LIMIT = 32 * 1024 * 1024
+ORDER = (3, 4, 2, 1, 0)
 WHOLE = 64 * 1024 * 1024
 
 
@@ -394,8 +395,7 @@
     hit = (iota(0, (5 * E, E)) == spot).astype(F32).astype(BF16)
     sums = dot(hit, faces[...].astype(BF16))
     left = iota(1, (64, 128)) < 64
-    for o in range(5):
-        ref = outs[o]
+    for ref, o in zip(outs, ORDER):
         mine = sums[o * E : o * E + E]
         ref[0:128] = mine[:, 0:128].astype(ref.dtype)
         ref[128:256] = mine[:, 128:256].astype(ref.dtype)
@@ -581,9 +581,9 @@
     )
     both = folded_of(route, target, code, hang, adjoint, tables["fold"])
     *parts, kept = sums_of(both)
-    for o in (0, 4, 3, 1):
-        pairs = [(i, (i + o - 2) % peers) for i in range(peers)]
-        parts[o] = lax.ppermute(parts[o], "dom", pairs)
+    for n in (0, 1, 3, 4):
+        pairs = [(i, (i + ORDER[n] - 2) % peers) for i in range(peers)]
+        parts[n] = lax.ppermute(parts[n], "dom", pairs)
     early, *factors = main_of(adjoint, met, vel, kept, tables, (0, 1), True)
     parts, early = lax.optimization_barrier((parts, early))
     lines = lines_of(parts, both)

time: 27 us -> 25.2 us (0.933)
  waiting for transfers between devices: 3.59 us -> 1.69 us
    ppermute x4, waiting for transfers between devices: 3.58 us -> 1.68 us  [shards(): parts[n] = lax.ppermute(parts[n], 'dom', pairs)]
  transfers between devices with their start and end apart: 6 -> 6, of which waited for: 1 -> 1; matrix products, arithmetic and copies ran while one was open for 0% -> 0% of each run, Pallas kernels for 18% -> 19%
where the time goes in v4:
time: 25.2 us; the launch traced here: 25 us
  starting transfers between devices  11.8 us (47%)
  Pallas kernels  10.3 us (41%)
  waiting for transfers between devices  1.69 us (7%)
  local copies, waits for them, and re-layouts  0.99 us (4%)
    ppermute x4, starting transfers between devices, shards(): parts[n] = lax.ppermute(parts[n], 'dom', pairs)  8.11 us
    pallas_call x2, Pallas kernels, main_of(): pl.pallas_call(body, out_shape=[jax.ShapeDtypeStruct(shape, F32) for shap...  4.77 us
    pallas_call x1, Pallas kernels, folded_of(): pl.pallas_call(fold_kernel, out_shape=jax.ShapeDtypeStruct((E + 32, 384),...  3.17 us
    ppermute x1, starting transfers between devices, shards(): inward = lax.ppermute(out_b, axes, inside)  2.95 us
    pallas_call x1, Pallas kernels, post_of(): pl.pallas_call(post_kernel, out_shape=jax.ShapeDtypeStruct((5, E, 512), F...  1.92 us
    ppermute x4, waiting for transfers between devices, shards(): parts[n] = lax.ppermute(parts[n], 'dom', pairs)  1.68 us
    unnamed x24, local copies, waits for them, and re-layouts  0.99 us
    ppermute x1, starting transfers between devices, shards(): outward = lax.ppermute(out_a, axes, across)  0.78 us
  transfers between devices with their start and end apart: 6, of which 1 were waited for; matrix products, arithmetic and copies ran while one was open for 0% of the time, Pallas kernels for 19%

profile of v4, /device:TPU:0, one launch (start us, length us, event | category | flops | bytes accessed | tf_op | source)
XLA Modules:
  0.0 25.0 jit_solution(16745640611538337341)
XLA Ops:
  0.0 3.2 %fold.1.both = f32[160,384]{1,0:T(8,128)} custom-call(s32[1,128]{1,0:T(1,128)} %bitcast.15, s32[1,128]{1,0:T(1,128)} %bitcast.16, s32[1,128]{1,0:T(1,128)} %bitcast.17, s32[1,128]{1,0:T(1,128)} %bitcast.18, f32[5,128,512]{2,1,0:T(8,128)} %bitcast.8, bf16[256,512]{1,0:T(8,128)(2,1)} %constant.16.clone.fold_hbm), custom_call_target="tpu_custom_call" | custom-call | tf_op jit(solution)/shard_map/fold/pallas_call | solution.py:266
  3.2 0.0 copy-start.1
  3.2 0.9 %copy-done.1 = f32[160,384]{1,0:T(8,128)S(1)} copy-done((f32[160,384]{1,0:T(8,128)S(1)}, f32[160,384]{1,0:T(8,128)}, u32[]{:S(2)}) %copy-start.1) | copy-done | bytes 245784
  4.1 0.0 copy-start
  4.1 0.0 copy-start.5
  4.1 0.0 copy-start.6
  4.1 0.0 copy-start.7
  4.1 0.0 copy-start.8
  4.2 0.0 copy-start.9
  4.2 0.0 copy-start.10
  4.2 0.0 copy-start.11
  4.2 0.3 %sums.1 = (bf16[320,128]{1,0:T(8,128)(2,1)S(1)}, bf16[320,128]{1,0:T(8,128)(2,1)S(1)}, f32[320,128]{1,0:T(8,128)S(1)}, bf16[320,128]{1,0:T(8,128)(2,1)S(1)}, bf1...) custom-call(f32[160,384]{1,0:T(8,128)S(1)} %copy-done.1), custom_call_target="tpu_custom_call" | custom-call | flops 8000000000 | bytes 30000000 | tf_op jit(solution)/shard_map/sums/pallas_call | solution.py:406
  4.5 3.0 %collective-permute-start = (bf16[320,128]{1,0:T(8,128)(2,1)S(1)}, bf16[320,128]{1,0:T(8,128)(2,1)S(1)}, u32[]{:S(2)}, u32[]{:S(2)}) collective-permute-start(bf16[320,128]{1,0:T(8,128)(2,1)S(1)} %get-tuple-element.27), channel_id=1, source_target_pairs={{0,4},{4,8},{8,12},{12,16},{16,20},{20,24},{24,28},{28,0},{1,5},{5... | collective-permute-start | bytes 245768 | tf_op jit(solution)/shard_map/ppermute | solution.py:586
  7.5 1.6 %collective-permute-start.1 = (bf16[320,128]{1,0:T(8,128)(2,1)S(1)}, bf16[320,128]{1,0:T(8,128)(2,1)S(1)}, u32[]{:S(2)}, u32[]{:S(2)}) collective-permute-start(bf16[320,128]{1,0:T(8,128)(2,1)S(1)} %get-tuple-element.28), channel_id=1, source_target_pairs={{0,8},{4,12},{8,16},{12,20},{16,24},{20,28},{24,0},{28,4},{1,9},{5... | collective-permute-start | bytes 245768 | tf_op jit(solution)/shard_map/ppermute | solution.py:586
  9.1 3.2 %collective-permute-start.2 = (bf16[320,128]{1,0:T(8,128)(2,1)S(1)}, bf16[320,128]{1,0:T(8,128)(2,1)S(1)}, u32[]{:S(2)}, u32[]{:S(2)}) collective-permute-start(bf16[320,128]{1,0:T(8,128)(2,1)S(1)} %get-tuple-element.30), channel_id=1, source_target_pairs={{0,28},{4,0},{8,4},{12,8},{16,12},{20,16},{24,20},{28,24},{1,29},{... | collective-permute-start | bytes 245768 | tf_op jit(solution)/shard_map/ppermute | solution.py:586
  12.3 0.3 %collective-permute-start.3 = (bf16[320,128]{1,0:T(8,128)(2,1)S(1)}, bf16[320,128]{1,0:T(8,128)(2,1)S(1)}, u32[]{:S(2)}, u32[]{:S(2)}) collective-permute-start(bf16[320,128]{1,0:T(8,128)(2,1)S(1)} %get-tuple-element.31), channel_id=1, source_target_pairs={{0,24},{4,28},{8,0},{12,4},{16,8},{20,12},{24,16},{28,20},{1,25},{... | collective-permute-start | bytes 245768 | tf_op jit(solution)/shard_map/ppermute | solution.py:586
  12.6 0.0 copy-done
  12.6 0.0 copy-done.5
  12.6 0.0 copy-done.6
  12.6 0.0 copy-done.7
  12.6 0.0 copy-done.8
  12.6 0.0 copy-done.9
  12.6 0.0 copy-done.10
  12.6 0.0 copy-done.11
  12.7 0.0 copy-start.2
  12.7 2.4 %inner.2 = (f32[2,128,512]{2,1,0:T(8,128)S(1)}, f32[128,512]{1,0:T(8,128)S(1)}, f32[4,128,128]{2,1,0:T(8,128)S(1)}, f32[2,4,8,128]{3,2,1,0:T(8,128)S(1)}, f32[2,4,8,128]{3,2,1,0:T(8,128)S(1)}) custom-call(f32[5,128,512]{2,1,0:T(8,128)S(1)} %bitcast.9, f32[3,128,512]{2,1,0:T(8,128)S(1)} %bitcast.11, f32[3,128,512]{2,1,0:T(8,128)S(1)} %bitcast.13, ...), custom_call_target="tpu_custom_call" | custom-call | flops 1600000000 | bytes 5000000 | tf_op jit(solution)/shard_map/inner/pallas_call | solution.py:426
  15.0 0.0 collective-permute-done.a
  15.0 0.0 collective-permute-done.1.b
  15.1 0.0 collective-permute-done.2.c.c2
  15.1 1.7 %collective-permute-done.3.d = bf16[320,128]{1,0:T(8,128)(2,1)S(1)} collective-permute-done((bf16[320,128]{1,0:T(8,128)(2,1)S(1)}, bf16[320,128]{1,0:T(8,128)(2,1)S(1)}, u32[]{:S(2)}, u32[]{:S(2)}) %collective-permute-start.3) | collective-permute-done | bytes 81952 | tf_op jit(solution)/shard_map/ppermute | solution.py:586
  16.7 0.0 copy-done.2
  16.7 0.1 lines.1
  16.9 0.0 copy-start.3
  16.9 0.0 copy-start.4
  16.9 0.8 %collective-permute-start.4 = (f32[8,128]{1,0:T(8,128)S(1)}, f32[8,128]{1,0:T(8,128)S(1)}, u32[]{:S(2)}, u32[]{:S(2)}) collective-permute-start(f32[8,128]{1,0:T(8,128)S(1)} %get-tuple-element.41), channel_id=1, source_target_pairs={{1,2},{2,1},{3,4},{4,3},{5,6},{6,5},{7,8},{8,7},{9,10},{10,9},{11,... | collective-permute-start | bytes 12296 | tf_op jit(solution)/shard_map/ppermute | solution.py:595
  17.7 2.9 %collective-permute-start.5 = (f32[8,128]{1,0:T(8,128)S(1)}, f32[8,128]{1,0:T(8,128)S(1)}, u32[]{:S(2)}, u32[]{:S(2)}) collective-permute-start(f32[8,128]{1,0:T(8,128)S(1)} %get-tuple-element.42), channel_id=1, source_target_pairs={{0,1},{1,0},{2,3},{3,2},{4,5},{5,4},{6,7},{7,6},{8,9},{9,8},{10,11... | collective-permute-start | bytes 12296 | tf_op jit(solution)/shard_map/ppermute | solution.py:596
  20.6 2.4 %inner.3.base_b = f32[3,128,512]{2,1,0:T(8,128)S(1)} custom-call(f32[5,128,512]{2,1,0:T(8,128)S(1)} %bitcast.10, f32[3,128,512]{2,1,0:T(8,128)S(1)} %bitcast.12, f32[3,128,512]{2,1,0:T(8,128)S(1)} %bitcast.14, f32[128,128]{1,0:T(8,128)S(1)} %get-tuple-element.44.refs_3_, bf16[256,256]{1,0:T(8,128)(2,1)S(1)} %copy-done.6, bf16[128,256]{1,0:T(8,128)(2,1)S(1)} %copy-done.8, ...), custom_call_target="tpu_custom_call" | custom-call | flops 2400000000 | bytes 5000000 | tf_op jit(solution)/shard_map/inner/pallas_call | solution.py:426
  23.0 0.0 collective-permute-done.4.across
  23.1 0.0 collective-permute-done.5.inside
  23.1 0.0 copy-done.3
  23.1 0.0 copy-done.4
  23.1 1.9 %outer.1 = f32[5,128,512]{2,1,0:T(8,128)} custom-call(bf16[320,128]{1,0:T(8,128)(2,1)S(1)} %collective-permute-done.a, bf16[320,128]{1,0:T(8,128)(2,1)S(1)} %collective-permute-done.1.b, f32[320,128]{1,0:T(8,128)S(1)} %get-tuple-element.36.own, bf16[320,128]{1,0:T(8,128)(2,1)S(1)} %collective-permute-done.2.c.c2, ...), custom_call_target="tpu_custom_call" | custom-call | tf_op jit(solution)/shard_map/outer/pallas_call | solution.py:559
Async XLA Ops:
  3.2 0.9 %copy-start.1 = (f32[160,384]{1,0:T(8,128)S(1)}, f32[160,384]{1,0:T(8,128)}, u32[]{:S(2)}) copy-start(f32[160,384]{1,0:T(8,128)} %fold.1.both) | copy-start | bytes 737284
  4.1 8.5 %copy-start = (f32[128,5,512]{2,0,1:T(8,128)S(1)}, f32[128,5,512]{2,0,1:T(8,128)}, u32[]{:S(2)}) copy-start(f32[128,5,512]{2,0,1:T(8,128)} %param.15) | copy-start | bytes 3932164
  4.1 8.5 %copy-start.5 = (bf16[256,256]{1,0:T(8,128)(2,1)S(1)}, bf16[256,256]{1,0:T(8,128)(2,1)}, u32[]{:S(2)}) copy-start(bf16[256,256]{1,0:T(8,128)(2,1)} %constant.19.clone.refs_6_.wb1) | copy-start | bytes 393220
  4.1 8.5 %copy-start.6 = (bf16[256,256]{1,0:T(8,128)(2,1)S(1)}, bf16[256,256]{1,0:T(8,128)(2,1)}, u32[]{:S(2)}) copy-start(bf16[256,256]{1,0:T(8,128)(2,1)} %constant.17.clone.refs_4_.wf1) | copy-start | bytes 393220
  4.1 8.5 %copy-start.7 = (bf16[256,128]{1,0:T(8,128)(2,1)S(1)}, bf16[256,128]{1,0:T(8,128)(2,1)}, u32[]{:S(2)}) copy-start(bf16[256,128]{1,0:T(8,128)(2,1)} %constant.20.clone.refs_7_.wb2) | copy-start | bytes 196612
  4.1 8.5 %copy-start.8 = (bf16[128,256]{1,0:T(8,128)(2,1)S(1)}, bf16[128,256]{1,0:T(8,128)(2,1)}, u32[]{:S(2)}) copy-start(bf16[128,256]{1,0:T(8,128)(2,1)} %constant.18.clone.refs_5_.wf2) | copy-start | bytes 196612
  4.2 8.5 %copy-start.9 = (f32[128,3,512]{2,0,1:T(8,128)S(1)}, f32[128,3,512]{2,0,1:T(8,128)}, u32[]{:S(2)}) copy-start(f32[128,3,512]{2,0,1:T(8,128)} %param.16) | copy-start | bytes 2359300
  4.2 8.5 %copy-start.10 = (f32[128,3,512]{2,0,1:T(8,128)S(1)}, f32[128,3,512]{2,0,1:T(8,128)}, u32[]{:S(2)}) copy-start(f32[128,3,512]{2,0,1:T(8,128)} %param.17) | copy-start | bytes 2359300
  4.2 8.5 %copy-start.11 = (f32[48,128]{1,0:T(8,128)S(1)}, f32[48,128]{1,0:T(8,128)}, u32[]{:S(2)}) copy-start(f32[48,128]{1,0:T(8,128)} %constant.21.clone.refs_8_) | copy-start | bytes 73732
  4.5 10.6 %collective-permute-start = (bf16[320,128]{1,0:T(8,128)(2,1)S(1)}, bf16[320,128]{1,0:T(8,128)(2,1)S(1)}, u32[]{:S(2)}, u32[]{:S(2)}) collective-permute-start(bf16[320,128]{1,0:T(8,128)(2,1)S(1)} %get-tuple-element.27), channel_id=1, source_target_pairs={{0,4},{4,8},{8,12},{12,16},{16,20},{20,24},{24,28},{28,0},{1,5},{5... | collective-permute-start | bytes 245768 | tf_op jit(solution)/shard_map/ppermute | solution.py:586
  7.5 7.6 %collective-permute-start.1 = (bf16[320,128]{1,0:T(8,128)(2,1)S(1)}, bf16[320,128]{1,0:T(8,128)(2,1)S(1)}, u32[]{:S(2)}, u32[]{:S(2)}) collective-permute-start(bf16[320,128]{1,0:T(8,128)(2,1)S(1)} %get-tuple-element.28), channel_id=1, source_target_pairs={{0,8},{4,12},{8,16},{12,20},{16,24},{20,28},{24,0},{28,4},{1,9},{5... | collective-permute-start | bytes 245768 | tf_op jit(solution)/shard_map/ppermute | solution.py:586
  9.1 6.0 %collective-permute-start.2 = (bf16[320,128]{1,0:T(8,128)(2,1)S(1)}, bf16[320,128]{1,0:T(8,128)(2,1)S(1)}, u32[]{:S(2)}, u32[]{:S(2)}) collective-permute-start(bf16[320,128]{1,0:T(8,128)(2,1)S(1)} %get-tuple-element.30), channel_id=1, source_target_pairs={{0,28},{4,0},{8,4},{12,8},{16,12},{20,16},{24,20},{28,24},{1,29},{... | collective-permute-start | bytes 245768 | tf_op jit(solution)/shard_map/ppermute | solution.py:586
  12.3 4.5 %collective-permute-start.3 = (bf16[320,128]{1,0:T(8,128)(2,1)S(1)}, bf16[320,128]{1,0:T(8,128)(2,1)S(1)}, u32[]{:S(2)}, u32[]{:S(2)}) collective-permute-start(bf16[320,128]{1,0:T(8,128)(2,1)S(1)} %get-tuple-element.31), channel_id=1, source_target_pairs={{0,24},{4,28},{8,0},{12,4},{16,8},{20,12},{24,16},{28,20},{1,25},{... | collective-permute-start | bytes 245768 | tf_op jit(solution)/shard_map/ppermute | solution.py:586
  12.7 4.1 %copy-start.2 = (f32[160,384]{1,0:T(8,128)S(1)}, f32[160,384]{1,0:T(8,128)}, u32[]{:S(2)}) copy-start(f32[160,384]{1,0:T(8,128)} %fold.1.both) | copy-start | bytes 737284
  16.9 6.2 %copy-start.3 = (bf16[256,1024]{1,0:T(8,128)(2,1)S(1)}, bf16[256,1024]{1,0:T(8,128)(2,1)}, u32[]{:S(2)}) copy-start(bf16[256,1024]{1,0:T(8,128)(2,1)} %constant.23.clone.place) | copy-start | bytes 1572868
  16.9 6.2 %copy-start.4 = (bf16[256,1024]{1,0:T(8,128)(2,1)S(1)}, bf16[256,1024]{1,0:T(8,128)(2,1)}, u32[]{:S(2)}) copy-start(bf16[256,1024]{1,0:T(8,128)(2,1)} %constant.22.clone.spread) | copy-start | bytes 1572868
  16.9 6.1 %collective-permute-start.4 = (f32[8,128]{1,0:T(8,128)S(1)}, f32[8,128]{1,0:T(8,128)S(1)}, u32[]{:S(2)}, u32[]{:S(2)}) collective-permute-start(f32[8,128]{1,0:T(8,128)S(1)} %get-tuple-element.41), channel_id=1, source_target_pairs={{1,2},{2,1},{3,4},{4,3},{5,6},{6,5},{7,8},{8,7},{9,10},{10,9},{11,... | collective-permute-start | bytes 12296 | tf_op jit(solution)/shard_map/ppermute | solution.py:595
  17.7 5.4 %collective-permute-start.5 = (f32[8,128]{1,0:T(8,128)S(1)}, f32[8,128]{1,0:T(8,128)S(1)}, u32[]{:S(2)}, u32[]{:S(2)}) collective-permute-start(f32[8,128]{1,0:T(8,128)S(1)} %get-tuple-element.42), channel_id=1, source_target_pairs={{0,1},{1,0},{2,3},{3,2},{4,5},{5,4},{6,7},{7,6},{8,9},{9,8},{10,11... | collective-permute-start | bytes 12296 | tf_op jit(solution)/shard_map/ppermute | solution.py:596

commit v5 on v2

--- a/solution.py
+++ b/solution.py
@@ -25,6 +25,7 @@
 HBM = pl.BlockSpec(memory_space=pltpu.HBM)
 VM = pl.BlockSpec(memory_space=pltpu.VMEM)
 LIMIT = 32 * 1024 * 1024
+ORDER = (3, 4, 2, 1, 0)
 WHOLE = 64 * 1024 * 1024
 
 
@@ -205,7 +206,7 @@
         + [(fold_hbm, fold)],
         sems,
     )
-    for copy in copies[:4]:
+    for copy in copies:
         copy.wait()
     route, target, code, hang = (ints[n] for n in range(4))
     lane = iota(1)
@@ -216,7 +217,6 @@
     odd = lane % 16 >= 8
     group = (lane // 16 + 1) % 4
     for f in range(5):
-        copies[4 + f].wait()
         packed = jnp.zeros((E, 128), F32)
         for c in range(4):
             moved = x[f, :, 128 * c : 128 * c + 128]
@@ -228,7 +228,6 @@
         both = jnp.where(odd, high_f, pltpu.roll(packed - high_f, 8, 1)).astype(BF16)
         wide[E * f : E * f + E, 0:128] = both
         wide[E * f : E * f + E, 128:256] = high
-    copies[9].wait()
     mapped = dot(wide[...], fold[...])
     faces = []
     for f in range(5):
@@ -241,8 +240,7 @@
     f01 = jnp.where(left, faces[0], faces[1]).astype(BF16)
     f23 = jnp.where(left, faces[2], faces[3]).astype(BF16)
     sums = dot(hit, jnp.concatenate([f01, f23, faces[4].astype(BF16)], 1))
-    for o in range(5):
-        ref = outs[o]
+    for ref, o in zip(outs, ORDER):
         mine = sums[o * E : o * E + E]
         last = jnp.where(left[:64], mine[:64, 256:384], mine[64:, 256:384])
         ref[0:128] = mine[:, 0:128].astype(ref.dtype)
@@ -408,7 +406,7 @@
         out_specs=VM,
         compiler_params=pltpu.CompilerParams(vmem_limit_bytes=16 * 1024 * 1024),
         cost_estimate=pl.CostEstimate(
-            flops=1_200_000_000, bytes_accessed=1_000_000, transcendentals=0
+            flops=8_000_000_000, bytes_accessed=30_000_000, transcendentals=0
         ),
         name="keep",
     )(marks)
@@ -443,7 +441,7 @@
     return lax.rem(index, 2) == 1
 
 
-def line_kernel(a, b, own, c, d, edges, across, inside):
+def line_kernel(a, b, own, c, d, edges, inside, across):
     def rows(start):
         return sum(ref[start : start + 16].astype(F32) for ref in (a, b, own, c, d))
 
@@ -574,20 +572,20 @@
         x.reshape(1, E) for x in (mortar_route, mortar_element, face_code, hanging)
     )
     *parts, edges, marks = folded_of(route, target, code, hang, adjoint, tables["fold"])
-    for o in (0, 4, 1, 3):
-        pairs = [(i, (i + o - 2) % peers) for i in range(peers)]
-        parts[o] = lax.ppermute(parts[o], "dom", pairs)
+    for n in (0, 1, 3, 4):
+        pairs = [(i, (i + ORDER[n] - 2) % peers) for i in range(peers)]
+        parts[n] = lax.ppermute(parts[n], "dom", pairs)
     kept = kept_of(marks)
     early, *factors = main_of(adjoint, met, vel, kept, tables, (0, 1), True)
     parts, early = lax.optimization_barrier((parts, early))
     lines = lines_of(parts, edges)
-    (out_a, out_b), kept = lax.optimization_barrier((lines, kept))
+    (out_b, out_a), kept = lax.optimization_barrier((lines, kept))
     axes = ("dom", "sub")
     count = lax.axis_size(axes)
     inside = [(i, i ^ 1) for i in range(count)]
     across = [(i, i + 1 if i % 2 else i - 1) for i in range(1, count - 1)]
+    inward = lax.ppermute(out_b, axes, inside)
     outward = lax.ppermute(out_a, axes, across)
-    inward = lax.ppermute(out_b, axes, inside)
     (late,) = main_of(adjoint, met, vel, kept, tables, (2, 3, 4), False)
     result = post_of(parts, outward, inward, (early, late, *factors), tables)
     return jnp.transpose(result, (1, 0, 2))

time: 26.2 us -> 25 us (0.954)
  waiting for transfers between devices: 1.3 us -> 0.02 us
    ppermute x4, waiting for transfers between devices: 1.29 us -> 0.01 us  [shards(): parts[n] = lax.ppermute(parts[n], 'dom', pairs)]
  transfers between devices with their start and end apart: 6 -> 6, of which waited for: 1 -> 0; matrix products, arithmetic and copies ran while one was open for 0% -> 0% of each run, Pallas kernels for 19% -> 20%
where the time goes in v5:
time: 25 us; the launch traced here: 24.8 us
  starting transfers between devices  12 us (48%)
  Pallas kernels  10.2 us (41%)
  local copies, waits for them, and re-layouts  2.41 us (10%)
    ppermute x4, starting transfers between devices, shards(): parts[n] = lax.ppermute(parts[n], 'dom', pairs)  8.12 us
    pallas_call x2, Pallas kernels, main_of(): pl.pallas_call(body, out_shape=[jax.ShapeDtypeStruct(shape, F32) for shap...  4.76 us
    pallas_call x1, Pallas kernels, folded_of(): pl.pallas_call(fold_kernel, out_shape=[jax.ShapeDtypeStruct((320, 128), F...  3.25 us
    ppermute x1, starting transfers between devices, shards(): inward = lax.ppermute(out_b, axes, inside)  3.08 us
    unnamed x26, local copies, waits for them, and re-layouts  2.41 us
    pallas_call x1, Pallas kernels, post_of(): pl.pallas_call(post_kernel, out_shape=jax.ShapeDtypeStruct((5, E, 512), F...  1.92 us
    ppermute x1, starting transfers between devices, shards(): outward = lax.ppermute(out_a, axes, across)  0.78 us
  transfers between devices with their start and end apart: 6, of which 0 were waited for; matrix products, arithmetic and copies ran while one was open for 0% of the time, Pallas kernels for 20%

profile of v5, /device:TPU:0, one launch (start us, length us, event | category | flops | bytes accessed | tf_op | source)
XLA Modules:
  0.0 24.8 jit_solution(428239134568768266)
XLA Ops:
  0.0 3.2 %fold.1 = (bf16[320,128]{1,0:T(8,128)(2,1)}, bf16[320,128]{1,0:T(8,128)(2,1)}, f32[320,128]{1,0:T(8,128)}, bf16[320,128]{1,0:T(8,128)(2,1)}, bf16[320,128]{1,0:T...) custom-call(s32[1,128]{1,0:T(1,128)} %bitcast.15, s32[1,128]{1,0:T(1,128)} %bitcast.16, s32[1,128]{1,0:T(1,128)} %bitcast.17, ...), custom_call_target="tpu_custom_call" | custom-call | tf_op jit(solution)/shard_map/fold/pallas_call | solution.py:269
  3.3 3.0 %collective-permute-start = (bf16[320,128]{1,0:T(8,128)(2,1)}, bf16[320,128]{1,0:T(8,128)(2,1)S(1)}, u32[]{:S(2)}, u32[]{:S(2)}) collective-permute-start(bf16[320,128]{1,0:T(8,128)(2,1)} %get-tuple-element.28), channel_id=1, source_target_pairs={{0,4},{4,8},{8,12},{12,16},{16,20},{20,24},{24,28},{28,0},{1,5},{5... | collective-permute-start | bytes 245768 | tf_op jit(solution)/shard_map/ppermute | solution.py:577
  6.2 1.6 %collective-permute-start.1 = (bf16[320,128]{1,0:T(8,128)(2,1)}, bf16[320,128]{1,0:T(8,128)(2,1)S(1)}, u32[]{:S(2)}, u32[]{:S(2)}) collective-permute-start(bf16[320,128]{1,0:T(8,128)(2,1)} %get-tuple-element.29), channel_id=1, source_target_pairs={{0,8},{4,12},{8,16},{12,20},{16,24},{20,28},{24,0},{28,4},{1,9},{5... | collective-permute-start | bytes 245768 | tf_op jit(solution)/shard_map/ppermute | solution.py:577
  7.8 3.2 %collective-permute-start.2 = (bf16[320,128]{1,0:T(8,128)(2,1)}, bf16[320,128]{1,0:T(8,128)(2,1)S(1)}, u32[]{:S(2)}, u32[]{:S(2)}) collective-permute-start(bf16[320,128]{1,0:T(8,128)(2,1)} %get-tuple-element.31), channel_id=1, source_target_pairs={{0,28},{4,0},{8,4},{12,8},{16,12},{20,16},{24,20},{28,24},{1,29},{... | collective-permute-start | bytes 245768 | tf_op jit(solution)/shard_map/ppermute | solution.py:577
  11.1 0.3 %collective-permute-start.3 = (bf16[320,128]{1,0:T(8,128)(2,1)}, bf16[320,128]{1,0:T(8,128)(2,1)S(1)}, u32[]{:S(2)}, u32[]{:S(2)}) collective-permute-start(bf16[320,128]{1,0:T(8,128)(2,1)} %get-tuple-element.32), channel_id=1, source_target_pairs={{0,24},{4,28},{8,0},{12,4},{16,8},{20,12},{24,16},{28,20},{1,25},{... | collective-permute-start | bytes 245768 | tf_op jit(solution)/shard_map/ppermute | solution.py:577
  11.4 0.0 copy-start.11
  11.4 0.7 %copy-done.11 = f32[8,128]{1,0:T(8,128)S(1)} copy-done((f32[8,128]{1,0:T(8,128)S(1)}, f32[8,128]{1,0:T(8,128)}, u32[]{:S(2)}) %copy-start.11) | copy-done | bytes 4120
  12.1 0.0 copy-start
  12.1 0.0 copy-start.4
  12.1 0.0 copy-start.5
  12.1 0.0 copy-start.6
  12.1 0.0 copy-start.7
  12.1 0.0 copy-start.9
  12.1 0.0 copy-start.10
  12.1 0.0 copy-start.12
  12.1 0.1 keep.1.refs_3_
  12.3 1.1 %copy-done = f32[128,5,512]{2,0,1:T(8,128)S(1)} copy-done((f32[128,5,512]{2,0,1:T(8,128)S(1)}, f32[128,5,512]{2,0,1:T(8,128)}, u32[]{:S(2)}) %copy-start) | copy-done | bytes 1310744
  13.4 0.0 copy-done.4
  13.4 0.0 copy-done.5
  13.4 0.0 copy-done.6
  13.4 0.0 copy-done.7
  13.4 0.3 %copy-done.9 = f32[128,3,512]{2,0,1:T(8,128)S(1)} copy-done((f32[128,3,512]{2,0,1:T(8,128)S(1)}, f32[128,3,512]{2,0,1:T(8,128)}, u32[]{:S(2)}) %copy-start.9) | copy-done | bytes 786456
  13.7 0.2 copy-done.10
  13.9 0.0 copy-done.12
  14.0 0.0 copy-start.1
  14.0 0.0 copy-start.8
  14.0 2.4 %inner.2 = (f32[2,128,512]{2,1,0:T(8,128)S(1)}, f32[128,512]{1,0:T(8,128)S(1)}, f32[4,128,128]{2,1,0:T(8,128)S(1)}, f32[2,4,8,128]{3,2,1,0:T(8,128)S(1)}, f32[2,4,8,128]{3,2,1,0:T(8,128)S(1)}) custom-call(f32[5,128,512]{2,1,0:T(8,128)S(1)} %bitcast.9, f32[3,128,512]{2,1,0:T(8,128)S(1)} %bitcast.11, f32[3,128,512]{2,1,0:T(8,128)S(1)} %bitcast.13, ...), custom_call_target="tpu_custom_call" | custom-call | flops 1600000000 | bytes 5000000 | tf_op jit(solution)/shard_map/inner/pallas_call | solution.py:419
  16.3 0.0 collective-permute-done.a
  16.3 0.0 collective-permute-done.1.b
  16.3 0.0 collective-permute-done.2.c.c2
  16.4 0.0 collective-permute-done.3.d
  16.4 0.0 copy-done.1
  16.4 0.0 copy-done.8
  16.4 0.1 lines.1
  16.5 0.0 copy-start.2
  16.5 0.0 copy-start.3
  16.5 0.8 %collective-permute-start.4 = (f32[8,128]{1,0:T(8,128)S(1)}, f32[8,128]{1,0:T(8,128)S(1)}, u32[]{:S(2)}, u32[]{:S(2)}) collective-permute-start(f32[8,128]{1,0:T(8,128)S(1)} %get-tuple-element.43), channel_id=1, source_target_pairs={{1,2},{2,1},{3,4},{4,3},{5,6},{6,5},{7,8},{8,7},{9,10},{10,9},{11,... | collective-permute-start | bytes 12296 | tf_op jit(solution)/shard_map/ppermute | solution.py:588
  17.3 3.1 %collective-permute-start.5 = (f32[8,128]{1,0:T(8,128)S(1)}, f32[8,128]{1,0:T(8,128)S(1)}, u32[]{:S(2)}, u32[]{:S(2)}) collective-permute-start(f32[8,128]{1,0:T(8,128)S(1)} %get-tuple-element.44), channel_id=1, source_target_pairs={{0,1},{1,0},{2,3},{3,2},{4,5},{5,4},{6,7},{7,6},{8,9},{9,8},{10,11... | collective-permute-start | bytes 12296 | tf_op jit(solution)/shard_map/ppermute | solution.py:587
  20.4 2.4 %inner.3.base_b = f32[3,128,512]{2,1,0:T(8,128)S(1)} custom-call(f32[5,128,512]{2,1,0:T(8,128)S(1)} %bitcast.10, f32[3,128,512]{2,1,0:T(8,128)S(1)} %bitcast.12, f32[3,128,512]{2,1,0:T(8,128)S(1)} %bitcast.14, f32[128,128]{1,0:T(8,128)S(1)} %keep.1.refs_3_, bf16[256,256]{1,0:T(8,128)(2,1)S(1)} %copy-done.5, bf16[128,256]{1,0:T(8,128)(2,1)S(1)} %copy-done.7, ...), custom_call_target="tpu_custom_call" | custom-call | flops 2400000000 | bytes 5000000 | tf_op jit(solution)/shard_map/inner/pallas_call | solution.py:419
  22.8 0.0 collective-permute-done.4.across
  22.8 0.0 collective-permute-done.5.inside
  22.8 0.0 copy-done.2
  22.8 0.0 copy-done.3
  22.8 1.9 %outer.1 = f32[5,128,512]{2,1,0:T(8,128)} custom-call(bf16[320,128]{1,0:T(8,128)(2,1)S(1)} %collective-permute-done.a, bf16[320,128]{1,0:T(8,128)(2,1)S(1)} %collective-permute-done.1.b, f32[320,128]{1,0:T(8,128)S(1)} %copy-done.1, bf16[320,128]{1,0:T(8,128)(2,1)S(1)} %collective-permute-done.2.c.c2, bf16[320,128]{1,0:T(8,128)(2,1)S(1)} %collective-permute-done.3.d, ...), custom_call_target="tpu_custom_call" | custom-call | tf_op jit(solution)/shard_map/outer/pallas_call | solution.py:551
Async XLA Ops:
  3.3 13.1 %collective-permute-start = (bf16[320,128]{1,0:T(8,128)(2,1)}, bf16[320,128]{1,0:T(8,128)(2,1)S(1)}, u32[]{:S(2)}, u32[]{:S(2)}) collective-permute-start(bf16[320,128]{1,0:T(8,128)(2,1)} %get-tuple-element.28), channel_id=1, source_target_pairs={{0,4},{4,8},{8,12},{12,16},{16,20},{20,24},{24,28},{28,0},{1,5},{5... | collective-permute-start | bytes 245768 | tf_op jit(solution)/shard_map/ppermute | solution.py:577
  6.2 10.1 %collective-permute-start.1 = (bf16[320,128]{1,0:T(8,128)(2,1)}, bf16[320,128]{1,0:T(8,128)(2,1)S(1)}, u32[]{:S(2)}, u32[]{:S(2)}) collective-permute-start(bf16[320,128]{1,0:T(8,128)(2,1)} %get-tuple-element.29), channel_id=1, source_target_pairs={{0,8},{4,12},{8,16},{12,20},{16,24},{20,28},{24,0},{28,4},{1,9},{5... | collective-permute-start | bytes 245768 | tf_op jit(solution)/shard_map/ppermute | solution.py:577
  7.8 8.5 %collective-permute-start.2 = (bf16[320,128]{1,0:T(8,128)(2,1)}, bf16[320,128]{1,0:T(8,128)(2,1)S(1)}, u32[]{:S(2)}, u32[]{:S(2)}) collective-permute-start(bf16[320,128]{1,0:T(8,128)(2,1)} %get-tuple-element.31), channel_id=1, source_target_pairs={{0,28},{4,0},{8,4},{12,8},{16,12},{20,16},{24,20},{28,24},{1,29},{... | collective-permute-start | bytes 245768 | tf_op jit(solution)/shard_map/ppermute | solution.py:577
  11.1 5.3 %collective-permute-start.3 = (bf16[320,128]{1,0:T(8,128)(2,1)}, bf16[320,128]{1,0:T(8,128)(2,1)S(1)}, u32[]{:S(2)}, u32[]{:S(2)}) collective-permute-start(bf16[320,128]{1,0:T(8,128)(2,1)} %get-tuple-element.32), channel_id=1, source_target_pairs={{0,24},{4,28},{8,0},{12,4},{16,8},{20,12},{24,16},{28,20},{1,25},{... | collective-permute-start | bytes 245768 | tf_op jit(solution)/shard_map/ppermute | solution.py:577
  11.4 0.7 %copy-start.11 = (f32[8,128]{1,0:T(8,128)S(1)}, f32[8,128]{1,0:T(8,128)}, u32[]{:S(2)}) copy-start(f32[8,128]{1,0:T(8,128)} %get-tuple-element.33.marks) | copy-start | bytes 12292
  12.1 1.3 %copy-start = (f32[128,5,512]{2,0,1:T(8,128)S(1)}, f32[128,5,512]{2,0,1:T(8,128)}, u32[]{:S(2)}) copy-start(f32[128,5,512]{2,0,1:T(8,128)} %param.15) | copy-start | bytes 3932164
  12.1 1.3 %copy-start.4 = (bf16[256,256]{1,0:T(8,128)(2,1)S(1)}, bf16[256,256]{1,0:T(8,128)(2,1)}, u32[]{:S(2)}) copy-start(bf16[256,256]{1,0:T(8,128)(2,1)} %constant.19.clone.refs_6_.wb1) | copy-start | bytes 393220
  12.1 1.3 %copy-start.5 = (bf16[256,256]{1,0:T(8,128)(2,1)S(1)}, bf16[256,256]{1,0:T(8,128)(2,1)}, u32[]{:S(2)}) copy-start(bf16[256,256]{1,0:T(8,128)(2,1)} %constant.17.clone.refs_4_.wf1) | copy-start | bytes 393220
  12.1 1.3 %copy-start.6 = (bf16[256,128]{1,0:T(8,128)(2,1)S(1)}, bf16[256,128]{1,0:T(8,128)(2,1)}, u32[]{:S(2)}) copy-start(bf16[256,128]{1,0:T(8,128)(2,1)} %constant.20.clone.refs_7_.wb2) | copy-start | bytes 196612
  12.1 1.3 %copy-start.7 = (bf16[128,256]{1,0:T(8,128)(2,1)S(1)}, bf16[128,256]{1,0:T(8,128)(2,1)}, u32[]{:S(2)}) copy-start(bf16[128,256]{1,0:T(8,128)(2,1)} %constant.18.clone.refs_5_.wf2) | copy-start | bytes 196612
  12.1 1.6 %copy-start.9 = (f32[128,3,512]{2,0,1:T(8,128)S(1)}, f32[128,3,512]{2,0,1:T(8,128)}, u32[]{:S(2)}) copy-start(f32[128,3,512]{2,0,1:T(8,128)} %param.16) | copy-start | bytes 2359300
  12.1 1.8 %copy-start.10 = (f32[128,3,512]{2,0,1:T(8,128)S(1)}, f32[128,3,512]{2,0,1:T(8,128)}, u32[]{:S(2)}) copy-start(f32[128,3,512]{2,0,1:T(8,128)} %param.17) | copy-start | bytes 2359300
  12.1 1.8 %copy-start.12 = (f32[48,128]{1,0:T(8,128)S(1)}, f32[48,128]{1,0:T(8,128)}, u32[]{:S(2)}) copy-start(f32[48,128]{1,0:T(8,128)} %constant.21.clone.refs_8_) | copy-start | bytes 73732
  14.0 2.4 %copy-start.1 = (f32[320,128]{1,0:T(8,128)S(1)}, f32[320,128]{1,0:T(8,128)}, u32[]{:S(2)}) copy-start(f32[320,128]{1,0:T(8,128)} %get-tuple-element.37.own) | copy-start | bytes 491524
  14.0 2.4 %copy-start.8 = (f32[16,128]{1,0:T(8,128)S(1)}, f32[16,128]{1,0:T(8,128)}, u32[]{:S(2)}) copy-start(f32[16,128]{1,0:T(8,128)} %get-tuple-element.40.edges) | copy-start | bytes 24580
  16.5 6.3 %copy-start.2 = (bf16[256,1024]{1,0:T(8,128)(2,1)S(1)}, bf16[256,1024]{1,0:T(8,128)(2,1)}, u32[]{:S(2)}) copy-start(bf16[256,1024]{1,0:T(8,128)(2,1)} %constant.23.clone.place) | copy-start | bytes 1572868
  16.5 6.3 %copy-start.3 = (bf16[256,1024]{1,0:T(8,128)(2,1)S(1)}, bf16[256,1024]{1,0:T(8,128)(2,1)}, u32[]{:S(2)}) copy-start(bf16[256,1024]{1,0:T(8,128)(2,1)} %constant.22.clone.spread) | copy-start | bytes 1572868
  16.5 6.3 %collective-permute-start.4 = (f32[8,128]{1,0:T(8,128)S(1)}, f32[8,128]{1,0:T(8,128)S(1)}, u32[]{:S(2)}, u32[]{:S(2)}) collective-permute-start(f32[8,128]{1,0:T(8,128)S(1)} %get-tuple-element.43), channel_id=1, source_target_pairs={{1,2},{2,1},{3,4},{4,3},{5,6},{6,5},{7,8},{8,7},{9,10},{10,9},{11,... | collective-permute-start | bytes 12296 | tf_op jit(solution)/shard_map/ppermute | solution.py:588
  17.3 5.5 %collective-permute-start.5 = (f32[8,128]{1,0:T(8,128)S(1)}, f32[8,128]{1,0:T(8,128)S(1)}, u32[]{:S(2)}, u32[]{:S(2)}) collective-permute-start(f32[8,128]{1,0:T(8,128)S(1)} %get-tuple-element.44), channel_id=1, source_target_pairs={{0,1},{1,0},{2,3},{3,2},{4,5},{5,4},{6,7},{7,6},{8,9},{9,8},{10,11... | collective-permute-start | bytes 12296 | tf_op jit(solution)/shard_map/ppermute | solution.py:587

commit v6 on v5

--- a/solution.py
+++ b/solution.py
@@ -360,36 +360,61 @@
             end_mv[end, n] = ref[d, rows, at]
 
 
-def main_kernel(fields, x_ref, met, vel, keep_ref, wf1, wf2, wb1, wb2, coef, out, *factors):
+def main_kernel(fields, x_ref, met, vel, keep_ref, wf, wb1, wb2, coef, out, *refs):
+    factors, (wide_x, xs, wide_in) = refs[:-3], refs[-3:]
     lane, row = iota(1), iota(0)
     keep = keep_ref[...]
     left = lane < 64
     if factors:
         factors_of(met, vel, wb1, wb2, coef, *factors)
 
-    def field(n, carry):
-        f = n + fields[0]
-        x = [x_ref[f, :, 128 * c : 128 * c + 128] * keep for c in range(4)]
-        low_faces = pltpu.roll(swap(x[0]), E - 1, 0)
-        high_faces = pltpu.roll(swap(x[3]), 1, 0)
-        x[0] = x[0] + jnp.where(left & (row > 0), high_faces, 0.0)
-        x[3] = x[3] + jnp.where(left | (row == E - 1), 0.0, low_faces)
-        stacked = jnp.concatenate(x, 0)
-        rest = two_dims(
-            stacked, chunks_of(met, 1), chunks_of(met, 2), chunks_of(vel, 1), chunks_of(vel, 2),
-            wf1, wf2, wb1, wb2,
-        )
-        g0 = along_first(x, coef, 0)
-        inner0 = []
+    tile = 32
+    for n, f in enumerate(fields):
+        low_faces = pltpu.roll(swap(x_ref[f, :, 0:128] * keep), E - 1, 0)
+        high_faces = pltpu.roll(swap(x_ref[f, :, 384:512] * keep), 1, 0)
+        low_faces = jnp.where(left | (row == E - 1), 0.0, low_faces)
+        high_faces = jnp.where(left & (row > 0), high_faces, 0.0)
+        for r in range(0, E, tile):
+            rows = slice(r, r + tile)
+            x = [x_ref[f, rows, 128 * c : 128 * c + 128] * keep[rows] for c in range(4)]
+            x[0] = x[0] + high_faces[rows]
+            x[3] = x[3] + low_faces[rows]
+            for c in range(4):
+                spot = slice(E * c + r, E * c + r + tile)
+                high, low = parts_of(x[c])
+                xs[n, spot] = x[c]
+                wide_x[n, spot, 0:128] = high
+                wide_x[n, spot, 128:256] = low
+                wide_x[n, spot, 256:384] = high
+            g0 = along_first(x, coef, 0)
+            inner0 = []
+            for c in range(4):
+                at = slice(128 * c, 128 * c + 128)
+                inner0.append(met[0, rows, at] * g0[c] + vel[0, rows, at] * x[c])
+            back = along_first(inner0, coef, 16)
+            for c in range(4):
+                out[n, rows, 128 * c : 128 * c + 128] = back[c]
+        g = dot(wide_x[n], wf[...])
         for c in range(4):
             at = slice(128 * c, 128 * c + 128)
-            inner0.append(met[0, :, at] * g0[c] + vel[0, :, at] * x[c])
-        back = along_first(inner0, coef, 16)
+            for r in range(0, E, tile):
+                rows = slice(r, r + tile)
+                spot = slice(E * c + r, E * c + r + tile)
+                x = xs[n, spot]
+                high1, low1 = parts_of(met[1, rows, at] * g[spot, 0:128] + vel[1, rows, at] * x)
+                high2, low2 = parts_of(met[2, rows, at] * g[spot, 128:256] + vel[2, rows, at] * x)
+                wide_in[n, spot, 0:128] = high1
+                wide_in[n, spot, 128:256] = high2
+                wide_in[n, spot, 256:384] = low1
+                wide_in[n, spot, 384:512] = low2
+        wide = dot(wide_in[n, :, 0:256], wb1[...])
+        low = dot(wide_in[n, :, 256:512], wb2[...])
         for c in range(4):
-            out[n, :, 128 * c : 128 * c + 128] = rest[E * c : E * c + E] + back[c]
-        return carry
-
-    lax.fori_loop(0, len(fields), field, 0)
+            at = slice(128 * c, 128 * c + 128)
+            for r in range(0, E, tile):
+                rows = slice(r, r + tile)
+                spot = slice(E * c + r, E * c + r + tile)
+                out[n, rows, at] += wide[spot, 0:128] + wide[spot, 128:256] + low[spot]
 
 
 def keep_kernel(marks, out):
@@ -423,8 +448,13 @@
             for shape in [(len(fields), E, 512)]
             + [(E, 512), (4, E, 128), (2, 4, 8, 128), (2, 4, 8, 128)] * factors
         ],
-        in_specs=[VM] * 9,
+        in_specs=[VM] * 8,
         out_specs=[VM] * (5 if factors else 1),
+        scratch_shapes=[
+            pltpu.VMEM((len(fields), 4 * E, 384), BF16),
+            pltpu.VMEM((len(fields), 4 * E, 128), F32),
+            pltpu.VMEM((len(fields), 4 * E, 512), BF16),
+        ],
         compiler_params=pltpu.CompilerParams(vmem_limit_bytes=LIMIT),
         cost_estimate=pl.CostEstimate(
             flops=800_000_000 * len(fields), bytes_accessed=5_000_000, transcendentals=0
@@ -432,7 +462,7 @@
         name="inner",
     )(
         adjoint, metric, velocity, keep,
-        *tables["forward"], *tables["backward"], tables["coef"],
+        np.concatenate(tables["forward"], 0), *tables["backward"], tables["coef"],
     )
 
 

time: 25 us -> 27.6 us (1.10)
  Pallas kernels: 10.2 us -> 12.9 us
    pallas_call x2, Pallas kernels: 4.76 us -> 7.42 us  [main_of(): pl.pallas_call(body, out_shape=[jax.ShapeDtypeStruct(shape, F32) for shap...]
    unnamed x26 -> x28, local copies, waits for them, and re-layouts: 2.41 us -> 2.39 us
  transfers between devices with their start and end apart: 6 -> 6, of which waited for: 0 -> 0; matrix products, arithmetic and copies ran while one was open for 0% -> 0% of each run, Pallas kernels for 20% -> 28%
where the time goes in v6:
time: 27.6 us; the launch traced here: 27.4 us
  Pallas kernels  12.9 us (47%)
  starting transfers between devices  12 us (43%)
  local copies, waits for them, and re-layouts  2.39 us (9%)
    ppermute x4, starting transfers between devices, shards(): parts[n] = lax.ppermute(parts[n], 'dom', pairs)  8.12 us
    pallas_call x2, Pallas kernels, main_of(): pl.pallas_call(body, out_shape=[jax.ShapeDtypeStruct(shape, F32) for shap...  7.42 us
    pallas_call x1, Pallas kernels, folded_of(): pl.pallas_call(fold_kernel, out_shape=[jax.ShapeDtypeStruct((320, 128), F...  3.25 us
    ppermute x1, starting transfers between devices, shards(): inward = lax.ppermute(out_b, axes, inside)  3.07 us
    unnamed x28, local copies, waits for them, and re-layouts  2.39 us
    pallas_call x1, Pallas kernels, post_of(): pl.pallas_call(post_kernel, out_shape=jax.ShapeDtypeStruct((5, E, 512), F...  1.93 us
    ppermute x1, starting transfers between devices, shards(): outward = lax.ppermute(out_a, axes, across)  0.79 us
  transfers between devices with their start and end apart: 6, of which 0 were waited for; matrix products, arithmetic and copies ran while one was open for 0% of the time, Pallas kernels for 28%

profile of v6, /device:TPU:0, one launch (start us, length us, event | category | flops | bytes accessed | tf_op | source)
XLA Modules:
  0.0 27.4 jit_solution(7710780724262367910)
XLA Ops:
  0.0 3.2 %fold.1 = (bf16[320,128]{1,0:T(8,128)(2,1)}, bf16[320,128]{1,0:T(8,128)(2,1)}, f32[320,128]{1,0:T(8,128)}, bf16[320,128]{1,0:T(8,128)(2,1)}, bf16[320,128]{1,0:T...) custom-call(s32[1,128]{1,0:T(1,128)} %bitcast.15, s32[1,128]{1,0:T(1,128)} %bitcast.16, s32[1,128]{1,0:T(1,128)} %bitcast.17, ...), custom_call_target="tpu_custom_call" | custom-call | tf_op jit(solution)/shard_map/fold/pallas_call | solution.py:269
  3.3 3.0 %collective-permute-start = (bf16[320,128]{1,0:T(8,128)(2,1)}, bf16[320,128]{1,0:T(8,128)(2,1)S(1)}, u32[]{:S(2)}, u32[]{:S(2)}) collective-permute-start(bf16[320,128]{1,0:T(8,128)(2,1)} %get-tuple-element.28), channel_id=1, source_target_pairs={{0,4},{4,8},{8,12},{12,16},{16,20},{20,24},{24,28},{28,0},{1,5},{5... | collective-permute-start | bytes 245768 | tf_op jit(solution)/shard_map/ppermute | solution.py:607
  6.2 1.6 %collective-permute-start.1 = (bf16[320,128]{1,0:T(8,128)(2,1)}, bf16[320,128]{1,0:T(8,128)(2,1)S(1)}, u32[]{:S(2)}, u32[]{:S(2)}) collective-permute-start(bf16[320,128]{1,0:T(8,128)(2,1)} %get-tuple-element.29), channel_id=1, source_target_pairs={{0,8},{4,12},{8,16},{12,20},{16,24},{20,28},{24,0},{28,4},{1,9},{5... | collective-permute-start | bytes 245768 | tf_op jit(solution)/shard_map/ppermute | solution.py:607
  7.8 3.2 %collective-permute-start.2 = (bf16[320,128]{1,0:T(8,128)(2,1)}, bf16[320,128]{1,0:T(8,128)(2,1)S(1)}, u32[]{:S(2)}, u32[]{:S(2)}) collective-permute-start(bf16[320,128]{1,0:T(8,128)(2,1)} %get-tuple-element.31), channel_id=1, source_target_pairs={{0,28},{4,0},{8,4},{12,8},{16,12},{20,16},{24,20},{28,24},{1,29},{... | collective-permute-start | bytes 245768 | tf_op jit(solution)/shard_map/ppermute | solution.py:607
  11.1 0.3 %collective-permute-start.3 = (bf16[320,128]{1,0:T(8,128)(2,1)}, bf16[320,128]{1,0:T(8,128)(2,1)S(1)}, u32[]{:S(2)}, u32[]{:S(2)}) collective-permute-start(bf16[320,128]{1,0:T(8,128)(2,1)} %get-tuple-element.32), channel_id=1, source_target_pairs={{0,24},{4,28},{8,0},{12,4},{16,8},{20,12},{24,16},{28,20},{1,25},{... | collective-permute-start | bytes 245768 | tf_op jit(solution)/shard_map/ppermute | solution.py:607
  11.4 0.0 copy-start.11
  11.4 0.7 %copy-done.11 = f32[8,128]{1,0:T(8,128)S(1)} copy-done((f32[8,128]{1,0:T(8,128)S(1)}, f32[8,128]{1,0:T(8,128)}, u32[]{:S(2)}) %copy-start.11) | copy-done | bytes 4120
  12.1 0.0 copy-start
  12.1 0.0 copy-start.4
  12.1 0.0 copy-start.6
  12.1 0.0 copy-start.9
  12.1 0.0 copy-start.10
  12.1 0.0 copy-start.12
  12.1 0.0 copy-start.13
  12.1 0.1 keep.1.refs_3_
  12.2 1.1 %copy-done = f32[128,5,512]{2,0,1:T(8,128)S(1)} copy-done((f32[128,5,512]{2,0,1:T(8,128)S(1)}, f32[128,5,512]{2,0,1:T(8,128)}, u32[]{:S(2)}) %copy-start) | copy-done | bytes 1310744
  13.4 0.0 copy-done.4
  13.4 0.0 copy-done.6
  13.4 0.3 copy-done.9
  13.6 0.2 copy-done.10
  13.9 0.0 copy-done.12
  13.9 0.0 copy-done.13
  13.9 0.0 copy-start.1
  13.9 0.0 copy-start.8
  13.9 3.8 %inner.2 = (f32[2,128,512]{2,1,0:T(8,128)S(1)}, f32[128,512]{1,0:T(8,128)S(1)}, f32[4,128,128]{2,1,0:T(8,128)S(1)}, f32[2,4,8,128]{3,2,1,0:T(8,128)S(1)}, f32[2,4,8,128]{3,2,1,0:T(8,128)S(1)}) custom-call(f32[5,128,512]{2,1,0:T(8,128)S(1)} %bitcast.9, f32[3,128,512]{2,1,0:T(8,128)S(1)} %bitcast.11, f32[3,128,512]{2,1,0:T(8,128)S(1)} %bitcast.13, ...), custom_call_target="tpu_custom_call" | custom-call | flops 1600000000 | bytes 5000000 | tf_op jit(solution)/shard_map/inner/pallas_call | solution.py:444
  17.7 0.0 collective-permute-done.a
  17.7 0.0 collective-permute-done.1.b
  17.7 0.0 collective-permute-done.2.c.c2
  17.7 0.0 collective-permute-done.3.d
  17.7 0.0 copy-done.1
  17.7 0.0 copy-done.8
  17.7 0.1 lines.1
  17.9 0.0 copy-start.2
  17.9 0.0 copy-start.3
  17.9 0.0 copy-start.5
  17.9 0.0 copy-start.7
  17.9 0.8 %collective-permute-start.4 = (f32[8,128]{1,0:T(8,128)S(1)}, f32[8,128]{1,0:T(8,128)S(1)}, u32[]{:S(2)}, u32[]{:S(2)}) collective-permute-start(f32[8,128]{1,0:T(8,128)S(1)} %get-tuple-element.43), channel_id=1, source_target_pairs={{1,2},{2,1},{3,4},{4,3},{5,6},{6,5},{7,8},{8,7},{9,10},{10,9},{11,... | collective-permute-start | bytes 12296 | tf_op jit(solution)/shard_map/ppermute | solution.py:618
  18.7 3.1 %collective-permute-start.5 = (f32[8,128]{1,0:T(8,128)S(1)}, f32[8,128]{1,0:T(8,128)S(1)}, u32[]{:S(2)}, u32[]{:S(2)}) collective-permute-start(f32[8,128]{1,0:T(8,128)S(1)} %get-tuple-element.44), channel_id=1, source_target_pairs={{0,1},{1,0},{2,3},{3,2},{4,5},{5,4},{6,7},{7,6},{8,9},{9,8},{10,11... | collective-permute-start | bytes 12296 | tf_op jit(solution)/shard_map/ppermute | solution.py:617
  21.8 3.7 %inner.3.base_b = f32[3,128,512]{2,1,0:T(8,128)S(1)} custom-call(f32[5,128,512]{2,1,0:T(8,128)S(1)} %bitcast.10, f32[3,128,512]{2,1,0:T(8,128)S(1)} %bitcast.12, f32[3,128,512]{2,1,0:T(8,128)S(1)} %bitcast.14, f32[128,128]{1,0:T(8,128)S(1)} %keep.1.refs_3_, bf16[384,256]{1,0:T(8,128)(2,1)S(1)} %copy-done.12, bf16[256,256]{1,0:T(8,128)(2,1)S(1)} %copy-done.4, ...), custom_call_target="tpu_custom_call" | custom-call | flops 2400000000 | bytes 5000000 | tf_op jit(solution)/shard_map/inner/pallas_call | solution.py:444
  25.5 0.0 collective-permute-done.4.across
  25.5 0.0 collective-permute-done.5.inside
  25.5 0.0 copy-done.2
  25.5 0.0 copy-done.3
  25.5 0.0 copy-done.5
  25.5 0.0 copy-done.7
  25.5 1.9 %outer.1 = f32[5,128,512]{2,1,0:T(8,128)} custom-call(bf16[320,128]{1,0:T(8,128)(2,1)S(1)} %collective-permute-done.a, bf16[320,128]{1,0:T(8,128)(2,1)S(1)} %collective-permute-done.1.b, f32[320,128]{1,0:T(8,128)S(1)} %copy-done.1, bf16[320,128]{1,0:T(8,128)(2,1)S(1)} %collective-permute-done.2.c.c2, bf16[320,128]{1,0:T(8,128)(2,1)S(1)} %collective-permute-done.3.d, ...), custom_call_target="tpu_custom_call" | custom-call | tf_op jit(solution)/shard_map/outer/pallas_call | solution.py:581
Async XLA Ops:
  3.3 14.4 %collective-permute-start = (bf16[320,128]{1,0:T(8,128)(2,1)}, bf16[320,128]{1,0:T(8,128)(2,1)S(1)}, u32[]{:S(2)}, u32[]{:S(2)}) collective-permute-start(bf16[320,128]{1,0:T(8,128)(2,1)} %get-tuple-element.28), channel_id=1, source_target_pairs={{0,4},{4,8},{8,12},{12,16},{16,20},{20,24},{24,28},{28,0},{1,5},{5... | collective-permute-start | bytes 245768 | tf_op jit(solution)/shard_map/ppermute | solution.py:607
  6.2 11.4 %collective-permute-start.1 = (bf16[320,128]{1,0:T(8,128)(2,1)}, bf16[320,128]{1,0:T(8,128)(2,1)S(1)}, u32[]{:S(2)}, u32[]{:S(2)}) collective-permute-start(bf16[320,128]{1,0:T(8,128)(2,1)} %get-tuple-element.29), channel_id=1, source_target_pairs={{0,8},{4,12},{8,16},{12,20},{16,24},{20,28},{24,0},{28,4},{1,9},{5... | collective-permute-start | bytes 245768 | tf_op jit(solution)/shard_map/ppermute | solution.py:607
  7.8 9.9 %collective-permute-start.2 = (bf16[320,128]{1,0:T(8,128)(2,1)}, bf16[320,128]{1,0:T(8,128)(2,1)S(1)}, u32[]{:S(2)}, u32[]{:S(2)}) collective-permute-start(bf16[320,128]{1,0:T(8,128)(2,1)} %get-tuple-element.31), channel_id=1, source_target_pairs={{0,28},{4,0},{8,4},{12,8},{16,12},{20,16},{24,20},{28,24},{1,29},{... | collective-permute-start | bytes 245768 | tf_op jit(solution)/shard_map/ppermute | solution.py:607
  11.1 6.7 %collective-permute-start.3 = (bf16[320,128]{1,0:T(8,128)(2,1)}, bf16[320,128]{1,0:T(8,128)(2,1)S(1)}, u32[]{:S(2)}, u32[]{:S(2)}) collective-permute-start(bf16[320,128]{1,0:T(8,128)(2,1)} %get-tuple-element.32), channel_id=1, source_target_pairs={{0,24},{4,28},{8,0},{12,4},{16,8},{20,12},{24,16},{28,20},{1,25},{... | collective-permute-start | bytes 245768 | tf_op jit(solution)/shard_map/ppermute | solution.py:607
  11.4 0.7 %copy-start.11 = (f32[8,128]{1,0:T(8,128)S(1)}, f32[8,128]{1,0:T(8,128)}, u32[]{:S(2)}) copy-start(f32[8,128]{1,0:T(8,128)} %get-tuple-element.33.marks) | copy-start | bytes 12292
  12.1 1.3 %copy-start = (f32[128,5,512]{2,0,1:T(8,128)S(1)}, f32[128,5,512]{2,0,1:T(8,128)}, u32[]{:S(2)}) copy-start(f32[128,5,512]{2,0,1:T(8,128)} %param.17) | copy-start | bytes 3932164
  12.1 1.3 %copy-start.4 = (bf16[256,256]{1,0:T(8,128)(2,1)S(1)}, bf16[256,256]{1,0:T(8,128)(2,1)}, u32[]{:S(2)}) copy-start(bf16[256,256]{1,0:T(8,128)(2,1)} %constant.20.clone.refs_5_.wb1) | copy-start | bytes 393220
  12.1 1.3 %copy-start.6 = (bf16[256,128]{1,0:T(8,128)(2,1)S(1)}, bf16[256,128]{1,0:T(8,128)(2,1)}, u32[]{:S(2)}) copy-start(bf16[256,128]{1,0:T(8,128)(2,1)} %constant.21.clone.refs_6_.wb2) | copy-start | bytes 196612
  12.1 1.6 %copy-start.9 = (f32[128,3,512]{2,0,1:T(8,128)S(1)}, f32[128,3,512]{2,0,1:T(8,128)}, u32[]{:S(2)}) copy-start(f32[128,3,512]{2,0,1:T(8,128)} %param.18) | copy-start | bytes 2359300
  12.1 1.8 %copy-start.10 = (f32[128,3,512]{2,0,1:T(8,128)S(1)}, f32[128,3,512]{2,0,1:T(8,128)}, u32[]{:S(2)}) copy-start(f32[128,3,512]{2,0,1:T(8,128)} %param.19) | copy-start | bytes 2359300
  12.1 1.8 %copy-start.12 = (bf16[384,256]{1,0:T(8,128)(2,1)S(1)}, bf16[384,256]{1,0:T(8,128)(2,1)}, u32[]{:S(2)}) copy-start(bf16[384,256]{1,0:T(8,128)(2,1)} %constant.19.clone.refs_4_) | copy-start | bytes 589828
  12.1 1.8 %copy-start.13 = (f32[48,128]{1,0:T(8,128)S(1)}, f32[48,128]{1,0:T(8,128)}, u32[]{:S(2)}) copy-start(f32[48,128]{1,0:T(8,128)} %constant.22.clone.refs_7_) | copy-start | bytes 73732
  13.9 3.8 %copy-start.1 = (f32[320,128]{1,0:T(8,128)S(1)}, f32[320,128]{1,0:T(8,128)}, u32[]{:S(2)}) copy-start(f32[320,128]{1,0:T(8,128)} %get-tuple-element.37.own) | copy-start | bytes 491524
  13.9 3.8 %copy-start.8 = (f32[16,128]{1,0:T(8,128)S(1)}, f32[16,128]{1,0:T(8,128)}, u32[]{:S(2)}) copy-start(f32[16,128]{1,0:T(8,128)} %get-tuple-element.40.edges) | copy-start | bytes 24580
  17.9 7.6 %copy-start.2 = (bf16[256,1024]{1,0:T(8,128)(2,1)S(1)}, bf16[256,1024]{1,0:T(8,128)(2,1)}, u32[]{:S(2)}) copy-start(bf16[256,1024]{1,0:T(8,128)(2,1)} %constant.26.clone.place) | copy-start | bytes 1572868
  17.9 7.6 %copy-start.3 = (bf16[256,1024]{1,0:T(8,128)(2,1)S(1)}, bf16[256,1024]{1,0:T(8,128)(2,1)}, u32[]{:S(2)}) copy-start(bf16[256,1024]{1,0:T(8,128)(2,1)} %constant.25.clone.spread) | copy-start | bytes 1572868
  17.9 7.6 %copy-start.5 = (bf16[256,256]{1,0:T(8,128)(2,1)S(1)}, bf16[256,256]{1,0:T(8,128)(2,1)}, u32[]{:S(2)}) copy-start(bf16[256,256]{1,0:T(8,128)(2,1)} %constant.23.clone.wf1) | copy-start | bytes 393220
  17.9 7.6 %copy-start.7 = (bf16[128,256]{1,0:T(8,128)(2,1)S(1)}, bf16[128,256]{1,0:T(8,128)(2,1)}, u32[]{:S(2)}) copy-start(bf16[128,256]{1,0:T(8,128)(2,1)} %constant.24.clone.wf2) | copy-start | bytes 196612
  17.9 7.6 %collective-permute-start.4 = (f32[8,128]{1,0:T(8,128)S(1)}, f32[8,128]{1,0:T(8,128)S(1)}, u32[]{:S(2)}, u32[]{:S(2)}) collective-permute-start(f32[8,128]{1,0:T(8,128)S(1)} %get-tuple-element.43), channel_id=1, source_target_pairs={{1,2},{2,1},{3,4},{4,3},{5,6},{6,5},{7,8},{8,7},{9,10},{10,9},{11,... | collective-permute-start | bytes 12296 | tf_op jit(solution)/shard_map/ppermute | solution.py:618
  18.7 6.8 %collective-permute-start.5 = (f32[8,128]{1,0:T(8,128)S(1)}, f32[8,128]{1,0:T(8,128)S(1)}, u32[]{:S(2)}, u32[]{:S(2)}) collective-permute-start(f32[8,128]{1,0:T(8,128)S(1)} %get-tuple-element.44), channel_id=1, source_target_pairs={{0,1},{1,0},{2,3},{3,2},{4,5},{5,4},{6,7},{7,6},{8,9},{9,8},{10,11... | collective-permute-start | bytes 12296 | tf_op jit(solution)/shard_map/ppermute | solution.py:617

commit v7 on v5

--- a/solution.py
+++ b/solution.py
@@ -198,7 +198,7 @@
 def fold_kernel(
     route_hbm, target_hbm, code_hbm, hang_hbm, adj_hbm, fold_hbm, *refs
 ):
-    outs, edges_out, marks_out, ints, x, fold, wide, sems = refs[:5], *refs[5:]
+    outs, edges_out, marks_out, ints, x, fold, faces, sems = refs[:5], *refs[5:]
     peers = lax.axis_size("dom")
     copies = fetch(
         [(ref, ints.at[n]) for n, ref in enumerate((route_hbm, target_hbm, code_hbm, hang_hbm))]
@@ -216,7 +216,7 @@
     marked = down(jnp.where(hang == 1, code, -2)) - (lane // 64).astype(F32)
     odd = lane % 16 >= 8
     group = (lane // 16 + 1) % 4
-    for f in range(5):
+    def field(f, carry):
         packed = jnp.zeros((E, 128), F32)
         for c in range(4):
             moved = x[f, :, 128 * c : 128 * c + 128]
@@ -226,17 +226,16 @@
         high = packed.astype(BF16)
         high_f = high.astype(F32)
         both = jnp.where(odd, high_f, pltpu.roll(packed - high_f, 8, 1)).astype(BF16)
-        wide[E * f : E * f + E, 0:128] = both
-        wide[E * f : E * f + E, 128:256] = high
-    mapped = dot(wide[...], fold[...])
-    faces = []
-    for f in range(5):
+        mapped = dot(jnp.concatenate([both, high], 1), fold[...])
         total = jnp.zeros((E, 128), F32)
         for q in range(4):
             total = total + jnp.where(
-                marked == 2.0 * q, mapped[E * f : E * f + E, 128 * q : 128 * q + 128], 0.0
+                marked == 2.0 * q, mapped[:, 128 * q : 128 * q + 128], 0.0
             )
-        faces.append(total + pltpu.roll(total, 64, 1))
+        faces[f] = total + pltpu.roll(total, 64, 1)
+        return carry
+
+    lax.fori_loop(0, 5, field, 0)
     f01 = jnp.where(left, faces[0], faces[1]).astype(BF16)
     f23 = jnp.where(left, faces[2], faces[3]).astype(BF16)
     sums = dot(hit, jnp.concatenate([f01, f23, faces[4].astype(BF16)], 1))
@@ -278,7 +277,7 @@
             pltpu.VMEM((4, 1, E), jnp.int32),
             pltpu.VMEM((5, E, 512), F32),
             pltpu.VMEM((256, 512), BF16),
-            pltpu.VMEM((5 * E, 256), BF16),
+            pltpu.VMEM((5, E, 128), F32),
             pltpu.SemaphoreType.DMA((10,)),
         ],
         compiler_params=pltpu.CompilerParams(vmem_limit_bytes=WHOLE),
@@ -472,7 +471,7 @@
 
 def post_kernel(
     a, b, own, c2, d, across, inside, base_a, base_b, q_ref, plane, end_q, end_mv,
-    wf1, wf2, wb1, wb2, spread, place, out_hbm, out, out_sems,
+    wf1, wf2, wb1, wb2, spread, place, out_hbm, out, out_sems, y_parts, r_parts, rows_of,
 ):
     out_copies = [
         pltpu.make_async_copy(out.at[f], out_hbm.at[f], out_sems.at[f]) for f in range(5)
@@ -521,28 +520,40 @@
     ]
     r = two_dims(stacked, *factors, wf1, wf2, wb1, wb2)
     ends = r[3 * E :]
-    y_parts = jnp.concatenate(parts_of(stacked[: 3 * E]), 1)
-    r_parts = jnp.concatenate(parts_of(r[: 3 * E]), 1)
-    for n in range(3):
-        rows = slice(E * n, E * n + E)
-        for f in range(2 * n, min(2 * n + 2, 5)):
-            cols = slice(512 * (f - 2 * n), 512 * (f - 2 * n) + 512)
-            out[f] = (
-                (base_a[f] if f < 2 else base_b[f - 2])
-                + q_ref[...] * dot(y_parts[rows], spread[:, cols])
-                + dot(r_parts[rows], place[:, cols])
-            )
-            for c in range(4):
-                at = slice(128 * c, 128 * c + 128)
-                first = end_q[0, c, 0:1] * halo[0][f : f + 1]
-                final = end_q[1, c, 7:8] * halo[1][f : f + 1]
-                if c == 0:
-                    first = first + jnp.where(small_left, ends[f : f + 1], 0.0)
-                if c == 3:
-                    final = final + jnp.where(small_left, 0.0, ends[8 + f : 9 + f])
-                out[f, 0:1, at] += first
-                out[f, E - 1 : E, at] += final
-            out_copies[f].start()
+    y_parts[...] = jnp.concatenate(parts_of(stacked[: 3 * E]), 1)
+    r_parts[...] = jnp.concatenate(parts_of(r[: 3 * E]), 1)
+    rows_of[0], rows_of[1] = halo
+    rows_of[2], rows_of[3] = ends[0:8], ends[8:16]
+
+    def field(base, first_field, n):
+        f = first_field + n
+        rows = pl.ds(pl.multiple_of(E * lax.div(f, 2), E), E)
+        cols = pl.ds(pl.multiple_of(512 * lax.rem(f, 2), 512), 512)
+        out[f] = (
+            base[n]
+            + q_ref[...] * dot(y_parts[rows], spread[:, cols])
+            + dot(r_parts[rows], place[:, cols])
+        )
+        low, high, low_end, high_end = (rows_of[t, pl.ds(f, 1)] for t in range(4))
+        for c in range(4):
+            at = slice(128 * c, 128 * c + 128)
+            first = end_q[0, c, 0:1] * low
+            final = end_q[1, c, 7:8] * high
+            if c == 0:
+                first = first + jnp.where(small_left, low_end, 0.0)
+            if c == 3:
+                final = final + jnp.where(small_left, 0.0, high_end)
+            out[f, 0:1, at] += first
+            out[f, E - 1 : E, at] += final
+        pltpu.make_async_copy(out.at[f], out_hbm.at[f], out_sems.at[f]).start()
+
+    for base, first_field, count in ((base_a, 0, 2), (base_b, 2, 3)):
+
+        def step(n, carry, base=base, first_field=first_field):
+            field(base, first_field, n)
+            return carry
+
+        lax.fori_loop(0, count, step, 0)
     for copy in out_copies:
         copy.wait()
 
@@ -553,7 +564,13 @@
         out_shape=jax.ShapeDtypeStruct((5, E, 512), F32),
         in_specs=[VM] * 19,
         out_specs=HBM,
-        scratch_shapes=[pltpu.VMEM((5, E, 512), F32), pltpu.SemaphoreType.DMA((5,))],
+        scratch_shapes=[
+            pltpu.VMEM((5, E, 512), F32),
+            pltpu.SemaphoreType.DMA((5,)),
+            pltpu.VMEM((3 * E, 256), BF16),
+            pltpu.VMEM((3 * E, 256), BF16),
+            pltpu.VMEM((4, 8, 128), F32),
+        ],
         compiler_params=pltpu.CompilerParams(vmem_limit_bytes=LIMIT),
         name="outer",
     )(

time: 25 us -> 27.1 us (1.084)
  Pallas kernels: 10.2 us -> 12.3 us
    pallas_call x1, Pallas kernels: 3.25 us -> 4.58 us  [folded_of(): pl.pallas_call(fold_kernel, out_shape=[jax.ShapeDtypeStruct((320, 128), F...]
    pallas_call x1, Pallas kernels: 1.92 us -> 2.71 us  [post_of(): pl.pallas_call(post_kernel, out_shape=jax.ShapeDtypeStruct((5, E, 512), F...]
  transfers between devices with their start and end apart: 6 -> 6, of which waited for: 0 -> 0; matrix products, arithmetic and copies ran while one was open for 0% -> 0% of each run, Pallas kernels for 20% -> 18%
where the time goes in v7:
time: 27.1 us; the launch traced here: 26.9 us
  Pallas kernels  12.3 us (45%)
  starting transfers between devices  12 us (44%)
  local copies, waits for them, and re-layouts  2.41 us (9%)
    ppermute x4, starting transfers between devices, shards(): parts[n] = lax.ppermute(parts[n], 'dom', pairs)  8.12 us
    pallas_call x2, Pallas kernels, main_of(): pl.pallas_call(body, out_shape=[jax.ShapeDtypeStruct(shape, F32) for shap...  4.76 us
    pallas_call x1, Pallas kernels, folded_of(): pl.pallas_call(fold_kernel, out_shape=[jax.ShapeDtypeStruct((320, 128), F...  4.58 us
    ppermute x1, starting transfers between devices, shards(): inward = lax.ppermute(out_b, axes, inside)  3.07 us
    pallas_call x1, Pallas kernels, post_of(): pl.pallas_call(post_kernel, out_shape=jax.ShapeDtypeStruct((5, E, 512), F...  2.71 us
    unnamed x26, local copies, waits for them, and re-layouts  2.41 us
    ppermute x1, starting transfers between devices, shards(): outward = lax.ppermute(out_a, axes, across)  0.78 us
  transfers between devices with their start and end apart: 6, of which 0 were waited for; matrix products, arithmetic and copies ran while one was open for 0% of the time, Pallas kernels for 18%

profile of v7, /device:TPU:0, one launch (start us, length us, event | category | flops | bytes accessed | tf_op | source)
XLA Modules:
  0.0 26.9 jit_solution(12918373530705845480)
XLA Ops:
  0.0 4.6 %fold.1 = (bf16[320,128]{1,0:T(8,128)(2,1)}, bf16[320,128]{1,0:T(8,128)(2,1)}, f32[320,128]{1,0:T(8,128)}, bf16[320,128]{1,0:T(8,128)(2,1)}, bf16[320,128]{1,0:T...) custom-call(s32[1,128]{1,0:T(1,128)} %bitcast.15, s32[1,128]{1,0:T(1,128)} %bitcast.16, s32[1,128]{1,0:T(1,128)} %bitcast.17, ...), custom_call_target="tpu_custom_call" | custom-call | tf_op jit(solution)/shard_map/fold/pallas_call | solution.py:268
  4.6 3.0 %collective-permute-start = (bf16[320,128]{1,0:T(8,128)(2,1)}, bf16[320,128]{1,0:T(8,128)(2,1)S(1)}, u32[]{:S(2)}, u32[]{:S(2)}) collective-permute-start(bf16[320,128]{1,0:T(8,128)(2,1)} %get-tuple-element.28), channel_id=1, source_target_pairs={{0,4},{4,8},{8,12},{12,16},{16,20},{20,24},{24,28},{28,0},{1,5},{5... | collective-permute-start | bytes 245768 | tf_op jit(solution)/shard_map/ppermute | solution.py:594
  7.6 1.6 %collective-permute-start.1 = (bf16[320,128]{1,0:T(8,128)(2,1)}, bf16[320,128]{1,0:T(8,128)(2,1)S(1)}, u32[]{:S(2)}, u32[]{:S(2)}) collective-permute-start(bf16[320,128]{1,0:T(8,128)(2,1)} %get-tuple-element.29), channel_id=1, source_target_pairs={{0,8},{4,12},{8,16},{12,20},{16,24},{20,28},{24,0},{28,4},{1,9},{5... | collective-permute-start | bytes 245768 | tf_op jit(solution)/shard_map/ppermute | solution.py:594
  9.2 3.2 %collective-permute-start.2 = (bf16[320,128]{1,0:T(8,128)(2,1)}, bf16[320,128]{1,0:T(8,128)(2,1)S(1)}, u32[]{:S(2)}, u32[]{:S(2)}) collective-permute-start(bf16[320,128]{1,0:T(8,128)(2,1)} %get-tuple-element.31), channel_id=1, source_target_pairs={{0,28},{4,0},{8,4},{12,8},{16,12},{20,16},{24,20},{28,24},{1,29},{... | collective-permute-start | bytes 245768 | tf_op jit(solution)/shard_map/ppermute | solution.py:594
  12.4 0.3 %collective-permute-start.3 = (bf16[320,128]{1,0:T(8,128)(2,1)}, bf16[320,128]{1,0:T(8,128)(2,1)S(1)}, u32[]{:S(2)}, u32[]{:S(2)}) collective-permute-start(bf16[320,128]{1,0:T(8,128)(2,1)} %get-tuple-element.32), channel_id=1, source_target_pairs={{0,24},{4,28},{8,0},{12,4},{16,8},{20,12},{24,16},{28,20},{1,25},{... | collective-permute-start | bytes 245768 | tf_op jit(solution)/shard_map/ppermute | solution.py:594
  12.7 0.0 copy-start.11
  12.7 0.7 %copy-done.11 = f32[8,128]{1,0:T(8,128)S(1)} copy-done((f32[8,128]{1,0:T(8,128)S(1)}, f32[8,128]{1,0:T(8,128)}, u32[]{:S(2)}) %copy-start.11) | copy-done | bytes 4120
  13.4 0.0 copy-start
  13.4 0.0 copy-start.4
  13.4 0.0 copy-start.5
  13.4 0.0 copy-start.6
  13.4 0.0 copy-start.7
  13.4 0.0 copy-start.9
  13.4 0.0 copy-start.10
  13.4 0.0 copy-start.12
  13.5 0.1 keep.1.refs_3_
  13.6 1.1 %copy-done = f32[128,5,512]{2,0,1:T(8,128)S(1)} copy-done((f32[128,5,512]{2,0,1:T(8,128)S(1)}, f32[128,5,512]{2,0,1:T(8,128)}, u32[]{:S(2)}) %copy-start) | copy-done | bytes 1310744
  14.7 0.0 copy-done.4
  14.7 0.0 copy-done.5
  14.7 0.0 copy-done.6
  14.7 0.0 copy-done.7
  14.7 0.3 %copy-done.9 = f32[128,3,512]{2,0,1:T(8,128)S(1)} copy-done((f32[128,3,512]{2,0,1:T(8,128)S(1)}, f32[128,3,512]{2,0,1:T(8,128)}, u32[]{:S(2)}) %copy-start.9) | copy-done | bytes 786456
  15.0 0.2 copy-done.10
  15.3 0.0 copy-done.12
  15.3 0.0 copy-start.1
  15.3 0.0 copy-start.8
  15.3 2.4 %inner.2 = (f32[2,128,512]{2,1,0:T(8,128)S(1)}, f32[128,512]{1,0:T(8,128)S(1)}, f32[4,128,128]{2,1,0:T(8,128)S(1)}, f32[2,4,8,128]{3,2,1,0:T(8,128)S(1)}, f32[2,4,8,128]{3,2,1,0:T(8,128)S(1)}) custom-call(f32[5,128,512]{2,1,0:T(8,128)S(1)} %bitcast.9, f32[3,128,512]{2,1,0:T(8,128)S(1)} %bitcast.11, f32[3,128,512]{2,1,0:T(8,128)S(1)} %bitcast.13, ...), custom_call_target="tpu_custom_call" | custom-call | flops 1600000000 | bytes 5000000 | tf_op jit(solution)/shard_map/inner/pallas_call | solution.py:418
  17.7 0.0 collective-permute-done.a
  17.7 0.0 collective-permute-done.1.b
  17.7 0.0 collective-permute-done.2.c.c2
  17.7 0.0 collective-permute-done.3.d
  17.7 0.0 copy-done.1
  17.7 0.0 copy-done.8
  17.7 0.1 lines.1
  17.9 0.0 copy-start.2
  17.9 0.0 copy-start.3
  17.9 0.8 %collective-permute-start.4 = (f32[8,128]{1,0:T(8,128)S(1)}, f32[8,128]{1,0:T(8,128)S(1)}, u32[]{:S(2)}, u32[]{:S(2)}) collective-permute-start(f32[8,128]{1,0:T(8,128)S(1)} %get-tuple-element.43), channel_id=1, source_target_pairs={{1,2},{2,1},{3,4},{4,3},{5,6},{6,5},{7,8},{8,7},{9,10},{10,9},{11,... | collective-permute-start | bytes 12296 | tf_op jit(solution)/shard_map/ppermute | solution.py:605
  18.7 3.1 %collective-permute-start.5 = (f32[8,128]{1,0:T(8,128)S(1)}, f32[8,128]{1,0:T(8,128)S(1)}, u32[]{:S(2)}, u32[]{:S(2)}) collective-permute-start(f32[8,128]{1,0:T(8,128)S(1)} %get-tuple-element.44), channel_id=1, source_target_pairs={{0,1},{1,0},{2,3},{3,2},{4,5},{5,4},{6,7},{7,6},{8,9},{9,8},{10,11... | collective-permute-start | bytes 12296 | tf_op jit(solution)/shard_map/ppermute | solution.py:604
  21.7 2.4 %inner.3.base_b = f32[3,128,512]{2,1,0:T(8,128)S(1)} custom-call(f32[5,128,512]{2,1,0:T(8,128)S(1)} %bitcast.10, f32[3,128,512]{2,1,0:T(8,128)S(1)} %bitcast.12, f32[3,128,512]{2,1,0:T(8,128)S(1)} %bitcast.14, f32[128,128]{1,0:T(8,128)S(1)} %keep.1.refs_3_, bf16[256,256]{1,0:T(8,128)(2,1)S(1)} %copy-done.5, bf16[128,256]{1,0:T(8,128)(2,1)S(1)} %copy-done.7, ...), custom_call_target="tpu_custom_call" | custom-call | flops 2400000000 | bytes 5000000 | tf_op jit(solution)/shard_map/inner/pallas_call | solution.py:418
  24.1 0.0 collective-permute-done.4.across
  24.1 0.0 collective-permute-done.5.inside
  24.2 0.0 copy-done.2
  24.2 0.0 copy-done.3
  24.2 2.7 %outer.1 = f32[5,128,512]{2,1,0:T(8,128)} custom-call(bf16[320,128]{1,0:T(8,128)(2,1)S(1)} %collective-permute-done.a, bf16[320,128]{1,0:T(8,128)(2,1)S(1)} %collective-permute-done.1.b, f32[320,128]{1,0:T(8,128)S(1)} %copy-done.1, bf16[320,128]{1,0:T(8,128)(2,1)S(1)} %collective-permute-done.2.c.c2, bf16[320,128]{1,0:T(8,128)(2,1)S(1)} %collective-permute-done.3.d, ...), custom_call_target="tpu_custom_call" | custom-call | tf_op jit(solution)/shard_map/outer/pallas_call | solution.py:562
Async XLA Ops:
  4.6 13.1 %collective-permute-start = (bf16[320,128]{1,0:T(8,128)(2,1)}, bf16[320,128]{1,0:T(8,128)(2,1)S(1)}, u32[]{:S(2)}, u32[]{:S(2)}) collective-permute-start(bf16[320,128]{1,0:T(8,128)(2,1)} %get-tuple-element.28), channel_id=1, source_target_pairs={{0,4},{4,8},{8,12},{12,16},{16,20},{20,24},{24,28},{28,0},{1,5},{5... | collective-permute-start | bytes 245768 | tf_op jit(solution)/shard_map/ppermute | solution.py:594
  7.6 10.1 %collective-permute-start.1 = (bf16[320,128]{1,0:T(8,128)(2,1)}, bf16[320,128]{1,0:T(8,128)(2,1)S(1)}, u32[]{:S(2)}, u32[]{:S(2)}) collective-permute-start(bf16[320,128]{1,0:T(8,128)(2,1)} %get-tuple-element.29), channel_id=1, source_target_pairs={{0,8},{4,12},{8,16},{12,20},{16,24},{20,28},{24,0},{28,4},{1,9},{5... | collective-permute-start | bytes 245768 | tf_op jit(solution)/shard_map/ppermute | solution.py:594
  9.2 8.5 %collective-permute-start.2 = (bf16[320,128]{1,0:T(8,128)(2,1)}, bf16[320,128]{1,0:T(8,128)(2,1)S(1)}, u32[]{:S(2)}, u32[]{:S(2)}) collective-permute-start(bf16[320,128]{1,0:T(8,128)(2,1)} %get-tuple-element.31), channel_id=1, source_target_pairs={{0,28},{4,0},{8,4},{12,8},{16,12},{20,16},{24,20},{28,24},{1,29},{... | collective-permute-start | bytes 245768 | tf_op jit(solution)/shard_map/ppermute | solution.py:594
  12.4 5.3 %collective-permute-start.3 = (bf16[320,128]{1,0:T(8,128)(2,1)}, bf16[320,128]{1,0:T(8,128)(2,1)S(1)}, u32[]{:S(2)}, u32[]{:S(2)}) collective-permute-start(bf16[320,128]{1,0:T(8,128)(2,1)} %get-tuple-element.32), channel_id=1, source_target_pairs={{0,24},{4,28},{8,0},{12,4},{16,8},{20,12},{24,16},{28,20},{1,25},{... | collective-permute-start | bytes 245768 | tf_op jit(solution)/shard_map/ppermute | solution.py:594
  12.7 0.7 %copy-start.11 = (f32[8,128]{1,0:T(8,128)S(1)}, f32[8,128]{1,0:T(8,128)}, u32[]{:S(2)}) copy-start(f32[8,128]{1,0:T(8,128)} %get-tuple-element.33.marks) | copy-start | bytes 12292
  13.4 1.3 %copy-start = (f32[128,5,512]{2,0,1:T(8,128)S(1)}, f32[128,5,512]{2,0,1:T(8,128)}, u32[]{:S(2)}) copy-start(f32[128,5,512]{2,0,1:T(8,128)} %param.15) | copy-start | bytes 3932164
  13.4 1.3 %copy-start.4 = (bf16[256,256]{1,0:T(8,128)(2,1)S(1)}, bf16[256,256]{1,0:T(8,128)(2,1)}, u32[]{:S(2)}) copy-start(bf16[256,256]{1,0:T(8,128)(2,1)} %constant.19.clone.refs_6_.wb1) | copy-start | bytes 393220
  13.4 1.3 %copy-start.5 = (bf16[256,256]{1,0:T(8,128)(2,1)S(1)}, bf16[256,256]{1,0:T(8,128)(2,1)}, u32[]{:S(2)}) copy-start(bf16[256,256]{1,0:T(8,128)(2,1)} %constant.17.clone.refs_4_.wf1) | copy-start | bytes 393220
  13.4 1.3 %copy-start.6 = (bf16[256,128]{1,0:T(8,128)(2,1)S(1)}, bf16[256,128]{1,0:T(8,128)(2,1)}, u32[]{:S(2)}) copy-start(bf16[256,128]{1,0:T(8,128)(2,1)} %constant.20.clone.refs_7_.wb2) | copy-start | bytes 196612
  13.4 1.3 %copy-start.7 = (bf16[128,256]{1,0:T(8,128)(2,1)S(1)}, bf16[128,256]{1,0:T(8,128)(2,1)}, u32[]{:S(2)}) copy-start(bf16[128,256]{1,0:T(8,128)(2,1)} %constant.18.clone.refs_5_.wf2) | copy-start | bytes 196612
  13.4 1.6 %copy-start.9 = (f32[128,3,512]{2,0,1:T(8,128)S(1)}, f32[128,3,512]{2,0,1:T(8,128)}, u32[]{:S(2)}) copy-start(f32[128,3,512]{2,0,1:T(8,128)} %param.16) | copy-start | bytes 2359300
  13.4 1.8 %copy-start.10 = (f32[128,3,512]{2,0,1:T(8,128)S(1)}, f32[128,3,512]{2,0,1:T(8,128)}, u32[]{:S(2)}) copy-start(f32[128,3,512]{2,0,1:T(8,128)} %param.17) | copy-start | bytes 2359300
  13.4 1.8 %copy-start.12 = (f32[48,128]{1,0:T(8,128)S(1)}, f32[48,128]{1,0:T(8,128)}, u32[]{:S(2)}) copy-start(f32[48,128]{1,0:T(8,128)} %constant.21.clone.refs_8_) | copy-start | bytes 73732
  15.3 2.4 %copy-start.1 = (f32[320,128]{1,0:T(8,128)S(1)}, f32[320,128]{1,0:T(8,128)}, u32[]{:S(2)}) copy-start(f32[320,128]{1,0:T(8,128)} %get-tuple-element.37.own) | copy-start | bytes 491524
  15.3 2.4 %copy-start.8 = (f32[16,128]{1,0:T(8,128)S(1)}, f32[16,128]{1,0:T(8,128)}, u32[]{:S(2)}) copy-start(f32[16,128]{1,0:T(8,128)} %get-tuple-element.40.edges) | copy-start | bytes 24580
  17.9 6.3 %copy-start.2 = (bf16[256,1024]{1,0:T(8,128)(2,1)S(1)}, bf16[256,1024]{1,0:T(8,128)(2,1)}, u32[]{:S(2)}) copy-start(bf16[256,1024]{1,0:T(8,128)(2,1)} %constant.23.clone.place) | copy-start | bytes 1572868
  17.9 6.3 %copy-start.3 = (bf16[256,1024]{1,0:T(8,128)(2,1)S(1)}, bf16[256,1024]{1,0:T(8,128)(2,1)}, u32[]{:S(2)}) copy-start(bf16[256,1024]{1,0:T(8,128)(2,1)} %constant.22.clone.spread) | copy-start | bytes 1572868
  17.9 6.3 %collective-permute-start.4 = (f32[8,128]{1,0:T(8,128)S(1)}, f32[8,128]{1,0:T(8,128)S(1)}, u32[]{:S(2)}, u32[]{:S(2)}) collective-permute-start(f32[8,128]{1,0:T(8,128)S(1)} %get-tuple-element.43), channel_id=1, source_target_pairs={{1,2},{2,1},{3,4},{4,3},{5,6},{6,5},{7,8},{8,7},{9,10},{10,9},{11,... | collective-permute-start | bytes 12296 | tf_op jit(solution)/shard_map/ppermute | solution.py:605
  18.7 5.5 %collective-permute-start.5 = (f32[8,128]{1,0:T(8,128)S(1)}, f32[8,128]{1,0:T(8,128)S(1)}, u32[]{:S(2)}, u32[]{:S(2)}) collective-permute-start(f32[8,128]{1,0:T(8,128)S(1)} %get-tuple-element.44), channel_id=1, source_target_pairs={{0,1},{1,0},{2,3},{3,2},{4,5},{5,4},{6,7},{7,6},{8,9},{9,8},{10,11... | collective-permute-start | bytes 12296 | tf_op jit(solution)/shard_map/ppermute | solution.py:604

commit v8 on v4

--- a/solution.py
+++ b/solution.py
@@ -25,7 +25,7 @@
 HBM = pl.BlockSpec(memory_space=pltpu.HBM)
 VM = pl.BlockSpec(memory_space=pltpu.VMEM)
 LIMIT = 32 * 1024 * 1024
-ORDER = (3, 4, 2, 1, 0)
+ORDER = (3, 4, 2, 0, 1)
 WHOLE = 64 * 1024 * 1024
 
 

time: 25.2 us -> 24.2 us (0.960)
  waiting for transfers between devices: 1.69 us -> 0.68 us
    ppermute x4, waiting for transfers between devices: 1.68 us -> 0.68 us  [shards(): parts[n] = lax.ppermute(parts[n], 'dom', pairs)]
  transfers between devices with their start and end apart: 6 -> 6, of which waited for: 1 -> 1; matrix products, arithmetic and copies ran while one was open for 0% -> 0% of each run, Pallas kernels for 19% -> 20%
where the time goes in v8:
time: 24.2 us; the launch traced here: 24 us
  starting transfers between devices  11.8 us (49%)
  Pallas kernels  10.3 us (43%)
  local copies, waits for them, and re-layouts  0.99 us (4%)
  waiting for transfers between devices  0.68 us (3%)
    ppermute x4, starting transfers between devices, shards(): parts[n] = lax.ppermute(parts[n], 'dom', pairs)  8.11 us
    pallas_call x2, Pallas kernels, main_of(): pl.pallas_call(body, out_shape=[jax.ShapeDtypeStruct(shape, F32) for shap...  4.77 us
    pallas_call x1, Pallas kernels, folded_of(): pl.pallas_call(fold_kernel, out_shape=jax.ShapeDtypeStruct((E + 32, 384),...  3.17 us
    ppermute x1, starting transfers between devices, shards(): inward = lax.ppermute(out_b, axes, inside)  2.95 us
    pallas_call x1, Pallas kernels, post_of(): pl.pallas_call(post_kernel, out_shape=jax.ShapeDtypeStruct((5, E, 512), F...  1.92 us
    unnamed x24, local copies, waits for them, and re-layouts  0.99 us
    ppermute x1, starting transfers between devices, shards(): outward = lax.ppermute(out_a, axes, across)  0.78 us
    ppermute x4, waiting for transfers between devices, shards(): parts[n] = lax.ppermute(parts[n], 'dom', pairs)  0.68 us
  transfers between devices with their start and end apart: 6, of which 1 were waited for; matrix products, arithmetic and copies ran while one was open for 0% of the time, Pallas kernels for 20%

profile of v8, /device:TPU:0, one launch (start us, length us, event | category | flops | bytes accessed | tf_op | source)
XLA Modules:
  0.0 24.0 jit_solution(11412925233817745623)
XLA Ops:
  0.0 3.2 %fold.1.both = f32[160,384]{1,0:T(8,128)} custom-call(s32[1,128]{1,0:T(1,128)} %bitcast.15, s32[1,128]{1,0:T(1,128)} %bitcast.16, s32[1,128]{1,0:T(1,128)} %bitcast.17, s32[1,128]{1,0:T(1,128)} %bitcast.18, f32[5,128,512]{2,1,0:T(8,128)} %bitcast.8, bf16[256,512]{1,0:T(8,128)(2,1)} %constant.16.clone.fold_hbm), custom_call_target="tpu_custom_call" | custom-call | tf_op jit(solution)/shard_map/fold/pallas_call | solution.py:266
  3.2 0.0 copy-start.1
  3.2 0.9 %copy-done.1 = f32[160,384]{1,0:T(8,128)S(1)} copy-done((f32[160,384]{1,0:T(8,128)S(1)}, f32[160,384]{1,0:T(8,128)}, u32[]{:S(2)}) %copy-start.1) | copy-done | bytes 245784
  4.1 0.0 copy-start
  4.1 0.0 copy-start.5
  4.1 0.0 copy-start.6
  4.1 0.0 copy-start.7
  4.1 0.0 copy-start.8
  4.2 0.0 copy-start.9
  4.2 0.0 copy-start.10
  4.2 0.0 copy-start.11
  4.2 0.3 %sums.1 = (bf16[320,128]{1,0:T(8,128)(2,1)S(1)}, bf16[320,128]{1,0:T(8,128)(2,1)S(1)}, f32[320,128]{1,0:T(8,128)S(1)}, bf16[320,128]{1,0:T(8,128)(2,1)S(1)}, bf1...) custom-call(f32[160,384]{1,0:T(8,128)S(1)} %copy-done.1), custom_call_target="tpu_custom_call" | custom-call | flops 8000000000 | bytes 30000000 | tf_op jit(solution)/shard_map/sums/pallas_call | solution.py:406
  4.5 3.0 %collective-permute-start = (bf16[320,128]{1,0:T(8,128)(2,1)S(1)}, bf16[320,128]{1,0:T(8,128)(2,1)S(1)}, u32[]{:S(2)}, u32[]{:S(2)}) collective-permute-start(bf16[320,128]{1,0:T(8,128)(2,1)S(1)} %get-tuple-element.27), channel_id=1, source_target_pairs={{0,4},{4,8},{8,12},{12,16},{16,20},{20,24},{24,28},{28,0},{1,5},{5... | collective-permute-start | bytes 245768 | tf_op jit(solution)/shard_map/ppermute | solution.py:586
  7.5 1.6 %collective-permute-start.1 = (bf16[320,128]{1,0:T(8,128)(2,1)S(1)}, bf16[320,128]{1,0:T(8,128)(2,1)S(1)}, u32[]{:S(2)}, u32[]{:S(2)}) collective-permute-start(bf16[320,128]{1,0:T(8,128)(2,1)S(1)} %get-tuple-element.28), channel_id=1, source_target_pairs={{0,8},{4,12},{8,16},{12,20},{16,24},{20,28},{24,0},{28,4},{1,9},{5... | collective-permute-start | bytes 245768 | tf_op jit(solution)/shard_map/ppermute | solution.py:586
  9.1 2.2 %collective-permute-start.2 = (bf16[320,128]{1,0:T(8,128)(2,1)S(1)}, bf16[320,128]{1,0:T(8,128)(2,1)S(1)}, u32[]{:S(2)}, u32[]{:S(2)}) collective-permute-start(bf16[320,128]{1,0:T(8,128)(2,1)S(1)} %get-tuple-element.30), channel_id=1, source_target_pairs={{0,24},{4,28},{8,0},{12,4},{16,8},{20,12},{24,16},{28,20},{1,25},{... | collective-permute-start | bytes 245768 | tf_op jit(solution)/shard_map/ppermute | solution.py:586
  11.3 1.3 %collective-permute-start.3 = (bf16[320,128]{1,0:T(8,128)(2,1)S(1)}, bf16[320,128]{1,0:T(8,128)(2,1)S(1)}, u32[]{:S(2)}, u32[]{:S(2)}) collective-permute-start(bf16[320,128]{1,0:T(8,128)(2,1)S(1)} %get-tuple-element.31), channel_id=1, source_target_pairs={{0,28},{4,0},{8,4},{12,8},{16,12},{20,16},{24,20},{28,24},{1,29},{... | collective-permute-start | bytes 245768 | tf_op jit(solution)/shard_map/ppermute | solution.py:586
  12.6 0.0 copy-done
  12.6 0.0 copy-done.5
  12.6 0.0 copy-done.6
  12.6 0.0 copy-done.7
  12.6 0.0 copy-done.8
  12.6 0.0 copy-done.9
  12.6 0.0 copy-done.10
  12.6 0.0 copy-done.11
  12.7 0.0 copy-start.2
  12.7 2.4 %inner.2 = (f32[2,128,512]{2,1,0:T(8,128)S(1)}, f32[128,512]{1,0:T(8,128)S(1)}, f32[4,128,128]{2,1,0:T(8,128)S(1)}, f32[2,4,8,128]{3,2,1,0:T(8,128)S(1)}, f32[2,4,8,128]{3,2,1,0:T(8,128)S(1)}) custom-call(f32[5,128,512]{2,1,0:T(8,128)S(1)} %bitcast.9, f32[3,128,512]{2,1,0:T(8,128)S(1)} %bitcast.11, f32[3,128,512]{2,1,0:T(8,128)S(1)} %bitcast.13, ...), custom_call_target="tpu_custom_call" | custom-call | flops 1600000000 | bytes 5000000 | tf_op jit(solution)/shard_map/inner/pallas_call | solution.py:426
  15.0 0.0 collective-permute-done.a
  15.0 0.0 collective-permute-done.1.b
  15.1 0.0 collective-permute-done.2.c.c2
  15.1 0.7 %collective-permute-done.3.d = bf16[320,128]{1,0:T(8,128)(2,1)S(1)} collective-permute-done((bf16[320,128]{1,0:T(8,128)(2,1)S(1)}, bf16[320,128]{1,0:T(8,128)(2,1)S(1)}, u32[]{:S(2)}, u32[]{:S(2)}) %collective-permute-start.3) | collective-permute-done | bytes 81952 | tf_op jit(solution)/shard_map/ppermute | solution.py:586
  15.7 0.0 copy-done.2
  15.7 0.1 lines.1
  15.9 0.0 copy-start.3
  15.9 0.0 copy-start.4
  15.9 0.8 %collective-permute-start.4 = (f32[8,128]{1,0:T(8,128)S(1)}, f32[8,128]{1,0:T(8,128)S(1)}, u32[]{:S(2)}, u32[]{:S(2)}) collective-permute-start(f32[8,128]{1,0:T(8,128)S(1)} %get-tuple-element.41), channel_id=1, source_target_pairs={{1,2},{2,1},{3,4},{4,3},{5,6},{6,5},{7,8},{8,7},{9,10},{10,9},{11,... | collective-permute-start | bytes 12296 | tf_op jit(solution)/shard_map/ppermute | solution.py:595
  16.7 2.9 %collective-permute-start.5 = (f32[8,128]{1,0:T(8,128)S(1)}, f32[8,128]{1,0:T(8,128)S(1)}, u32[]{:S(2)}, u32[]{:S(2)}) collective-permute-start(f32[8,128]{1,0:T(8,128)S(1)} %get-tuple-element.42), channel_id=1, source_target_pairs={{0,1},{1,0},{2,3},{3,2},{4,5},{5,4},{6,7},{7,6},{8,9},{9,8},{10,11... | collective-permute-start | bytes 12296 | tf_op jit(solution)/shard_map/ppermute | solution.py:596
  19.6 2.4 %inner.3.base_b = f32[3,128,512]{2,1,0:T(8,128)S(1)} custom-call(f32[5,128,512]{2,1,0:T(8,128)S(1)} %bitcast.10, f32[3,128,512]{2,1,0:T(8,128)S(1)} %bitcast.12, f32[3,128,512]{2,1,0:T(8,128)S(1)} %bitcast.14, f32[128,128]{1,0:T(8,128)S(1)} %get-tuple-element.44.refs_3_, bf16[256,256]{1,0:T(8,128)(2,1)S(1)} %copy-done.6, bf16[128,256]{1,0:T(8,128)(2,1)S(1)} %copy-done.8, ...), custom_call_target="tpu_custom_call" | custom-call | flops 2400000000 | bytes 5000000 | tf_op jit(solution)/shard_map/inner/pallas_call | solution.py:426
  22.0 0.0 collective-permute-done.4.across
  22.0 0.0 collective-permute-done.5.inside
  22.1 0.0 copy-done.3
  22.1 0.0 copy-done.4
  22.1 1.9 %outer.1 = f32[5,128,512]{2,1,0:T(8,128)} custom-call(bf16[320,128]{1,0:T(8,128)(2,1)S(1)} %collective-permute-done.a, bf16[320,128]{1,0:T(8,128)(2,1)S(1)} %collective-permute-done.1.b, f32[320,128]{1,0:T(8,128)S(1)} %get-tuple-element.36.own, bf16[320,128]{1,0:T(8,128)(2,1)S(1)} %collective-permute-done.2.c.c2, ...), custom_call_target="tpu_custom_call" | custom-call | tf_op jit(solution)/shard_map/outer/pallas_call | solution.py:559
Async XLA Ops:
  3.2 0.9 %copy-start.1 = (f32[160,384]{1,0:T(8,128)S(1)}, f32[160,384]{1,0:T(8,128)}, u32[]{:S(2)}) copy-start(f32[160,384]{1,0:T(8,128)} %fold.1.both) | copy-start | bytes 737284
  4.1 8.5 %copy-start = (f32[128,5,512]{2,0,1:T(8,128)S(1)}, f32[128,5,512]{2,0,1:T(8,128)}, u32[]{:S(2)}) copy-start(f32[128,5,512]{2,0,1:T(8,128)} %param.15) | copy-start | bytes 3932164
  4.1 8.5 %copy-start.5 = (bf16[256,256]{1,0:T(8,128)(2,1)S(1)}, bf16[256,256]{1,0:T(8,128)(2,1)}, u32[]{:S(2)}) copy-start(bf16[256,256]{1,0:T(8,128)(2,1)} %constant.19.clone.refs_6_.wb1) | copy-start | bytes 393220
  4.1 8.5 %copy-start.6 = (bf16[256,256]{1,0:T(8,128)(2,1)S(1)}, bf16[256,256]{1,0:T(8,128)(2,1)}, u32[]{:S(2)}) copy-start(bf16[256,256]{1,0:T(8,128)(2,1)} %constant.17.clone.refs_4_.wf1) | copy-start | bytes 393220
  4.1 8.5 %copy-start.7 = (bf16[256,128]{1,0:T(8,128)(2,1)S(1)}, bf16[256,128]{1,0:T(8,128)(2,1)}, u32[]{:S(2)}) copy-start(bf16[256,128]{1,0:T(8,128)(2,1)} %constant.20.clone.refs_7_.wb2) | copy-start | bytes 196612
  4.1 8.5 %copy-start.8 = (bf16[128,256]{1,0:T(8,128)(2,1)S(1)}, bf16[128,256]{1,0:T(8,128)(2,1)}, u32[]{:S(2)}) copy-start(bf16[128,256]{1,0:T(8,128)(2,1)} %constant.18.clone.refs_5_.wf2) | copy-start | bytes 196612
  4.2 8.5 %copy-start.9 = (f32[128,3,512]{2,0,1:T(8,128)S(1)}, f32[128,3,512]{2,0,1:T(8,128)}, u32[]{:S(2)}) copy-start(f32[128,3,512]{2,0,1:T(8,128)} %param.16) | copy-start | bytes 2359300
  4.2 8.5 %copy-start.10 = (f32[128,3,512]{2,0,1:T(8,128)S(1)}, f32[128,3,512]{2,0,1:T(8,128)}, u32[]{:S(2)}) copy-start(f32[128,3,512]{2,0,1:T(8,128)} %param.17) | copy-start | bytes 2359300
  4.2 8.5 %copy-start.11 = (f32[48,128]{1,0:T(8,128)S(1)}, f32[48,128]{1,0:T(8,128)}, u32[]{:S(2)}) copy-start(f32[48,128]{1,0:T(8,128)} %constant.21.clone.refs_8_) | copy-start | bytes 73732
  4.5 10.6 %collective-permute-start = (bf16[320,128]{1,0:T(8,128)(2,1)S(1)}, bf16[320,128]{1,0:T(8,128)(2,1)S(1)}, u32[]{:S(2)}, u32[]{:S(2)}) collective-permute-start(bf16[320,128]{1,0:T(8,128)(2,1)S(1)} %get-tuple-element.27), channel_id=1, source_target_pairs={{0,4},{4,8},{8,12},{12,16},{16,20},{20,24},{24,28},{28,0},{1,5},{5... | collective-permute-start | bytes 245768 | tf_op jit(solution)/shard_map/ppermute | solution.py:586
  7.5 7.6 %collective-permute-start.1 = (bf16[320,128]{1,0:T(8,128)(2,1)S(1)}, bf16[320,128]{1,0:T(8,128)(2,1)S(1)}, u32[]{:S(2)}, u32[]{:S(2)}) collective-permute-start(bf16[320,128]{1,0:T(8,128)(2,1)S(1)} %get-tuple-element.28), channel_id=1, source_target_pairs={{0,8},{4,12},{8,16},{12,20},{16,24},{20,28},{24,0},{28,4},{1,9},{5... | collective-permute-start | bytes 245768 | tf_op jit(solution)/shard_map/ppermute | solution.py:586
  9.1 6.0 %collective-permute-start.2 = (bf16[320,128]{1,0:T(8,128)(2,1)S(1)}, bf16[320,128]{1,0:T(8,128)(2,1)S(1)}, u32[]{:S(2)}, u32[]{:S(2)}) collective-permute-start(bf16[320,128]{1,0:T(8,128)(2,1)S(1)} %get-tuple-element.30), channel_id=1, source_target_pairs={{0,24},{4,28},{8,0},{12,4},{16,8},{20,12},{24,16},{28,20},{1,25},{... | collective-permute-start | bytes 245768 | tf_op jit(solution)/shard_map/ppermute | solution.py:586
  11.3 4.4 %collective-permute-start.3 = (bf16[320,128]{1,0:T(8,128)(2,1)S(1)}, bf16[320,128]{1,0:T(8,128)(2,1)S(1)}, u32[]{:S(2)}, u32[]{:S(2)}) collective-permute-start(bf16[320,128]{1,0:T(8,128)(2,1)S(1)} %get-tuple-element.31), channel_id=1, source_target_pairs={{0,28},{4,0},{8,4},{12,8},{16,12},{20,16},{24,20},{28,24},{1,29},{... | collective-permute-start | bytes 245768 | tf_op jit(solution)/shard_map/ppermute | solution.py:586
  12.7 3.1 %copy-start.2 = (f32[160,384]{1,0:T(8,128)S(1)}, f32[160,384]{1,0:T(8,128)}, u32[]{:S(2)}) copy-start(f32[160,384]{1,0:T(8,128)} %fold.1.both) | copy-start | bytes 737284
  15.9 6.2 %copy-start.3 = (bf16[256,1024]{1,0:T(8,128)(2,1)S(1)}, bf16[256,1024]{1,0:T(8,128)(2,1)}, u32[]{:S(2)}) copy-start(bf16[256,1024]{1,0:T(8,128)(2,1)} %constant.23.clone.place) | copy-start | bytes 1572868
  15.9 6.2 %copy-start.4 = (bf16[256,1024]{1,0:T(8,128)(2,1)S(1)}, bf16[256,1024]{1,0:T(8,128)(2,1)}, u32[]{:S(2)}) copy-start(bf16[256,1024]{1,0:T(8,128)(2,1)} %constant.22.clone.spread) | copy-start | bytes 1572868
  15.9 6.1 %collective-permute-start.4 = (f32[8,128]{1,0:T(8,128)S(1)}, f32[8,128]{1,0:T(8,128)S(1)}, u32[]{:S(2)}, u32[]{:S(2)}) collective-permute-start(f32[8,128]{1,0:T(8,128)S(1)} %get-tuple-element.41), channel_id=1, source_target_pairs={{1,2},{2,1},{3,4},{4,3},{5,6},{6,5},{7,8},{8,7},{9,10},{10,9},{11,... | collective-permute-start | bytes 12296 | tf_op jit(solution)/shard_map/ppermute | solution.py:595
  16.7 5.4 %collective-permute-start.5 = (f32[8,128]{1,0:T(8,128)S(1)}, f32[8,128]{1,0:T(8,128)S(1)}, u32[]{:S(2)}, u32[]{:S(2)}) collective-permute-start(f32[8,128]{1,0:T(8,128)S(1)} %get-tuple-element.42), channel_id=1, source_target_pairs={{0,1},{1,0},{2,3},{3,2},{4,5},{5,4},{6,7},{7,6},{8,9},{9,8},{10,11... | collective-permute-start | bytes 12296 | tf_op jit(solution)/shard_map/ppermute | solution.py:596

commit v9 on v8

--- a/solution.py
+++ b/solution.py
@@ -216,8 +216,9 @@
     marked = down(jnp.where(hang == 1, code, -2)) - (lane // 64).astype(F32)
     odd = lane % 16 >= 8
     group = (lane // 16 + 1) % 4
+    for copy in copies[4:]:
+        copy.wait()
     for f in range(5):
-        copies[4 + f].wait()
         packed = jnp.zeros((E, 128), F32)
         for c in range(4):
             moved = x[f, :, 128 * c : 128 * c + 128]
@@ -229,7 +230,6 @@
         both = jnp.where(odd, high_f, pltpu.roll(packed - high_f, 8, 1)).astype(BF16)
         wide[E * f : E * f + E, 0:128] = both
         wide[E * f : E * f + E, 128:256] = high
-    copies[9].wait()
     mapped = dot(wide[...], fold[...])
     faces = []
     for f in range(5):
@@ -536,7 +536,7 @@
         for f in range(2 * n, min(2 * n + 2, 5)):
             cols = slice(512 * (f - 2 * n), 512 * (f - 2 * n) + 512)
             out[f] = (
-                (base_a[f] if f < 2 else base_b[f - 2])
+                (base_a[f] if f < 3 else base_b[f - 3])
                 + q_ref[...] * dot(y_parts[rows], spread[:, cols])
                 + dot(r_parts[rows], place[:, cols])
             )
@@ -584,7 +584,7 @@
     for n in (0, 1, 3, 4):
         pairs = [(i, (i + ORDER[n] - 2) % peers) for i in range(peers)]
         parts[n] = lax.ppermute(parts[n], "dom", pairs)
-    early, *factors = main_of(adjoint, met, vel, kept, tables, (0, 1), True)
+    early, *factors = main_of(adjoint, met, vel, kept, tables, (0, 1, 2), True)
     parts, early = lax.optimization_barrier((parts, early))
     lines = lines_of(parts, both)
     (out_a, out_b), kept = lax.optimization_barrier((lines, kept))
@@ -594,7 +594,7 @@
     across = [(i, i + 1 if i % 2 else i - 1) for i in range(1, count - 1)]
     outward = lax.ppermute(out_a, axes, across)
     inward = lax.ppermute(out_b, axes, inside)
-    (late,) = main_of(adjoint, met, vel, kept, tables, (2, 3, 4), False)
+    (late,) = main_of(adjoint, met, vel, kept, tables, (3, 4), False)
     result = post_of(parts, outward, inward, (early, late, *factors), tables)
     return jnp.transpose(result, (1, 0, 2))
 

time: 24.2 us -> 23.4 us (0.967)
  waiting for transfers between devices: 0.68 us -> 0.02 us
    ppermute x4, waiting for transfers between devices: 0.68 us -> 0.01 us  [shards(): parts[n] = lax.ppermute(parts[n], 'dom', pairs)]
  transfers between devices with their start and end apart: 6 -> 6, of which waited for: 1 -> 0; matrix products, arithmetic and copies ran while one was open for 0% -> 0% of each run, Pallas kernels for 20% -> 21%
where the time goes in v9:
time: 23.4 us; the launch traced here: 23.2 us
  starting transfers between devices  12 us (51%)
  Pallas kernels  10.1 us (43%)
  local copies, waits for them, and re-layouts  0.99 us (4%)
    ppermute x4, starting transfers between devices, shards(): parts[n] = lax.ppermute(parts[n], 'dom', pairs)  8.12 us
    pallas_call x2, Pallas kernels, main_of(): pl.pallas_call(body, out_shape=[jax.ShapeDtypeStruct(shape, F32) for shap...  4.77 us
    ppermute x1, starting transfers between devices, shards(): inward = lax.ppermute(out_b, axes, inside)  3.08 us
    pallas_call x1, Pallas kernels, folded_of(): pl.pallas_call(fold_kernel, out_shape=jax.ShapeDtypeStruct((E + 32, 384),...  2.93 us
    pallas_call x1, Pallas kernels, post_of(): pl.pallas_call(post_kernel, out_shape=jax.ShapeDtypeStruct((5, E, 512), F...  1.92 us
    unnamed x24, local copies, waits for them, and re-layouts  0.99 us
    ppermute x1, starting transfers between devices, shards(): outward = lax.ppermute(out_a, axes, across)  0.78 us
  transfers between devices with their start and end apart: 6, of which 0 were waited for; matrix products, arithmetic and copies ran while one was open for 0% of the time, Pallas kernels for 21%

profile of v9, /device:TPU:0, one launch (start us, length us, event | category | flops | bytes accessed | tf_op | source)
XLA Modules:
  0.0 23.2 jit_solution(8067554459824956812)
XLA Ops:
  0.0 2.9 %fold.1.both = f32[160,384]{1,0:T(8,128)} custom-call(s32[1,128]{1,0:T(1,128)} %bitcast.15, s32[1,128]{1,0:T(1,128)} %bitcast.16, s32[1,128]{1,0:T(1,128)} %bitcast.17, s32[1,128]{1,0:T(1,128)} %bitcast.18, f32[5,128,512]{2,1,0:T(8,128)} %bitcast.8, bf16[256,512]{1,0:T(8,128)(2,1)} %constant.16.clone.fold_hbm), custom_call_target="tpu_custom_call" | custom-call | tf_op jit(solution)/shard_map/fold/pallas_call | solution.py:266
  2.9 0.0 copy-start.1
  3.0 0.9 %copy-done.1 = f32[160,384]{1,0:T(8,128)S(1)} copy-done((f32[160,384]{1,0:T(8,128)S(1)}, f32[160,384]{1,0:T(8,128)}, u32[]{:S(2)}) %copy-start.1) | copy-done | bytes 245784
  3.9 0.0 copy-start
  3.9 0.0 copy-start.5
  3.9 0.0 copy-start.6
  3.9 0.0 copy-start.7
  3.9 0.0 copy-start.8
  3.9 0.0 copy-start.9
  3.9 0.0 copy-start.10
  3.9 0.0 copy-start.11
  3.9 0.3 %sums.1 = (bf16[320,128]{1,0:T(8,128)(2,1)S(1)}, bf16[320,128]{1,0:T(8,128)(2,1)S(1)}, f32[320,128]{1,0:T(8,128)S(1)}, bf16[320,128]{1,0:T(8,128)(2,1)S(1)}, bf1...) custom-call(f32[160,384]{1,0:T(8,128)S(1)} %copy-done.1), custom_call_target="tpu_custom_call" | custom-call | flops 8000000000 | bytes 30000000 | tf_op jit(solution)/shard_map/sums/pallas_call | solution.py:406
  4.2 3.0 %collective-permute-start = (bf16[320,128]{1,0:T(8,128)(2,1)S(1)}, bf16[320,128]{1,0:T(8,128)(2,1)S(1)}, u32[]{:S(2)}, u32[]{:S(2)}) collective-permute-start(bf16[320,128]{1,0:T(8,128)(2,1)S(1)} %get-tuple-element.27), channel_id=1, source_target_pairs={{0,4},{4,8},{8,12},{12,16},{16,20},{20,24},{24,28},{28,0},{1,5},{5... | collective-permute-start | bytes 245768 | tf_op jit(solution)/shard_map/ppermute | solution.py:586
  7.2 1.6 %collective-permute-start.1 = (bf16[320,128]{1,0:T(8,128)(2,1)S(1)}, bf16[320,128]{1,0:T(8,128)(2,1)S(1)}, u32[]{:S(2)}, u32[]{:S(2)}) collective-permute-start(bf16[320,128]{1,0:T(8,128)(2,1)S(1)} %get-tuple-element.28), channel_id=1, source_target_pairs={{0,8},{4,12},{8,16},{12,20},{16,24},{20,28},{24,0},{28,4},{1,9},{5... | collective-permute-start | bytes 245768 | tf_op jit(solution)/shard_map/ppermute | solution.py:586
  8.8 2.2 %collective-permute-start.2 = (bf16[320,128]{1,0:T(8,128)(2,1)S(1)}, bf16[320,128]{1,0:T(8,128)(2,1)S(1)}, u32[]{:S(2)}, u32[]{:S(2)}) collective-permute-start(bf16[320,128]{1,0:T(8,128)(2,1)S(1)} %get-tuple-element.30), channel_id=1, source_target_pairs={{0,24},{4,28},{8,0},{12,4},{16,8},{20,12},{24,16},{28,20},{1,25},{... | collective-permute-start | bytes 245768 | tf_op jit(solution)/shard_map/ppermute | solution.py:586
  11.1 1.3 %collective-permute-start.3 = (bf16[320,128]{1,0:T(8,128)(2,1)S(1)}, bf16[320,128]{1,0:T(8,128)(2,1)S(1)}, u32[]{:S(2)}, u32[]{:S(2)}) collective-permute-start(bf16[320,128]{1,0:T(8,128)(2,1)S(1)} %get-tuple-element.31), channel_id=1, source_target_pairs={{0,28},{4,0},{8,4},{12,8},{16,12},{20,16},{24,20},{28,24},{1,29},{... | collective-permute-start | bytes 245768 | tf_op jit(solution)/shard_map/ppermute | solution.py:586
  12.4 0.0 copy-done
  12.4 0.0 copy-done.5
  12.4 0.0 copy-done.6
  12.4 0.0 copy-done.7
  12.4 0.0 copy-done.8
  12.4 0.0 copy-done.9
  12.4 0.0 copy-done.10
  12.4 0.0 copy-done.11
  12.4 0.0 copy-start.2
  12.4 3.2 %inner.2 = (f32[3,128,512]{2,1,0:T(8,128)S(1)}, f32[128,512]{1,0:T(8,128)S(1)}, f32[4,128,128]{2,1,0:T(8,128)S(1)}, f32[2,4,8,128]{3,2,1,0:T(8,128)S(1)}, f32[2,4,8,128]{3,2,1,0:T(8,128)S(1)}) custom-call(f32[5,128,512]{2,1,0:T(8,128)S(1)} %bitcast.9, f32[3,128,512]{2,1,0:T(8,128)S(1)} %bitcast.11, f32[3,128,512]{2,1,0:T(8,128)S(1)} %bitcast.13, ...), custom_call_target="tpu_custom_call" | custom-call | flops 2400000000 | bytes 5000000 | tf_op jit(solution)/shard_map/inner/pallas_call | solution.py:426
  15.6 0.0 collective-permute-done.a
  15.6 0.0 collective-permute-done.1.b
  15.6 0.0 collective-permute-done.2.c.c2
  15.6 0.0 collective-permute-done.3.d
  15.6 0.0 copy-done.2
  15.7 0.1 lines.1
  15.8 0.0 copy-start.3
  15.8 0.0 copy-start.4
  15.8 0.8 %collective-permute-start.4 = (f32[8,128]{1,0:T(8,128)S(1)}, f32[8,128]{1,0:T(8,128)S(1)}, u32[]{:S(2)}, u32[]{:S(2)}) collective-permute-start(f32[8,128]{1,0:T(8,128)S(1)} %get-tuple-element.41), channel_id=1, source_target_pairs={{1,2},{2,1},{3,4},{4,3},{5,6},{6,5},{7,8},{8,7},{9,10},{10,9},{11,... | collective-permute-start | bytes 12296 | tf_op jit(solution)/shard_map/ppermute | solution.py:595
  16.6 3.1 %collective-permute-start.5 = (f32[8,128]{1,0:T(8,128)S(1)}, f32[8,128]{1,0:T(8,128)S(1)}, u32[]{:S(2)}, u32[]{:S(2)}) collective-permute-start(f32[8,128]{1,0:T(8,128)S(1)} %get-tuple-element.42), channel_id=1, source_target_pairs={{0,1},{1,0},{2,3},{3,2},{4,5},{5,4},{6,7},{7,6},{8,9},{9,8},{10,11... | collective-permute-start | bytes 12296 | tf_op jit(solution)/shard_map/ppermute | solution.py:596
  19.7 1.6 %inner.3.base_b = f32[2,128,512]{2,1,0:T(8,128)S(1)} custom-call(f32[5,128,512]{2,1,0:T(8,128)S(1)} %bitcast.10, f32[3,128,512]{2,1,0:T(8,128)S(1)} %bitcast.12, f32[3,128,512]{2,1,0:T(8,128)S(1)} %bitcast.14, f32[128,128]{1,0:T(8,128)S(1)} %get-tuple-element.44.refs_3_, bf16[256,256]{1,0:T(8,128)(2,1)S(1)} %copy-done.6, bf16[128,256]{1,0:T(8,128)(2,1)S(1)} %copy-done.8, ...), custom_call_target="tpu_custom_call" | custom-call | flops 1600000000 | bytes 5000000 | tf_op jit(solution)/shard_map/inner/pallas_call | solution.py:426
  21.3 0.0 collective-permute-done.4.across
  21.3 0.0 collective-permute-done.5.inside
  21.3 0.0 copy-done.3
  21.3 0.0 copy-done.4
  21.3 1.9 %outer.1 = f32[5,128,512]{2,1,0:T(8,128)} custom-call(bf16[320,128]{1,0:T(8,128)(2,1)S(1)} %collective-permute-done.a, bf16[320,128]{1,0:T(8,128)(2,1)S(1)} %collective-permute-done.1.b, f32[320,128]{1,0:T(8,128)S(1)} %get-tuple-element.36.own, bf16[320,128]{1,0:T(8,128)(2,1)S(1)} %collective-permute-done.2.c.c2, ...), custom_call_target="tpu_custom_call" | custom-call | tf_op jit(solution)/shard_map/outer/pallas_call | solution.py:559
Async XLA Ops:
  2.9 0.9 %copy-start.1 = (f32[160,384]{1,0:T(8,128)S(1)}, f32[160,384]{1,0:T(8,128)}, u32[]{:S(2)}) copy-start(f32[160,384]{1,0:T(8,128)} %fold.1.both) | copy-start | bytes 737284
  3.9 8.5 %copy-start = (f32[128,5,512]{2,0,1:T(8,128)S(1)}, f32[128,5,512]{2,0,1:T(8,128)}, u32[]{:S(2)}) copy-start(f32[128,5,512]{2,0,1:T(8,128)} %param.15) | copy-start | bytes 3932164
  3.9 8.5 %copy-start.5 = (bf16[256,256]{1,0:T(8,128)(2,1)S(1)}, bf16[256,256]{1,0:T(8,128)(2,1)}, u32[]{:S(2)}) copy-start(bf16[256,256]{1,0:T(8,128)(2,1)} %constant.19.clone.refs_6_.wb1) | copy-start | bytes 393220
  3.9 8.5 %copy-start.6 = (bf16[256,256]{1,0:T(8,128)(2,1)S(1)}, bf16[256,256]{1,0:T(8,128)(2,1)}, u32[]{:S(2)}) copy-start(bf16[256,256]{1,0:T(8,128)(2,1)} %constant.17.clone.refs_4_.wf1) | copy-start | bytes 393220
  3.9 8.5 %copy-start.7 = (bf16[256,128]{1,0:T(8,128)(2,1)S(1)}, bf16[256,128]{1,0:T(8,128)(2,1)}, u32[]{:S(2)}) copy-start(bf16[256,128]{1,0:T(8,128)(2,1)} %constant.20.clone.refs_7_.wb2) | copy-start | bytes 196612
  3.9 8.5 %copy-start.8 = (bf16[128,256]{1,0:T(8,128)(2,1)S(1)}, bf16[128,256]{1,0:T(8,128)(2,1)}, u32[]{:S(2)}) copy-start(bf16[128,256]{1,0:T(8,128)(2,1)} %constant.18.clone.refs_5_.wf2) | copy-start | bytes 196612
  3.9 8.5 %copy-start.9 = (f32[128,3,512]{2,0,1:T(8,128)S(1)}, f32[128,3,512]{2,0,1:T(8,128)}, u32[]{:S(2)}) copy-start(f32[128,3,512]{2,0,1:T(8,128)} %param.16) | copy-start | bytes 2359300
  3.9 8.5 %copy-start.10 = (f32[128,3,512]{2,0,1:T(8,128)S(1)}, f32[128,3,512]{2,0,1:T(8,128)}, u32[]{:S(2)}) copy-start(f32[128,3,512]{2,0,1:T(8,128)} %param.17) | copy-start | bytes 2359300
  3.9 8.5 %copy-start.11 = (f32[48,128]{1,0:T(8,128)S(1)}, f32[48,128]{1,0:T(8,128)}, u32[]{:S(2)}) copy-start(f32[48,128]{1,0:T(8,128)} %constant.21.clone.refs_8_) | copy-start | bytes 73732
  4.2 11.4 %collective-permute-start = (bf16[320,128]{1,0:T(8,128)(2,1)S(1)}, bf16[320,128]{1,0:T(8,128)(2,1)S(1)}, u32[]{:S(2)}, u32[]{:S(2)}) collective-permute-start(bf16[320,128]{1,0:T(8,128)(2,1)S(1)} %get-tuple-element.27), channel_id=1, source_target_pairs={{0,4},{4,8},{8,12},{12,16},{16,20},{20,24},{24,28},{28,0},{1,5},{5... | collective-permute-start | bytes 245768 | tf_op jit(solution)/shard_map/ppermute | solution.py:586
  7.2 8.4 %collective-permute-start.1 = (bf16[320,128]{1,0:T(8,128)(2,1)S(1)}, bf16[320,128]{1,0:T(8,128)(2,1)S(1)}, u32[]{:S(2)}, u32[]{:S(2)}) collective-permute-start(bf16[320,128]{1,0:T(8,128)(2,1)S(1)} %get-tuple-element.28), channel_id=1, source_target_pairs={{0,8},{4,12},{8,16},{12,20},{16,24},{20,28},{24,0},{28,4},{1,9},{5... | collective-permute-start | bytes 245768 | tf_op jit(solution)/shard_map/ppermute | solution.py:586
  8.8 6.8 %collective-permute-start.2 = (bf16[320,128]{1,0:T(8,128)(2,1)S(1)}, bf16[320,128]{1,0:T(8,128)(2,1)S(1)}, u32[]{:S(2)}, u32[]{:S(2)}) collective-permute-start(bf16[320,128]{1,0:T(8,128)(2,1)S(1)} %get-tuple-element.30), channel_id=1, source_target_pairs={{0,24},{4,28},{8,0},{12,4},{16,8},{20,12},{24,16},{28,20},{1,25},{... | collective-permute-start | bytes 245768 | tf_op jit(solution)/shard_map/ppermute | solution.py:586
  11.1 4.6 %collective-permute-start.3 = (bf16[320,128]{1,0:T(8,128)(2,1)S(1)}, bf16[320,128]{1,0:T(8,128)(2,1)S(1)}, u32[]{:S(2)}, u32[]{:S(2)}) collective-permute-start(bf16[320,128]{1,0:T(8,128)(2,1)S(1)} %get-tuple-element.31), channel_id=1, source_target_pairs={{0,28},{4,0},{8,4},{12,8},{16,12},{20,16},{24,20},{28,24},{1,29},{... | collective-permute-start | bytes 245768 | tf_op jit(solution)/shard_map/ppermute | solution.py:586
  12.4 3.2 %copy-start.2 = (f32[160,384]{1,0:T(8,128)S(1)}, f32[160,384]{1,0:T(8,128)}, u32[]{:S(2)}) copy-start(f32[160,384]{1,0:T(8,128)} %fold.1.both) | copy-start | bytes 737284
  15.8 5.5 %copy-start.3 = (bf16[256,1024]{1,0:T(8,128)(2,1)S(1)}, bf16[256,1024]{1,0:T(8,128)(2,1)}, u32[]{:S(2)}) copy-start(bf16[256,1024]{1,0:T(8,128)(2,1)} %constant.23.clone.place) | copy-start | bytes 1572868
  15.8 5.5 %copy-start.4 = (bf16[256,1024]{1,0:T(8,128)(2,1)S(1)}, bf16[256,1024]{1,0:T(8,128)(2,1)}, u32[]{:S(2)}) copy-start(bf16[256,1024]{1,0:T(8,128)(2,1)} %constant.22.clone.spread) | copy-start | bytes 1572868
  15.8 5.5 %collective-permute-start.4 = (f32[8,128]{1,0:T(8,128)S(1)}, f32[8,128]{1,0:T(8,128)S(1)}, u32[]{:S(2)}, u32[]{:S(2)}) collective-permute-start(f32[8,128]{1,0:T(8,128)S(1)} %get-tuple-element.41), channel_id=1, source_target_pairs={{1,2},{2,1},{3,4},{4,3},{5,6},{6,5},{7,8},{8,7},{9,10},{10,9},{11,... | collective-permute-start | bytes 12296 | tf_op jit(solution)/shard_map/ppermute | solution.py:595
  16.6 4.7 %collective-permute-start.5 = (f32[8,128]{1,0:T(8,128)S(1)}, f32[8,128]{1,0:T(8,128)S(1)}, u32[]{:S(2)}, u32[]{:S(2)}) collective-permute-start(f32[8,128]{1,0:T(8,128)S(1)} %get-tuple-element.42), channel_id=1, source_target_pairs={{0,1},{1,0},{2,3},{3,2},{4,5},{5,4},{6,7},{7,6},{8,9},{9,8},{10,11... | collective-permute-start | bytes 12296 | tf_op jit(solution)/shard_map/ppermute | solution.py:596

commit v10 on v9

--- a/solution.py
+++ b/solution.py
@@ -361,18 +361,24 @@
     if factors:
         factors_of(met, vel, wb1, wb2, coef, *factors)
 
-    def field(n, carry):
-        f = n + fields[0]
+    xs = []
+    for f in fields:
         x = [x_ref[f, :, 128 * c : 128 * c + 128] * keep for c in range(4)]
         low_faces = pltpu.roll(swap(x[0]), E - 1, 0)
         high_faces = pltpu.roll(swap(x[3]), 1, 0)
         x[0] = x[0] + jnp.where(left & (row > 0), high_faces, 0.0)
         x[3] = x[3] + jnp.where(left | (row == E - 1), 0.0, low_faces)
-        stacked = jnp.concatenate(x, 0)
-        rest = two_dims(
-            stacked, chunks_of(met, 1), chunks_of(met, 2), chunks_of(vel, 1), chunks_of(vel, 2),
-            wf1, wf2, wb1, wb2,
-        )
+        xs.append(x)
+    count = len(fields)
+    rest = two_dims(
+        jnp.concatenate(sum(xs, []), 0),
+        jnp.concatenate([chunks_of(met, 1)] * count, 0),
+        jnp.concatenate([chunks_of(met, 2)] * count, 0),
+        jnp.concatenate([chunks_of(vel, 1)] * count, 0),
+        jnp.concatenate([chunks_of(vel, 2)] * count, 0),
+        wf1, wf2, wb1, wb2,
+    )
+    for n, x in enumerate(xs):
         g0 = along_first(x, coef, 0)
         inner0 = []
         for c in range(4):
@@ -380,10 +386,8 @@
             inner0.append(met[0, :, at] * g0[c] + vel[0, :, at] * x[c])
         back = along_first(inner0, coef, 16)
         for c in range(4):
-            out[n, :, 128 * c : 128 * c + 128] = rest[E * c : E * c + E] + back[c]
-        return carry
-
-    lax.fori_loop(0, len(fields), field, 0)
+            start = E * (4 * n + c)
+            out[n, :, 128 * c : 128 * c + 128] = rest[start : start + E] + back[c]
 
 
 def sum_kernel(both, *outs):

time: 23.4 us -> 23.2 us (level)
  Pallas kernels: 10.1 us -> 9.71 us
    pallas_call x2, Pallas kernels: 4.77 us -> 4.43 us  [main_of(): pl.pallas_call(body, out_shape=[jax.ShapeDtypeStruct(shape, F32) for shap...]
  transfers between devices with their start and end apart: 6 -> 6, of which waited for: 0 -> 1; matrix products, arithmetic and copies ran while one was open for 0% -> 0% of each run, Pallas kernels for 21% -> 19%
where the time goes in v10:
time: 23.2 us; the launch traced here: 22.9 us
  starting transfers between devices  11.9 us (51%)
  Pallas kernels  9.71 us (42%)
  local copies, waits for them, and re-layouts  0.99 us (4%)
    ppermute x4, starting transfers between devices, shards(): parts[n] = lax.ppermute(parts[n], 'dom', pairs)  8.12 us
    pallas_call x2, Pallas kernels, main_of(): pl.pallas_call(body, out_shape=[jax.ShapeDtypeStruct(shape, F32) for shap...  4.43 us
    ppermute x1, starting transfers between devices, shards(): inward = lax.ppermute(out_b, axes, inside)  3.02 us
    pallas_call x1, Pallas kernels, folded_of(): pl.pallas_call(fold_kernel, out_shape=jax.ShapeDtypeStruct((E + 32, 384),...  2.93 us
    pallas_call x1, Pallas kernels, post_of(): pl.pallas_call(post_kernel, out_shape=jax.ShapeDtypeStruct((5, E, 512), F...  1.92 us
    unnamed x24, local copies, waits for them, and re-layouts  0.99 us
    ppermute x1, starting transfers between devices, shards(): outward = lax.ppermute(out_a, axes, across)  0.78 us
  transfers between devices with their start and end apart: 6, of which 1 were waited for; matrix products, arithmetic and copies ran while one was open for 0% of the time, Pallas kernels for 19%

profile of v10, /device:TPU:0, one launch (start us, length us, event | category | flops | bytes accessed | tf_op | source)
XLA Modules:
  0.0 22.9 jit_solution(5689254354813249029)
XLA Ops:
  0.0 2.9 %fold.1.both = f32[160,384]{1,0:T(8,128)} custom-call(s32[1,128]{1,0:T(1,128)} %bitcast.15, s32[1,128]{1,0:T(1,128)} %bitcast.16, s32[1,128]{1,0:T(1,128)} %bitcast.17, s32[1,128]{1,0:T(1,128)} %bitcast.18, f32[5,128,512]{2,1,0:T(8,128)} %bitcast.8, bf16[256,512]{1,0:T(8,128)(2,1)} %constant.16.clone.fold_hbm), custom_call_target="tpu_custom_call" | custom-call | tf_op jit(solution)/shard_map/fold/pallas_call | solution.py:266
  2.9 0.0 copy-start.1
  3.0 0.9 %copy-done.1 = f32[160,384]{1,0:T(8,128)S(1)} copy-done((f32[160,384]{1,0:T(8,128)S(1)}, f32[160,384]{1,0:T(8,128)}, u32[]{:S(2)}) %copy-start.1) | copy-done | bytes 245784
  3.9 0.0 copy-start
  3.9 0.0 copy-start.5
  3.9 0.0 copy-start.6
  3.9 0.0 copy-start.7
  3.9 0.0 copy-start.8
  3.9 0.0 copy-start.9
  3.9 0.0 copy-start.10
  3.9 0.0 copy-start.11
  3.9 0.3 %sums.1 = (bf16[320,128]{1,0:T(8,128)(2,1)S(1)}, bf16[320,128]{1,0:T(8,128)(2,1)S(1)}, f32[320,128]{1,0:T(8,128)S(1)}, bf16[320,128]{1,0:T(8,128)(2,1)S(1)}, bf1...) custom-call(f32[160,384]{1,0:T(8,128)S(1)} %copy-done.1), custom_call_target="tpu_custom_call" | custom-call | flops 8000000000 | bytes 30000000 | tf_op jit(solution)/shard_map/sums/pallas_call | solution.py:410
  4.2 3.0 %collective-permute-start = (bf16[320,128]{1,0:T(8,128)(2,1)S(1)}, bf16[320,128]{1,0:T(8,128)(2,1)S(1)}, u32[]{:S(2)}, u32[]{:S(2)}) collective-permute-start(bf16[320,128]{1,0:T(8,128)(2,1)S(1)} %get-tuple-element.27), channel_id=1, source_target_pairs={{0,4},{4,8},{8,12},{12,16},{16,20},{20,24},{24,28},{28,0},{1,5},{5... | collective-permute-start | bytes 245768 | tf_op jit(solution)/shard_map/ppermute | solution.py:590
  7.2 1.6 %collective-permute-start.1 = (bf16[320,128]{1,0:T(8,128)(2,1)S(1)}, bf16[320,128]{1,0:T(8,128)(2,1)S(1)}, u32[]{:S(2)}, u32[]{:S(2)}) collective-permute-start(bf16[320,128]{1,0:T(8,128)(2,1)S(1)} %get-tuple-element.28), channel_id=1, source_target_pairs={{0,8},{4,12},{8,16},{12,20},{16,24},{20,28},{24,0},{28,4},{1,9},{5... | collective-permute-start | bytes 245768 | tf_op jit(solution)/shard_map/ppermute | solution.py:590
  8.8 2.2 %collective-permute-start.2 = (bf16[320,128]{1,0:T(8,128)(2,1)S(1)}, bf16[320,128]{1,0:T(8,128)(2,1)S(1)}, u32[]{:S(2)}, u32[]{:S(2)}) collective-permute-start(bf16[320,128]{1,0:T(8,128)(2,1)S(1)} %get-tuple-element.30), channel_id=1, source_target_pairs={{0,24},{4,28},{8,0},{12,4},{16,8},{20,12},{24,16},{28,20},{1,25},{... | collective-permute-start | bytes 245768 | tf_op jit(solution)/shard_map/ppermute | solution.py:590
  11.1 1.3 %collective-permute-start.3 = (bf16[320,128]{1,0:T(8,128)(2,1)S(1)}, bf16[320,128]{1,0:T(8,128)(2,1)S(1)}, u32[]{:S(2)}, u32[]{:S(2)}) collective-permute-start(bf16[320,128]{1,0:T(8,128)(2,1)S(1)} %get-tuple-element.31), channel_id=1, source_target_pairs={{0,28},{4,0},{8,4},{12,8},{16,12},{20,16},{24,20},{28,24},{1,29},{... | collective-permute-start | bytes 245768 | tf_op jit(solution)/shard_map/ppermute | solution.py:590
  12.4 0.0 copy-done
  12.4 0.0 copy-done.5
  12.4 0.0 copy-done.6
  12.4 0.0 copy-done.7
  12.4 0.0 copy-done.8
  12.4 0.0 copy-done.9
  12.4 0.0 copy-done.10
  12.4 0.0 copy-done.11
  12.4 0.0 copy-start.2
  12.4 3.0 %inner.2 = (f32[3,128,512]{2,1,0:T(8,128)S(1)}, f32[128,512]{1,0:T(8,128)S(1)}, f32[4,128,128]{2,1,0:T(8,128)S(1)}, f32[2,4,8,128]{3,2,1,0:T(8,128)S(1)}, f32[2,4,8,128]{3,2,1,0:T(8,128)S(1)}) custom-call(f32[5,128,512]{2,1,0:T(8,128)S(1)} %bitcast.9, f32[3,128,512]{2,1,0:T(8,128)S(1)} %bitcast.11, f32[3,128,512]{2,1,0:T(8,128)S(1)} %bitcast.13, ...), custom_call_target="tpu_custom_call" | custom-call | flops 2400000000 | bytes 5000000 | tf_op jit(solution)/shard_map/inner/pallas_call | solution.py:430
  15.4 0.0 collective-permute-done.a
  15.4 0.0 collective-permute-done.1.b
  15.4 0.0 collective-permute-done.2.c.c2
  15.4 0.1 collective-permute-done.3.d
  15.5 0.0 copy-done.2
  15.5 0.1 lines.1
  15.6 0.0 copy-start.3
  15.6 0.0 copy-start.4
  15.6 0.8 %collective-permute-start.4 = (f32[8,128]{1,0:T(8,128)S(1)}, f32[8,128]{1,0:T(8,128)S(1)}, u32[]{:S(2)}, u32[]{:S(2)}) collective-permute-start(f32[8,128]{1,0:T(8,128)S(1)} %get-tuple-element.41), channel_id=1, source_target_pairs={{1,2},{2,1},{3,4},{4,3},{5,6},{6,5},{7,8},{8,7},{9,10},{10,9},{11,... | collective-permute-start | bytes 12296 | tf_op jit(solution)/shard_map/ppermute | solution.py:599
  16.4 3.0 %collective-permute-start.5 = (f32[8,128]{1,0:T(8,128)S(1)}, f32[8,128]{1,0:T(8,128)S(1)}, u32[]{:S(2)}, u32[]{:S(2)}) collective-permute-start(f32[8,128]{1,0:T(8,128)S(1)} %get-tuple-element.42), channel_id=1, source_target_pairs={{0,1},{1,0},{2,3},{3,2},{4,5},{5,4},{6,7},{7,6},{8,9},{9,8},{10,11... | collective-permute-start | bytes 12296 | tf_op jit(solution)/shard_map/ppermute | solution.py:600
  19.5 1.5 %inner.3.base_b = f32[2,128,512]{2,1,0:T(8,128)S(1)} custom-call(f32[5,128,512]{2,1,0:T(8,128)S(1)} %bitcast.10, f32[3,128,512]{2,1,0:T(8,128)S(1)} %bitcast.12, f32[3,128,512]{2,1,0:T(8,128)S(1)} %bitcast.14, f32[128,128]{1,0:T(8,128)S(1)} %get-tuple-element.44.refs_3_, bf16[256,256]{1,0:T(8,128)(2,1)S(1)} %copy-done.6, bf16[128,256]{1,0:T(8,128)(2,1)S(1)} %copy-done.8, ...), custom_call_target="tpu_custom_call" | custom-call | flops 1600000000 | bytes 5000000 | tf_op jit(solution)/shard_map/inner/pallas_call | solution.py:430
  20.9 0.0 collective-permute-done.4.across
  20.9 0.0 collective-permute-done.5.inside
  21.0 0.0 copy-done.3
  21.0 0.0 copy-done.4
  21.0 1.9 %outer.1 = f32[5,128,512]{2,1,0:T(8,128)} custom-call(bf16[320,128]{1,0:T(8,128)(2,1)S(1)} %collective-permute-done.a, bf16[320,128]{1,0:T(8,128)(2,1)S(1)} %collective-permute-done.1.b, f32[320,128]{1,0:T(8,128)S(1)} %get-tuple-element.36.own, bf16[320,128]{1,0:T(8,128)(2,1)S(1)} %collective-permute-done.2.c.c2, ...), custom_call_target="tpu_custom_call" | custom-call | tf_op jit(solution)/shard_map/outer/pallas_call | solution.py:563
Async XLA Ops:
  2.9 0.9 %copy-start.1 = (f32[160,384]{1,0:T(8,128)S(1)}, f32[160,384]{1,0:T(8,128)}, u32[]{:S(2)}) copy-start(f32[160,384]{1,0:T(8,128)} %fold.1.both) | copy-start | bytes 737284
  3.9 8.5 %copy-start = (f32[128,5,512]{2,0,1:T(8,128)S(1)}, f32[128,5,512]{2,0,1:T(8,128)}, u32[]{:S(2)}) copy-start(f32[128,5,512]{2,0,1:T(8,128)} %param.15) | copy-start | bytes 3932164
  3.9 8.5 %copy-start.5 = (bf16[256,256]{1,0:T(8,128)(2,1)S(1)}, bf16[256,256]{1,0:T(8,128)(2,1)}, u32[]{:S(2)}) copy-start(bf16[256,256]{1,0:T(8,128)(2,1)} %constant.19.clone.refs_6_.wb1) | copy-start | bytes 393220
  3.9 8.5 %copy-start.6 = (bf16[256,256]{1,0:T(8,128)(2,1)S(1)}, bf16[256,256]{1,0:T(8,128)(2,1)}, u32[]{:S(2)}) copy-start(bf16[256,256]{1,0:T(8,128)(2,1)} %constant.17.clone.refs_4_.wf1) | copy-start | bytes 393220
  3.9 8.5 %copy-start.7 = (bf16[256,128]{1,0:T(8,128)(2,1)S(1)}, bf16[256,128]{1,0:T(8,128)(2,1)}, u32[]{:S(2)}) copy-start(bf16[256,128]{1,0:T(8,128)(2,1)} %constant.20.clone.refs_7_.wb2) | copy-start | bytes 196612
  3.9 8.5 %copy-start.8 = (bf16[128,256]{1,0:T(8,128)(2,1)S(1)}, bf16[128,256]{1,0:T(8,128)(2,1)}, u32[]{:S(2)}) copy-start(bf16[128,256]{1,0:T(8,128)(2,1)} %constant.18.clone.refs_5_.wf2) | copy-start | bytes 196612
  3.9 8.5 %copy-start.9 = (f32[128,3,512]{2,0,1:T(8,128)S(1)}, f32[128,3,512]{2,0,1:T(8,128)}, u32[]{:S(2)}) copy-start(f32[128,3,512]{2,0,1:T(8,128)} %param.16) | copy-start | bytes 2359300
  3.9 8.5 %copy-start.10 = (f32[128,3,512]{2,0,1:T(8,128)S(1)}, f32[128,3,512]{2,0,1:T(8,128)}, u32[]{:S(2)}) copy-start(f32[128,3,512]{2,0,1:T(8,128)} %param.17) | copy-start | bytes 2359300
  3.9 8.5 %copy-start.11 = (f32[48,128]{1,0:T(8,128)S(1)}, f32[48,128]{1,0:T(8,128)}, u32[]{:S(2)}) copy-start(f32[48,128]{1,0:T(8,128)} %constant.21.clone.refs_8_) | copy-start | bytes 73732
  4.2 11.2 %collective-permute-start = (bf16[320,128]{1,0:T(8,128)(2,1)S(1)}, bf16[320,128]{1,0:T(8,128)(2,1)S(1)}, u32[]{:S(2)}, u32[]{:S(2)}) collective-permute-start(bf16[320,128]{1,0:T(8,128)(2,1)S(1)} %get-tuple-element.27), channel_id=1, source_target_pairs={{0,4},{4,8},{8,12},{12,16},{16,20},{20,24},{24,28},{28,0},{1,5},{5... | collective-permute-start | bytes 245768 | tf_op jit(solution)/shard_map/ppermute | solution.py:590
  7.2 8.2 %collective-permute-start.1 = (bf16[320,128]{1,0:T(8,128)(2,1)S(1)}, bf16[320,128]{1,0:T(8,128)(2,1)S(1)}, u32[]{:S(2)}, u32[]{:S(2)}) collective-permute-start(bf16[320,128]{1,0:T(8,128)(2,1)S(1)} %get-tuple-element.28), channel_id=1, source_target_pairs={{0,8},{4,12},{8,16},{12,20},{16,24},{20,28},{24,0},{28,4},{1,9},{5... | collective-permute-start | bytes 245768 | tf_op jit(solution)/shard_map/ppermute | solution.py:590
  8.8 6.6 %collective-permute-start.2 = (bf16[320,128]{1,0:T(8,128)(2,1)S(1)}, bf16[320,128]{1,0:T(8,128)(2,1)S(1)}, u32[]{:S(2)}, u32[]{:S(2)}) collective-permute-start(bf16[320,128]{1,0:T(8,128)(2,1)S(1)} %get-tuple-element.30), channel_id=1, source_target_pairs={{0,24},{4,28},{8,0},{12,4},{16,8},{20,12},{24,16},{28,20},{1,25},{... | collective-permute-start | bytes 245768 | tf_op jit(solution)/shard_map/ppermute | solution.py:590
  11.1 4.4 %collective-permute-start.3 = (bf16[320,128]{1,0:T(8,128)(2,1)S(1)}, bf16[320,128]{1,0:T(8,128)(2,1)S(1)}, u32[]{:S(2)}, u32[]{:S(2)}) collective-permute-start(bf16[320,128]{1,0:T(8,128)(2,1)S(1)} %get-tuple-element.31), channel_id=1, source_target_pairs={{0,28},{4,0},{8,4},{12,8},{16,12},{20,16},{24,20},{28,24},{1,29},{... | collective-permute-start | bytes 245768 | tf_op jit(solution)/shard_map/ppermute | solution.py:590
  12.4 3.1 %copy-start.2 = (f32[160,384]{1,0:T(8,128)S(1)}, f32[160,384]{1,0:T(8,128)}, u32[]{:S(2)}) copy-start(f32[160,384]{1,0:T(8,128)} %fold.1.both) | copy-start | bytes 737284
  15.6 5.3 %copy-start.3 = (bf16[256,1024]{1,0:T(8,128)(2,1)S(1)}, bf16[256,1024]{1,0:T(8,128)(2,1)}, u32[]{:S(2)}) copy-start(bf16[256,1024]{1,0:T(8,128)(2,1)} %constant.23.clone.place) | copy-start | bytes 1572868
  15.6 5.3 %copy-start.4 = (bf16[256,1024]{1,0:T(8,128)(2,1)S(1)}, bf16[256,1024]{1,0:T(8,128)(2,1)}, u32[]{:S(2)}) copy-start(bf16[256,1024]{1,0:T(8,128)(2,1)} %constant.22.clone.spread) | copy-start | bytes 1572868
  15.6 5.3 %collective-permute-start.4 = (f32[8,128]{1,0:T(8,128)S(1)}, f32[8,128]{1,0:T(8,128)S(1)}, u32[]{:S(2)}, u32[]{:S(2)}) collective-permute-start(f32[8,128]{1,0:T(8,128)S(1)} %get-tuple-element.41), channel_id=1, source_target_pairs={{1,2},{2,1},{3,4},{4,3},{5,6},{6,5},{7,8},{8,7},{9,10},{10,9},{11,... | collective-permute-start | bytes 12296 | tf_op jit(solution)/shard_map/ppermute | solution.py:599
  16.4 4.5 %collective-permute-start.5 = (f32[8,128]{1,0:T(8,128)S(1)}, f32[8,128]{1,0:T(8,128)S(1)}, u32[]{:S(2)}, u32[]{:S(2)}) collective-permute-start(f32[8,128]{1,0:T(8,128)S(1)} %get-tuple-element.42), channel_id=1, source_target_pairs={{0,1},{1,0},{2,3},{3,2},{4,5},{5,4},{6,7},{7,6},{8,9},{9,8},{10,11... | collective-permute-start | bytes 12296 | tf_op jit(solution)/shard_map/ppermute | solution.py:600

commit v11 on v10

--- a/solution.py
+++ b/solution.py
@@ -25,7 +25,7 @@
 HBM = pl.BlockSpec(memory_space=pltpu.HBM)
 VM = pl.BlockSpec(memory_space=pltpu.VMEM)
 LIMIT = 32 * 1024 * 1024
-ORDER = (3, 4, 2, 0, 1)
+ORDER = (3, 0, 2, 1, 4)
 WHOLE = 64 * 1024 * 1024
 
 
@@ -94,15 +94,12 @@
         fh, fl = two_parts(viscosity * first.T)
         sh, sl = two_parts(viscosity * second.T)
         top = np.concatenate([fh, sh], 1)
-        return np.concatenate([top, top], 0), np.concatenate([fl, sl], 1)
+        return np.concatenate([top, top, np.concatenate([fl, sl], 1)], 0)
 
     def backward(first, second):
         fh, fl = two_parts(first)
         sh, sl = two_parts(second)
-        return (
-            np.concatenate([np.concatenate([fh, fl], 1), np.concatenate([sh, sl], 1)], 0),
-            np.concatenate([fh, sh], 0),
-        )
+        return np.concatenate([fh, sh, fh, sh, fl, sl], 0)
 
     def split_parity(mat):
         vectors = []
@@ -304,25 +301,23 @@
     return jnp.concatenate([ref[d, :, 128 * c : 128 * c + 128] for c in range(4)], 0)
 
 
-def two_dims(y, m_first, m_second, v_first, v_second, wf1, wf2, wb1, wb2):
+def two_dims(y, m_first, m_second, v_first, v_second, wf, wb):
     high, low = parts_of(y)
-    g = dot(jnp.concatenate([high, low], 1), wf1[...]) + dot(high, wf2[...])
+    g = dot(jnp.concatenate([high, low, high], 1), wf[...])
     high1, low1 = parts_of(m_first * g[:, :128] + v_first * y)
     high2, low2 = parts_of(m_second * g[:, 128:] + v_second * y)
-    wide = dot(jnp.concatenate([high1, high2], 1), wb1[...])
-    low = dot(jnp.concatenate([low1, low2], 1), wb2[...])
-    return wide[:, :128] + wide[:, 128:] + low
-
-
-def factors_of(met, vel, wb1, wb2, coef, q_out, plane_out, end_q, end_mv):
+    return dot(jnp.concatenate([high1, high2, low1, low2, high1, high2], 1), wb[...])
+
+
+def factors_of(met, vel, wb, coef, q_out, plane_out, end_q, end_mv):
     lane = iota(1)
     left = lane < 64
     for c in range(4):
         at = slice(128 * c, 128 * c + 128)
         w = met[1, :, at] * coef[32:33] + jnp.where(lane % 64 < 8, vel[1, :, at], 0.0)
         high, low = parts_of(w)
-        wide = dot(high, wb1[0:128])
-        q_out[:, at] = wide[:, :128] + wide[:, 128:] + dot(low, wb2[0:128])
+        along = [wb[start : start + 128] for start in (0, 256, 512)]
+        q_out[:, at] = dot(jnp.concatenate([high, low, high], 1), jnp.concatenate(along, 0))
 
     for n, (ref, d) in enumerate(((met, 0), (met, 2), (vel, 0), (vel, 2))):
         packed = jnp.zeros((E, 128), F32)
@@ -354,12 +349,12 @@
             end_mv[end, n] = ref[d, rows, at]
 
 
-def main_kernel(fields, x_ref, met, vel, keep_ref, wf1, wf2, wb1, wb2, coef, out, *factors):
+def main_kernel(fields, x_ref, met, vel, keep_ref, wf, wb, coef, out, *factors):
     lane, row = iota(1), iota(0)
     keep = keep_ref[...]
     left = lane < 64
     if factors:
-        factors_of(met, vel, wb1, wb2, coef, *factors)
+        factors_of(met, vel, wb, coef, *factors)
 
     xs = []
     for f in fields:
@@ -376,7 +371,7 @@
         jnp.concatenate([chunks_of(met, 2)] * count, 0),
         jnp.concatenate([chunks_of(vel, 1)] * count, 0),
         jnp.concatenate([chunks_of(vel, 2)] * count, 0),
-        wf1, wf2, wb1, wb2,
+        wf, wb,
     )
     for n, x in enumerate(xs):
         g0 = along_first(x, coef, 0)
@@ -434,7 +429,7 @@
             for shape in [(len(fields), E, 512)]
             + [(E, 512), (4, E, 128), (2, 4, 8, 128), (2, 4, 8, 128)] * factors
         ],
-        in_specs=[VM] * 9,
+        in_specs=[VM] * 7,
         out_specs=[VM] * (5 if factors else 1),
         compiler_params=pltpu.CompilerParams(vmem_limit_bytes=LIMIT),
         cost_estimate=pl.CostEstimate(
@@ -443,7 +438,7 @@
         name="inner",
     )(
         adjoint, metric, velocity, keep,
-        *tables["forward"], *tables["backward"], tables["coef"],
+        tables["forward"], tables["backward"], tables["coef"],
     )
 
 
@@ -484,7 +479,7 @@
 
 def post_kernel(
     a, b, own, c2, d, across, inside, base_a, base_b, q_ref, plane, end_q, end_mv,
-    wf1, wf2, wb1, wb2, spread, place, out_hbm, out, out_sems,
+    wf, wb, spread, place, out_hbm, out, out_sems,
 ):
     out_copies = [
         pltpu.make_async_copy(out.at[f], out_hbm.at[f], out_sems.at[f]) for f in range(5)
@@ -531,7 +526,7 @@
         )
         for n, at in enumerate((0, 1, 2, 3))
     ]
-    r = two_dims(stacked, *factors, wf1, wf2, wb1, wb2)
+    r = two_dims(stacked, *factors, wf, wb)
     ends = r[3 * E :]
     y_parts = jnp.concatenate(parts_of(stacked[: 3 * E]), 1)
     r_parts = jnp.concatenate(parts_of(r[: 3 * E]), 1)
@@ -563,13 +558,13 @@
     return pl.pallas_call(
         post_kernel,
         out_shape=jax.ShapeDtypeStruct((5, E, 512), F32),
-        in_specs=[VM] * 19,
+        in_specs=[VM] * 17,
         out_specs=HBM,
         scratch_shapes=[pltpu.VMEM((5, E, 512), F32), pltpu.SemaphoreType.DMA((5,))],
         compiler_params=pltpu.CompilerParams(vmem_limit_bytes=LIMIT),
         name="outer",
     )(
-        *parts, across, inside, *local, *tables["forward"], *tables["backward"],
+        *parts, across, inside, *local, tables["forward"], tables["backward"],
         tables["spread"], tables["place"],
     )
 

time: 23.2 us -> 26.1 us (1.12)
  waiting for transfers between devices: 0.08 us -> 3.1 us
    ppermute x4, waiting for transfers between devices: 0.08 us -> 3.1 us  [shards(): parts[n] = lax.ppermute(parts[n], 'dom', pairs)]
    unnamed x24 -> x20, local copies, waits for them, and re-layouts: 0.99 us -> 0.98 us
  transfers between devices with their start and end apart: 6 -> 6, of which waited for: 1 -> 1; matrix products, arithmetic and copies ran while one was open for 0% -> 0% of each run, Pallas kernels for 19% -> 17%
where the time goes in v11:
time: 26.1 us; the launch traced here: 25.9 us
  starting transfers between devices  11.9 us (46%)
  Pallas kernels  9.85 us (38%)
  waiting for transfers between devices  3.1 us (12%)
  local copies, waits for them, and re-layouts  0.98 us (4%)
    ppermute x4, starting transfers between devices, shards(): parts[n] = lax.ppermute(parts[n], 'dom', pairs)  8.12 us
    pallas_call x2, Pallas kernels, main_of(): pl.pallas_call(body, out_shape=[jax.ShapeDtypeStruct(shape, F32) for shap...  4.4 us
    ppermute x4, waiting for transfers between devices, shards(): parts[n] = lax.ppermute(parts[n], 'dom', pairs)  3.1 us
    ppermute x1, starting transfers between devices, shards(): inward = lax.ppermute(out_b, axes, inside)  2.95 us
    pallas_call x1, Pallas kernels, folded_of(): pl.pallas_call(fold_kernel, out_shape=jax.ShapeDtypeStruct((E + 32, 384),...  2.93 us
    pallas_call x1, Pallas kernels, post_of(): pl.pallas_call(post_kernel, out_shape=jax.ShapeDtypeStruct((5, E, 512), F...  2.09 us
    unnamed x20, local copies, waits for them, and re-layouts  0.98 us
    ppermute x1, starting transfers between devices, shards(): outward = lax.ppermute(out_a, axes, across)  0.78 us
  transfers between devices with their start and end apart: 6, of which 1 were waited for; matrix products, arithmetic and copies ran while one was open for 0% of the time, Pallas kernels for 17%

profile of v11, /device:TPU:0, one launch (start us, length us, event | category | flops | bytes accessed | tf_op | source)
XLA Modules:
  0.0 25.9 jit_solution(16369711879175168395)
XLA Ops:
  0.0 2.9 %fold.1.both = f32[160,384]{1,0:T(8,128)} custom-call(s32[1,128]{1,0:T(1,128)} %bitcast.15, s32[1,128]{1,0:T(1,128)} %bitcast.16, s32[1,128]{1,0:T(1,128)} %bitcast.17, s32[1,128]{1,0:T(1,128)} %bitcast.18, f32[5,128,512]{2,1,0:T(8,128)} %bitcast.8, bf16[256,512]{1,0:T(8,128)(2,1)} %constant.12.clone.fold_hbm), custom_call_target="tpu_custom_call" | custom-call | tf_op jit(solution)/shard_map/fold/pallas_call | solution.py:263
  2.9 0.0 copy-start.1
  3.0 0.9 %copy-done.1 = f32[160,384]{1,0:T(8,128)S(1)} copy-done((f32[160,384]{1,0:T(8,128)S(1)}, f32[160,384]{1,0:T(8,128)}, u32[]{:S(2)}) %copy-start.1) | copy-done | bytes 245784
  3.9 0.0 copy-start
  3.9 0.0 copy-start.5
  3.9 0.0 copy-start.6
  3.9 0.0 copy-start.7
  3.9 0.0 copy-start.8
  3.9 0.0 copy-start.9
  3.9 0.3 %sums.1 = (bf16[320,128]{1,0:T(8,128)(2,1)S(1)}, bf16[320,128]{1,0:T(8,128)(2,1)S(1)}, f32[320,128]{1,0:T(8,128)S(1)}, bf16[320,128]{1,0:T(8,128)(2,1)S(1)}, bf1...) custom-call(f32[160,384]{1,0:T(8,128)S(1)} %copy-done.1), custom_call_target="tpu_custom_call" | custom-call | flops 8000000000 | bytes 30000000 | tf_op jit(solution)/shard_map/sums/pallas_call | solution.py:405
  4.2 3.0 %collective-permute-start = (bf16[320,128]{1,0:T(8,128)(2,1)S(1)}, bf16[320,128]{1,0:T(8,128)(2,1)S(1)}, u32[]{:S(2)}, u32[]{:S(2)}) collective-permute-start(bf16[320,128]{1,0:T(8,128)(2,1)S(1)} %get-tuple-element.27), channel_id=1, source_target_pairs={{0,4},{4,8},{8,12},{12,16},{16,20},{20,24},{24,28},{28,0},{1,5},{5... | collective-permute-start | bytes 245768 | tf_op jit(solution)/shard_map/ppermute | solution.py:585
  7.2 3.6 %collective-permute-start.1 = (bf16[320,128]{1,0:T(8,128)(2,1)S(1)}, bf16[320,128]{1,0:T(8,128)(2,1)S(1)}, u32[]{:S(2)}, u32[]{:S(2)}) collective-permute-start(bf16[320,128]{1,0:T(8,128)(2,1)S(1)} %get-tuple-element.28), channel_id=1, source_target_pairs={{0,24},{4,28},{8,0},{12,4},{16,8},{20,12},{24,16},{28,20},{1,25},{... | collective-permute-start | bytes 245768 | tf_op jit(solution)/shard_map/ppermute | solution.py:585
  10.8 1.4 %collective-permute-start.2 = (bf16[320,128]{1,0:T(8,128)(2,1)S(1)}, bf16[320,128]{1,0:T(8,128)(2,1)S(1)}, u32[]{:S(2)}, u32[]{:S(2)}) collective-permute-start(bf16[320,128]{1,0:T(8,128)(2,1)S(1)} %get-tuple-element.30), channel_id=1, source_target_pairs={{0,28},{4,0},{8,4},{12,8},{16,12},{20,16},{24,20},{28,24},{1,29},{... | collective-permute-start | bytes 245768 | tf_op jit(solution)/shard_map/ppermute | solution.py:585
  12.2 0.1 collective-permute-start.3
  12.3 0.0 copy-done
  12.3 0.0 copy-done.5
  12.3 0.0 copy-done.6
  12.3 0.0 copy-done.7
  12.4 0.0 copy-done.8
  12.4 0.0 copy-done.9
  12.4 0.0 copy-start.2
  12.4 3.0 %inner.2 = (f32[3,128,512]{2,1,0:T(8,128)S(1)}, f32[128,512]{1,0:T(8,128)S(1)}, f32[4,128,128]{2,1,0:T(8,128)S(1)}, f32[2,4,8,128]{3,2,1,0:T(8,128)S(1)}, f32[2,4,8,128]{3,2,1,0:T(8,128)S(1)}) custom-call(f32[5,128,512]{2,1,0:T(8,128)S(1)} %bitcast.9, f32[3,128,512]{2,1,0:T(8,128)S(1)} %bitcast.11, f32[3,128,512]{2,1,0:T(8,128)S(1)} %bitcast.13, ...), custom_call_target="tpu_custom_call" | custom-call | flops 2400000000 | bytes 5000000 | tf_op jit(solution)/shard_map/inner/pallas_call | solution.py:425
  15.4 0.0 collective-permute-done.a
  15.4 0.0 collective-permute-done.1.b
  15.4 0.0 collective-permute-done.2.c.c2
  15.4 3.1 %collective-permute-done.3.d = bf16[320,128]{1,0:T(8,128)(2,1)S(1)} collective-permute-done((bf16[320,128]{1,0:T(8,128)(2,1)S(1)}, bf16[320,128]{1,0:T(8,128)(2,1)S(1)}, u32[]{:S(2)}, u32[]{:S(2)}) %collective-permute-start.3) | collective-permute-done | bytes 81952 | tf_op jit(solution)/shard_map/ppermute | solution.py:585
  18.5 0.0 copy-done.2
  18.5 0.1 lines.1
  18.6 0.0 copy-start.3
  18.6 0.0 copy-start.4
  18.6 0.8 %collective-permute-start.4 = (f32[8,128]{1,0:T(8,128)S(1)}, f32[8,128]{1,0:T(8,128)S(1)}, u32[]{:S(2)}, u32[]{:S(2)}) collective-permute-start(f32[8,128]{1,0:T(8,128)S(1)} %get-tuple-element.41), channel_id=1, source_target_pairs={{1,2},{2,1},{3,4},{4,3},{5,6},{6,5},{7,8},{8,7},{9,10},{10,9},{11,... | collective-permute-start | bytes 12296 | tf_op jit(solution)/shard_map/ppermute | solution.py:594
  19.4 2.9 %collective-permute-start.5 = (f32[8,128]{1,0:T(8,128)S(1)}, f32[8,128]{1,0:T(8,128)S(1)}, u32[]{:S(2)}, u32[]{:S(2)}) collective-permute-start(f32[8,128]{1,0:T(8,128)S(1)} %get-tuple-element.42), channel_id=1, source_target_pairs={{0,1},{1,0},{2,3},{3,2},{4,5},{5,4},{6,7},{7,6},{8,9},{9,8},{10,11... | collective-permute-start | bytes 12296 | tf_op jit(solution)/shard_map/ppermute | solution.py:595
  22.4 1.4 %inner.3.base_b = f32[2,128,512]{2,1,0:T(8,128)S(1)} custom-call(f32[5,128,512]{2,1,0:T(8,128)S(1)} %bitcast.10, f32[3,128,512]{2,1,0:T(8,128)S(1)} %bitcast.12, f32[3,128,512]{2,1,0:T(8,128)S(1)} %bitcast.14, f32[128,128]{1,0:T(8,128)S(1)} %get-tuple-element.44.refs_3_, bf16[384,256]{1,0:T(8,128)(2,1)S(1)} %copy-done.6, bf16[768,128]{1,0:T(8,128)(2,1)S(1)} %copy-done.5, ...), custom_call_target="tpu_custom_call" | custom-call | flops 1600000000 | bytes 5000000 | tf_op jit(solution)/shard_map/inner/pallas_call | solution.py:425
  23.8 0.0 collective-permute-done.4.across
  23.8 0.0 collective-permute-done.5.inside
  23.8 0.0 copy-done.3
  23.8 0.0 copy-done.4
  23.9 2.1 %outer.1 = f32[5,128,512]{2,1,0:T(8,128)} custom-call(bf16[320,128]{1,0:T(8,128)(2,1)S(1)} %collective-permute-done.a, bf16[320,128]{1,0:T(8,128)(2,1)S(1)} %collective-permute-done.1.b, f32[320,128]{1,0:T(8,128)S(1)} %get-tuple-element.36.own, bf16[320,128]{1,0:T(8,128)(2,1)S(1)} %collective-permute-done.2.c.c2, ...), custom_call_target="tpu_custom_call" | custom-call | tf_op jit(solution)/shard_map/outer/pallas_call | solution.py:558
Async XLA Ops:
  2.9 0.9 %copy-start.1 = (f32[160,384]{1,0:T(8,128)S(1)}, f32[160,384]{1,0:T(8,128)}, u32[]{:S(2)}) copy-start(f32[160,384]{1,0:T(8,128)} %fold.1.both) | copy-start | bytes 737284
  3.9 8.5 %copy-start = (f32[128,5,512]{2,0,1:T(8,128)S(1)}, f32[128,5,512]{2,0,1:T(8,128)}, u32[]{:S(2)}) copy-start(f32[128,5,512]{2,0,1:T(8,128)} %param.13) | copy-start | bytes 3932164
  3.9 8.5 %copy-start.5 = (bf16[768,128]{1,0:T(8,128)(2,1)S(1)}, bf16[768,128]{1,0:T(8,128)(2,1)}, u32[]{:S(2)}) copy-start(bf16[768,128]{1,0:T(8,128)(2,1)} %constant.14.clone.refs_5_.wb) | copy-start | bytes 589828
  3.9 8.5 %copy-start.6 = (bf16[384,256]{1,0:T(8,128)(2,1)S(1)}, bf16[384,256]{1,0:T(8,128)(2,1)}, u32[]{:S(2)}) copy-start(bf16[384,256]{1,0:T(8,128)(2,1)} %constant.13.clone.refs_4_.wf) | copy-start | bytes 589828
  3.9 8.5 %copy-start.7 = (f32[128,3,512]{2,0,1:T(8,128)S(1)}, f32[128,3,512]{2,0,1:T(8,128)}, u32[]{:S(2)}) copy-start(f32[128,3,512]{2,0,1:T(8,128)} %param.14) | copy-start | bytes 2359300
  3.9 8.5 %copy-start.8 = (f32[128,3,512]{2,0,1:T(8,128)S(1)}, f32[128,3,512]{2,0,1:T(8,128)}, u32[]{:S(2)}) copy-start(f32[128,3,512]{2,0,1:T(8,128)} %param.15) | copy-start | bytes 2359300
  3.9 8.5 %copy-start.9 = (f32[48,128]{1,0:T(8,128)S(1)}, f32[48,128]{1,0:T(8,128)}, u32[]{:S(2)}) copy-start(f32[48,128]{1,0:T(8,128)} %constant.15.clone.refs_6_) | copy-start | bytes 73732
  4.2 11.2 %collective-permute-start = (bf16[320,128]{1,0:T(8,128)(2,1)S(1)}, bf16[320,128]{1,0:T(8,128)(2,1)S(1)}, u32[]{:S(2)}, u32[]{:S(2)}) collective-permute-start(bf16[320,128]{1,0:T(8,128)(2,1)S(1)} %get-tuple-element.27), channel_id=1, source_target_pairs={{0,4},{4,8},{8,12},{12,16},{16,20},{20,24},{24,28},{28,0},{1,5},{5... | collective-permute-start | bytes 245768 | tf_op jit(solution)/shard_map/ppermute | solution.py:585
  7.2 8.2 %collective-permute-start.1 = (bf16[320,128]{1,0:T(8,128)(2,1)S(1)}, bf16[320,128]{1,0:T(8,128)(2,1)S(1)}, u32[]{:S(2)}, u32[]{:S(2)}) collective-permute-start(bf16[320,128]{1,0:T(8,128)(2,1)S(1)} %get-tuple-element.28), channel_id=1, source_target_pairs={{0,24},{4,28},{8,0},{12,4},{16,8},{20,12},{24,16},{28,20},{1,25},{... | collective-permute-start | bytes 245768 | tf_op jit(solution)/shard_map/ppermute | solution.py:585
  10.8 4.6 %collective-permute-start.2 = (bf16[320,128]{1,0:T(8,128)(2,1)S(1)}, bf16[320,128]{1,0:T(8,128)(2,1)S(1)}, u32[]{:S(2)}, u32[]{:S(2)}) collective-permute-start(bf16[320,128]{1,0:T(8,128)(2,1)S(1)} %get-tuple-element.30), channel_id=1, source_target_pairs={{0,28},{4,0},{8,4},{12,8},{16,12},{20,16},{24,20},{28,24},{1,29},{... | collective-permute-start | bytes 245768 | tf_op jit(solution)/shard_map/ppermute | solution.py:585
  12.2 6.2 %collective-permute-start.3 = (bf16[320,128]{1,0:T(8,128)(2,1)S(1)}, bf16[320,128]{1,0:T(8,128)(2,1)S(1)}, u32[]{:S(2)}, u32[]{:S(2)}) collective-permute-start(bf16[320,128]{1,0:T(8,128)(2,1)S(1)} %get-tuple-element.31), channel_id=1, source_target_pairs={{0,8},{4,12},{8,16},{12,20},{16,24},{20,28},{24,0},{28,4},{1,9},{5... | collective-permute-start | bytes 245768 | tf_op jit(solution)/shard_map/ppermute | solution.py:585
  12.4 6.1 %copy-start.2 = (f32[160,384]{1,0:T(8,128)S(1)}, f32[160,384]{1,0:T(8,128)}, u32[]{:S(2)}) copy-start(f32[160,384]{1,0:T(8,128)} %fold.1.both) | copy-start | bytes 737284
  18.6 5.2 %copy-start.3 = (bf16[256,1024]{1,0:T(8,128)(2,1)S(1)}, bf16[256,1024]{1,0:T(8,128)(2,1)}, u32[]{:S(2)}) copy-start(bf16[256,1024]{1,0:T(8,128)(2,1)} %constant.17.clone.place) | copy-start | bytes 1572868
  18.6 5.2 %copy-start.4 = (bf16[256,1024]{1,0:T(8,128)(2,1)S(1)}, bf16[256,1024]{1,0:T(8,128)(2,1)}, u32[]{:S(2)}) copy-start(bf16[256,1024]{1,0:T(8,128)(2,1)} %constant.16.clone.spread) | copy-start | bytes 1572868
  18.6 5.2 %collective-permute-start.4 = (f32[8,128]{1,0:T(8,128)S(1)}, f32[8,128]{1,0:T(8,128)S(1)}, u32[]{:S(2)}, u32[]{:S(2)}) collective-permute-start(f32[8,128]{1,0:T(8,128)S(1)} %get-tuple-element.41), channel_id=1, source_target_pairs={{1,2},{2,1},{3,4},{4,3},{5,6},{6,5},{7,8},{8,7},{9,10},{10,9},{11,... | collective-permute-start | bytes 12296 | tf_op jit(solution)/shard_map/ppermute | solution.py:594
  19.4 4.4 %collective-permute-start.5 = (f32[8,128]{1,0:T(8,128)S(1)}, f32[8,128]{1,0:T(8,128)S(1)}, u32[]{:S(2)}, u32[]{:S(2)}) collective-permute-start(f32[8,128]{1,0:T(8,128)S(1)} %get-tuple-element.42), channel_id=1, source_target_pairs={{0,1},{1,0},{2,3},{3,2},{4,5},{5,4},{6,7},{7,6},{8,9},{9,8},{10,11... | collective-permute-start | bytes 12296 | tf_op jit(solution)/shard_map/ppermute | solution.py:595

commit v12 on v10

--- a/solution.py
+++ b/solution.py
@@ -535,14 +535,18 @@
     ends = r[3 * E :]
     y_parts = jnp.concatenate(parts_of(stacked[: 3 * E]), 1)
     r_parts = jnp.concatenate(parts_of(r[: 3 * E]), 1)
-    for n in range(3):
-        rows = slice(E * n, E * n + E)
-        for f in range(2 * n, min(2 * n + 2, 5)):
-            cols = slice(512 * (f - 2 * n), 512 * (f - 2 * n) + 512)
+    for odd_field in range(2):
+        fields = range(odd_field, 5, 2)
+        rows = slice(0, E * len(fields))
+        cols = slice(512 * odd_field, 512 * odd_field + 512)
+        spread_y = dot(y_parts[rows], spread[:, cols])
+        placed_r = dot(r_parts[rows], place[:, cols])
+        for n, f in enumerate(fields):
+            rows = slice(E * n, E * n + E)
             out[f] = (
                 (base_a[f] if f < 3 else base_b[f - 3])
-                + q_ref[...] * dot(y_parts[rows], spread[:, cols])
-                + dot(r_parts[rows], place[:, cols])
+                + q_ref[...] * spread_y[rows]
+                + placed_r[rows]
             )
             for c in range(4):
                 at = slice(128 * c, 128 * c + 128)

time: 23.2 us -> 23.3 us (level)
  no operation moved by 1% of the time
where the time goes in v12:
time: 23.3 us; the launch traced here: 23 us
  starting transfers between devices  11.9 us (51%)
  Pallas kernels  9.77 us (42%)
  local copies, waits for them, and re-layouts  0.99 us (4%)
    ppermute x4, starting transfers between devices, shards(): parts[n] = lax.ppermute(parts[n], 'dom', pairs)  8.12 us
    pallas_call x2, Pallas kernels, main_of(): pl.pallas_call(body, out_shape=[jax.ShapeDtypeStruct(shape, F32) for shap...  4.43 us
    ppermute x1, starting transfers between devices, shards(): inward = lax.ppermute(out_b, axes, inside)  3.02 us
    pallas_call x1, Pallas kernels, folded_of(): pl.pallas_call(fold_kernel, out_shape=jax.ShapeDtypeStruct((E + 32, 384),...  2.93 us
    pallas_call x1, Pallas kernels, post_of(): pl.pallas_call(post_kernel, out_shape=jax.ShapeDtypeStruct((5, E, 512), F...  1.98 us
    unnamed x24, local copies, waits for them, and re-layouts  0.99 us
    ppermute x1, starting transfers between devices, shards(): outward = lax.ppermute(out_a, axes, across)  0.78 us
  transfers between devices with their start and end apart: 6, of which 1 were waited for; matrix products, arithmetic and copies ran while one was open for 0% of the time, Pallas kernels for 19%

profile of v12, /device:TPU:0, one launch (start us, length us, event | category | flops | bytes accessed | tf_op | source)
XLA Modules:
  0.0 23.0 jit_solution(1639224489377322328)
XLA Ops:
  0.0 2.9 %fold.1.both = f32[160,384]{1,0:T(8,128)} custom-call(s32[1,128]{1,0:T(1,128)} %bitcast.15, s32[1,128]{1,0:T(1,128)} %bitcast.16, s32[1,128]{1,0:T(1,128)} %bitcast.17, s32[1,128]{1,0:T(1,128)} %bitcast.18, f32[5,128,512]{2,1,0:T(8,128)} %bitcast.8, bf16[256,512]{1,0:T(8,128)(2,1)} %constant.16.clone.fold_hbm), custom_call_target="tpu_custom_call" | custom-call | tf_op jit(solution)/shard_map/fold/pallas_call | solution.py:266
  2.9 0.0 copy-start.1
  3.0 0.9 %copy-done.1 = f32[160,384]{1,0:T(8,128)S(1)} copy-done((f32[160,384]{1,0:T(8,128)S(1)}, f32[160,384]{1,0:T(8,128)}, u32[]{:S(2)}) %copy-start.1) | copy-done | bytes 245784
  3.9 0.0 copy-start
  3.9 0.0 copy-start.5
  3.9 0.0 copy-start.6
  3.9 0.0 copy-start.7
  3.9 0.0 copy-start.8
  3.9 0.0 copy-start.9
  3.9 0.0 copy-start.10
  3.9 0.0 copy-start.11
  3.9 0.3 %sums.1 = (bf16[320,128]{1,0:T(8,128)(2,1)S(1)}, bf16[320,128]{1,0:T(8,128)(2,1)S(1)}, f32[320,128]{1,0:T(8,128)S(1)}, bf16[320,128]{1,0:T(8,128)(2,1)S(1)}, bf1...) custom-call(f32[160,384]{1,0:T(8,128)S(1)} %copy-done.1), custom_call_target="tpu_custom_call" | custom-call | flops 8000000000 | bytes 30000000 | tf_op jit(solution)/shard_map/sums/pallas_call | solution.py:410
  4.2 3.0 %collective-permute-start = (bf16[320,128]{1,0:T(8,128)(2,1)S(1)}, bf16[320,128]{1,0:T(8,128)(2,1)S(1)}, u32[]{:S(2)}, u32[]{:S(2)}) collective-permute-start(bf16[320,128]{1,0:T(8,128)(2,1)S(1)} %get-tuple-element.27), channel_id=1, source_target_pairs={{0,4},{4,8},{8,12},{12,16},{16,20},{20,24},{24,28},{28,0},{1,5},{5... | collective-permute-start | bytes 245768 | tf_op jit(solution)/shard_map/ppermute | solution.py:594
  7.2 1.6 %collective-permute-start.1 = (bf16[320,128]{1,0:T(8,128)(2,1)S(1)}, bf16[320,128]{1,0:T(8,128)(2,1)S(1)}, u32[]{:S(2)}, u32[]{:S(2)}) collective-permute-start(bf16[320,128]{1,0:T(8,128)(2,1)S(1)} %get-tuple-element.28), channel_id=1, source_target_pairs={{0,8},{4,12},{8,16},{12,20},{16,24},{20,28},{24,0},{28,4},{1,9},{5... | collective-permute-start | bytes 245768 | tf_op jit(solution)/shard_map/ppermute | solution.py:594
  8.8 2.2 %collective-permute-start.2 = (bf16[320,128]{1,0:T(8,128)(2,1)S(1)}, bf16[320,128]{1,0:T(8,128)(2,1)S(1)}, u32[]{:S(2)}, u32[]{:S(2)}) collective-permute-start(bf16[320,128]{1,0:T(8,128)(2,1)S(1)} %get-tuple-element.30), channel_id=1, source_target_pairs={{0,24},{4,28},{8,0},{12,4},{16,8},{20,12},{24,16},{28,20},{1,25},{... | collective-permute-start | bytes 245768 | tf_op jit(solution)/shard_map/ppermute | solution.py:594
  11.1 1.3 %collective-permute-start.3 = (bf16[320,128]{1,0:T(8,128)(2,1)S(1)}, bf16[320,128]{1,0:T(8,128)(2,1)S(1)}, u32[]{:S(2)}, u32[]{:S(2)}) collective-permute-start(bf16[320,128]{1,0:T(8,128)(2,1)S(1)} %get-tuple-element.31), channel_id=1, source_target_pairs={{0,28},{4,0},{8,4},{12,8},{16,12},{20,16},{24,20},{28,24},{1,29},{... | collective-permute-start | bytes 245768 | tf_op jit(solution)/shard_map/ppermute | solution.py:594
  12.4 0.0 copy-done
  12.4 0.0 copy-done.5
  12.4 0.0 copy-done.6
  12.4 0.0 copy-done.7
  12.4 0.0 copy-done.8
  12.4 0.0 copy-done.9
  12.4 0.0 copy-done.10
  12.4 0.0 copy-done.11
  12.4 0.0 copy-start.2
  12.4 3.0 %inner.2 = (f32[3,128,512]{2,1,0:T(8,128)S(1)}, f32[128,512]{1,0:T(8,128)S(1)}, f32[4,128,128]{2,1,0:T(8,128)S(1)}, f32[2,4,8,128]{3,2,1,0:T(8,128)S(1)}, f32[2,4,8,128]{3,2,1,0:T(8,128)S(1)}) custom-call(f32[5,128,512]{2,1,0:T(8,128)S(1)} %bitcast.9, f32[3,128,512]{2,1,0:T(8,128)S(1)} %bitcast.11, f32[3,128,512]{2,1,0:T(8,128)S(1)} %bitcast.13, ...), custom_call_target="tpu_custom_call" | custom-call | flops 2400000000 | bytes 5000000 | tf_op jit(solution)/shard_map/inner/pallas_call | solution.py:430
  15.4 0.0 collective-permute-done.a
  15.4 0.0 collective-permute-done.1.b
  15.4 0.0 collective-permute-done.2.c.c2
  15.4 0.1 collective-permute-done.3.d
  15.5 0.0 copy-done.2
  15.5 0.1 lines.1
  15.6 0.0 copy-start.3
  15.6 0.0 copy-start.4
  15.6 0.8 %collective-permute-start.4 = (f32[8,128]{1,0:T(8,128)S(1)}, f32[8,128]{1,0:T(8,128)S(1)}, u32[]{:S(2)}, u32[]{:S(2)}) collective-permute-start(f32[8,128]{1,0:T(8,128)S(1)} %get-tuple-element.41), channel_id=1, source_target_pairs={{1,2},{2,1},{3,4},{4,3},{5,6},{6,5},{7,8},{8,7},{9,10},{10,9},{11,... | collective-permute-start | bytes 12296 | tf_op jit(solution)/shard_map/ppermute | solution.py:603
  16.4 3.0 %collective-permute-start.5 = (f32[8,128]{1,0:T(8,128)S(1)}, f32[8,128]{1,0:T(8,128)S(1)}, u32[]{:S(2)}, u32[]{:S(2)}) collective-permute-start(f32[8,128]{1,0:T(8,128)S(1)} %get-tuple-element.42), channel_id=1, source_target_pairs={{0,1},{1,0},{2,3},{3,2},{4,5},{5,4},{6,7},{7,6},{8,9},{9,8},{10,11... | collective-permute-start | bytes 12296 | tf_op jit(solution)/shard_map/ppermute | solution.py:604
  19.5 1.5 %inner.3.base_b = f32[2,128,512]{2,1,0:T(8,128)S(1)} custom-call(f32[5,128,512]{2,1,0:T(8,128)S(1)} %bitcast.10, f32[3,128,512]{2,1,0:T(8,128)S(1)} %bitcast.12, f32[3,128,512]{2,1,0:T(8,128)S(1)} %bitcast.14, f32[128,128]{1,0:T(8,128)S(1)} %get-tuple-element.44.refs_3_, bf16[256,256]{1,0:T(8,128)(2,1)S(1)} %copy-done.6, bf16[128,256]{1,0:T(8,128)(2,1)S(1)} %copy-done.8, ...), custom_call_target="tpu_custom_call" | custom-call | flops 1600000000 | bytes 5000000 | tf_op jit(solution)/shard_map/inner/pallas_call | solution.py:430
  20.9 0.0 collective-permute-done.4.across
  20.9 0.0 collective-permute-done.5.inside
  21.0 0.0 copy-done.3
  21.0 0.0 copy-done.4
  21.0 2.0 %outer.1 = f32[5,128,512]{2,1,0:T(8,128)} custom-call(bf16[320,128]{1,0:T(8,128)(2,1)S(1)} %collective-permute-done.a, bf16[320,128]{1,0:T(8,128)(2,1)S(1)} %collective-permute-done.1.b, f32[320,128]{1,0:T(8,128)S(1)} %get-tuple-element.36.own, bf16[320,128]{1,0:T(8,128)(2,1)S(1)} %collective-permute-done.2.c.c2, ...), custom_call_target="tpu_custom_call" | custom-call | tf_op jit(solution)/shard_map/outer/pallas_call | solution.py:567
Async XLA Ops:
  2.9 0.9 %copy-start.1 = (f32[160,384]{1,0:T(8,128)S(1)}, f32[160,384]{1,0:T(8,128)}, u32[]{:S(2)}) copy-start(f32[160,384]{1,0:T(8,128)} %fold.1.both) | copy-start | bytes 737284
  3.9 8.5 %copy-start = (f32[128,5,512]{2,0,1:T(8,128)S(1)}, f32[128,5,512]{2,0,1:T(8,128)}, u32[]{:S(2)}) copy-start(f32[128,5,512]{2,0,1:T(8,128)} %param.15) | copy-start | bytes 3932164
  3.9 8.5 %copy-start.5 = (bf16[256,256]{1,0:T(8,128)(2,1)S(1)}, bf16[256,256]{1,0:T(8,128)(2,1)}, u32[]{:S(2)}) copy-start(bf16[256,256]{1,0:T(8,128)(2,1)} %constant.19.clone.refs_6_.wb1) | copy-start | bytes 393220
  3.9 8.5 %copy-start.6 = (bf16[256,256]{1,0:T(8,128)(2,1)S(1)}, bf16[256,256]{1,0:T(8,128)(2,1)}, u32[]{:S(2)}) copy-start(bf16[256,256]{1,0:T(8,128)(2,1)} %constant.17.clone.refs_4_.wf1) | copy-start | bytes 393220
  3.9 8.5 %copy-start.7 = (bf16[256,128]{1,0:T(8,128)(2,1)S(1)}, bf16[256,128]{1,0:T(8,128)(2,1)}, u32[]{:S(2)}) copy-start(bf16[256,128]{1,0:T(8,128)(2,1)} %constant.20.clone.refs_7_.wb2) | copy-start | bytes 196612
  3.9 8.5 %copy-start.8 = (bf16[128,256]{1,0:T(8,128)(2,1)S(1)}, bf16[128,256]{1,0:T(8,128)(2,1)}, u32[]{:S(2)}) copy-start(bf16[128,256]{1,0:T(8,128)(2,1)} %constant.18.clone.refs_5_.wf2) | copy-start | bytes 196612
  3.9 8.5 %copy-start.9 = (f32[128,3,512]{2,0,1:T(8,128)S(1)}, f32[128,3,512]{2,0,1:T(8,128)}, u32[]{:S(2)}) copy-start(f32[128,3,512]{2,0,1:T(8,128)} %param.16) | copy-start | bytes 2359300
  3.9 8.5 %copy-start.10 = (f32[128,3,512]{2,0,1:T(8,128)S(1)}, f32[128,3,512]{2,0,1:T(8,128)}, u32[]{:S(2)}) copy-start(f32[128,3,512]{2,0,1:T(8,128)} %param.17) | copy-start | bytes 2359300
  3.9 8.5 %copy-start.11 = (f32[48,128]{1,0:T(8,128)S(1)}, f32[48,128]{1,0:T(8,128)}, u32[]{:S(2)}) copy-start(f32[48,128]{1,0:T(8,128)} %constant.21.clone.refs_8_) | copy-start | bytes 73732
  4.2 11.2 %collective-permute-start = (bf16[320,128]{1,0:T(8,128)(2,1)S(1)}, bf16[320,128]{1,0:T(8,128)(2,1)S(1)}, u32[]{:S(2)}, u32[]{:S(2)}) collective-permute-start(bf16[320,128]{1,0:T(8,128)(2,1)S(1)} %get-tuple-element.27), channel_id=1, source_target_pairs={{0,4},{4,8},{8,12},{12,16},{16,20},{20,24},{24,28},{28,0},{1,5},{5... | collective-permute-start | bytes 245768 | tf_op jit(solution)/shard_map/ppermute | solution.py:594
  7.2 8.2 %collective-permute-start.1 = (bf16[320,128]{1,0:T(8,128)(2,1)S(1)}, bf16[320,128]{1,0:T(8,128)(2,1)S(1)}, u32[]{:S(2)}, u32[]{:S(2)}) collective-permute-start(bf16[320,128]{1,0:T(8,128)(2,1)S(1)} %get-tuple-element.28), channel_id=1, source_target_pairs={{0,8},{4,12},{8,16},{12,20},{16,24},{20,28},{24,0},{28,4},{1,9},{5... | collective-permute-start | bytes 245768 | tf_op jit(solution)/shard_map/ppermute | solution.py:594
  8.8 6.6 %collective-permute-start.2 = (bf16[320,128]{1,0:T(8,128)(2,1)S(1)}, bf16[320,128]{1,0:T(8,128)(2,1)S(1)}, u32[]{:S(2)}, u32[]{:S(2)}) collective-permute-start(bf16[320,128]{1,0:T(8,128)(2,1)S(1)} %get-tuple-element.30), channel_id=1, source_target_pairs={{0,24},{4,28},{8,0},{12,4},{16,8},{20,12},{24,16},{28,20},{1,25},{... | collective-permute-start | bytes 245768 | tf_op jit(solution)/shard_map/ppermute | solution.py:594
  11.1 4.4 %collective-permute-start.3 = (bf16[320,128]{1,0:T(8,128)(2,1)S(1)}, bf16[320,128]{1,0:T(8,128)(2,1)S(1)}, u32[]{:S(2)}, u32[]{:S(2)}) collective-permute-start(bf16[320,128]{1,0:T(8,128)(2,1)S(1)} %get-tuple-element.31), channel_id=1, source_target_pairs={{0,28},{4,0},{8,4},{12,8},{16,12},{20,16},{24,20},{28,24},{1,29},{... | collective-permute-start | bytes 245768 | tf_op jit(solution)/shard_map/ppermute | solution.py:594
  12.4 3.1 %copy-start.2 = (f32[160,384]{1,0:T(8,128)S(1)}, f32[160,384]{1,0:T(8,128)}, u32[]{:S(2)}) copy-start(f32[160,384]{1,0:T(8,128)} %fold.1.both) | copy-start | bytes 737284
  15.6 5.3 %copy-start.3 = (bf16[256,1024]{1,0:T(8,128)(2,1)S(1)}, bf16[256,1024]{1,0:T(8,128)(2,1)}, u32[]{:S(2)}) copy-start(bf16[256,1024]{1,0:T(8,128)(2,1)} %constant.23.clone.place) | copy-start | bytes 1572868
  15.6 5.3 %copy-start.4 = (bf16[256,1024]{1,0:T(8,128)(2,1)S(1)}, bf16[256,1024]{1,0:T(8,128)(2,1)}, u32[]{:S(2)}) copy-start(bf16[256,1024]{1,0:T(8,128)(2,1)} %constant.22.clone.spread) | copy-start | bytes 1572868
  15.6 5.3 %collective-permute-start.4 = (f32[8,128]{1,0:T(8,128)S(1)}, f32[8,128]{1,0:T(8,128)S(1)}, u32[]{:S(2)}, u32[]{:S(2)}) collective-permute-start(f32[8,128]{1,0:T(8,128)S(1)} %get-tuple-element.41), channel_id=1, source_target_pairs={{1,2},{2,1},{3,4},{4,3},{5,6},{6,5},{7,8},{8,7},{9,10},{10,9},{11,... | collective-permute-start | bytes 12296 | tf_op jit(solution)/shard_map/ppermute | solution.py:603
  16.4 4.5 %collective-permute-start.5 = (f32[8,128]{1,0:T(8,128)S(1)}, f32[8,128]{1,0:T(8,128)S(1)}, u32[]{:S(2)}, u32[]{:S(2)}) collective-permute-start(f32[8,128]{1,0:T(8,128)S(1)} %get-tuple-element.42), channel_id=1, source_target_pairs={{0,1},{1,0},{2,3},{3,2},{4,5},{5,4},{6,7},{7,6},{8,9},{9,8},{10,11... | collective-permute-start | bytes 12296 | tf_op jit(solution)/shard_map/ppermute | solution.py:604

commit v13 on v10

--- a/solution.py
+++ b/solution.py
@@ -25,7 +25,7 @@
 HBM = pl.BlockSpec(memory_space=pltpu.HBM)
 VM = pl.BlockSpec(memory_space=pltpu.VMEM)
 LIMIT = 32 * 1024 * 1024
-ORDER = (3, 4, 2, 0, 1)
+ORDER = (4, 3, 2, 0, 1)
 WHOLE = 64 * 1024 * 1024
 
 

time: 23.2 us -> 23.5 us (1.013)
  waiting for transfers between devices: 0.08 us -> 0.63 us
    ppermute x4, waiting for transfers between devices: 0.08 us -> 0.62 us  [shards(): parts[n] = lax.ppermute(parts[n], 'dom', pairs)]
where the time goes in v13:
time: 23.5 us; the launch traced here: 23.3 us
  starting transfers between devices  11.8 us (50%)
  Pallas kernels  9.71 us (41%)
  local copies, waits for them, and re-layouts  0.99 us (4%)
  waiting for transfers between devices  0.63 us (3%)
    ppermute x4, starting transfers between devices, shards(): parts[n] = lax.ppermute(parts[n], 'dom', pairs)  8.1 us
    pallas_call x2, Pallas kernels, main_of(): pl.pallas_call(body, out_shape=[jax.ShapeDtypeStruct(shape, F32) for shap...  4.43 us
    ppermute x1, starting transfers between devices, shards(): inward = lax.ppermute(out_b, axes, inside)  2.95 us
    pallas_call x1, Pallas kernels, folded_of(): pl.pallas_call(fold_kernel, out_shape=jax.ShapeDtypeStruct((E + 32, 384),...  2.93 us
    pallas_call x1, Pallas kernels, post_of(): pl.pallas_call(post_kernel, out_shape=jax.ShapeDtypeStruct((5, E, 512), F...  1.92 us
    unnamed x24, local copies, waits for them, and re-layouts  0.99 us
    ppermute x1, starting transfers between devices, shards(): outward = lax.ppermute(out_a, axes, across)  0.78 us
    ppermute x4, waiting for transfers between devices, shards(): parts[n] = lax.ppermute(parts[n], 'dom', pairs)  0.62 us
  transfers between devices with their start and end apart: 6, of which 1 were waited for; matrix products, arithmetic and copies ran while one was open for 0% of the time, Pallas kernels for 19%

profile of v13, /device:TPU:0, one launch (start us, length us, event | category | flops | bytes accessed | tf_op | source)
XLA Modules:
  0.0 23.3 jit_solution(15788779942253528177)
XLA Ops:
  0.0 2.9 %fold.1.both = f32[160,384]{1,0:T(8,128)} custom-call(s32[1,128]{1,0:T(1,128)} %bitcast.15, s32[1,128]{1,0:T(1,128)} %bitcast.16, s32[1,128]{1,0:T(1,128)} %bitcast.17, s32[1,128]{1,0:T(1,128)} %bitcast.18, f32[5,128,512]{2,1,0:T(8,128)} %bitcast.8, bf16[256,512]{1,0:T(8,128)(2,1)} %constant.16.clone.fold_hbm), custom_call_target="tpu_custom_call" | custom-call | tf_op jit(solution)/shard_map/fold/pallas_call | solution.py:266
  2.9 0.0 copy-start.1
  3.0 0.9 %copy-done.1 = f32[160,384]{1,0:T(8,128)S(1)} copy-done((f32[160,384]{1,0:T(8,128)S(1)}, f32[160,384]{1,0:T(8,128)}, u32[]{:S(2)}) %copy-start.1) | copy-done | bytes 245784
  3.9 0.0 copy-start
  3.9 0.0 copy-start.5
  3.9 0.0 copy-start.6
  3.9 0.0 copy-start.7
  3.9 0.0 copy-start.8
  3.9 0.0 copy-start.9
  3.9 0.0 copy-start.10
  3.9 0.0 copy-start.11
  3.9 0.3 %sums.1 = (bf16[320,128]{1,0:T(8,128)(2,1)S(1)}, bf16[320,128]{1,0:T(8,128)(2,1)S(1)}, f32[320,128]{1,0:T(8,128)S(1)}, bf16[320,128]{1,0:T(8,128)(2,1)S(1)}, bf1...) custom-call(f32[160,384]{1,0:T(8,128)S(1)} %copy-done.1), custom_call_target="tpu_custom_call" | custom-call | flops 8000000000 | bytes 30000000 | tf_op jit(solution)/shard_map/sums/pallas_call | solution.py:410
  4.2 3.1 %collective-permute-start = (bf16[320,128]{1,0:T(8,128)(2,1)S(1)}, bf16[320,128]{1,0:T(8,128)(2,1)S(1)}, u32[]{:S(2)}, u32[]{:S(2)}) collective-permute-start(bf16[320,128]{1,0:T(8,128)(2,1)S(1)} %get-tuple-element.27), channel_id=1, source_target_pairs={{0,8},{4,12},{8,16},{12,20},{16,24},{20,28},{24,0},{28,4},{1,9},{5... | collective-permute-start | bytes 245768 | tf_op jit(solution)/shard_map/ppermute | solution.py:590
  7.3 1.5 %collective-permute-start.1 = (bf16[320,128]{1,0:T(8,128)(2,1)S(1)}, bf16[320,128]{1,0:T(8,128)(2,1)S(1)}, u32[]{:S(2)}, u32[]{:S(2)}) collective-permute-start(bf16[320,128]{1,0:T(8,128)(2,1)S(1)} %get-tuple-element.28), channel_id=1, source_target_pairs={{0,4},{4,8},{8,12},{12,16},{16,20},{20,24},{24,28},{28,0},{1,5},{5... | collective-permute-start | bytes 245768 | tf_op jit(solution)/shard_map/ppermute | solution.py:590
  8.8 2.2 %collective-permute-start.2 = (bf16[320,128]{1,0:T(8,128)(2,1)S(1)}, bf16[320,128]{1,0:T(8,128)(2,1)S(1)}, u32[]{:S(2)}, u32[]{:S(2)}) collective-permute-start(bf16[320,128]{1,0:T(8,128)(2,1)S(1)} %get-tuple-element.30), channel_id=1, source_target_pairs={{0,24},{4,28},{8,0},{12,4},{16,8},{20,12},{24,16},{28,20},{1,25},{... | collective-permute-start | bytes 245768 | tf_op jit(solution)/shard_map/ppermute | solution.py:590
  11.1 1.3 %collective-permute-start.3 = (bf16[320,128]{1,0:T(8,128)(2,1)S(1)}, bf16[320,128]{1,0:T(8,128)(2,1)S(1)}, u32[]{:S(2)}, u32[]{:S(2)}) collective-permute-start(bf16[320,128]{1,0:T(8,128)(2,1)S(1)} %get-tuple-element.31), channel_id=1, source_target_pairs={{0,28},{4,0},{8,4},{12,8},{16,12},{20,16},{24,20},{28,24},{1,29},{... | collective-permute-start | bytes 245768 | tf_op jit(solution)/shard_map/ppermute | solution.py:590
  12.3 0.0 copy-done
  12.3 0.0 copy-done.5
  12.3 0.0 copy-done.6
  12.3 0.0 copy-done.7
  12.3 0.0 copy-done.8
  12.4 0.0 copy-done.9
  12.4 0.0 copy-done.10
  12.4 0.0 copy-done.11
  12.4 0.0 copy-start.2
  12.4 3.0 %inner.2 = (f32[3,128,512]{2,1,0:T(8,128)S(1)}, f32[128,512]{1,0:T(8,128)S(1)}, f32[4,128,128]{2,1,0:T(8,128)S(1)}, f32[2,4,8,128]{3,2,1,0:T(8,128)S(1)}, f32[2,4,8,128]{3,2,1,0:T(8,128)S(1)}) custom-call(f32[5,128,512]{2,1,0:T(8,128)S(1)} %bitcast.9, f32[3,128,512]{2,1,0:T(8,128)S(1)} %bitcast.11, f32[3,128,512]{2,1,0:T(8,128)S(1)} %bitcast.13, ...), custom_call_target="tpu_custom_call" | custom-call | flops 2400000000 | bytes 5000000 | tf_op jit(solution)/shard_map/inner/pallas_call | solution.py:430
  15.4 0.0 collective-permute-done.a
  15.4 0.0 collective-permute-done.1.b
  15.4 0.0 collective-permute-done.2.c.c2
  15.4 0.6 %collective-permute-done.3.d = bf16[320,128]{1,0:T(8,128)(2,1)S(1)} collective-permute-done((bf16[320,128]{1,0:T(8,128)(2,1)S(1)}, bf16[320,128]{1,0:T(8,128)(2,1)S(1)}, u32[]{:S(2)}, u32[]{:S(2)}) %collective-permute-start.3) | collective-permute-done | bytes 81952 | tf_op jit(solution)/shard_map/ppermute | solution.py:590
  16.0 0.0 copy-done.2
  16.0 0.1 lines.1
  16.1 0.0 copy-start.3
  16.2 0.0 copy-start.4
  16.2 0.8 %collective-permute-start.4 = (f32[8,128]{1,0:T(8,128)S(1)}, f32[8,128]{1,0:T(8,128)S(1)}, u32[]{:S(2)}, u32[]{:S(2)}) collective-permute-start(f32[8,128]{1,0:T(8,128)S(1)} %get-tuple-element.41), channel_id=1, source_target_pairs={{1,2},{2,1},{3,4},{4,3},{5,6},{6,5},{7,8},{8,7},{9,10},{10,9},{11,... | collective-permute-start | bytes 12296 | tf_op jit(solution)/shard_map/ppermute | solution.py:599
  16.9 2.9 %collective-permute-start.5 = (f32[8,128]{1,0:T(8,128)S(1)}, f32[8,128]{1,0:T(8,128)S(1)}, u32[]{:S(2)}, u32[]{:S(2)}) collective-permute-start(f32[8,128]{1,0:T(8,128)S(1)} %get-tuple-element.42), channel_id=1, source_target_pairs={{0,1},{1,0},{2,3},{3,2},{4,5},{5,4},{6,7},{7,6},{8,9},{9,8},{10,11... | collective-permute-start | bytes 12296 | tf_op jit(solution)/shard_map/ppermute | solution.py:600
  19.9 1.5 %inner.3.base_b = f32[2,128,512]{2,1,0:T(8,128)S(1)} custom-call(f32[5,128,512]{2,1,0:T(8,128)S(1)} %bitcast.10, f32[3,128,512]{2,1,0:T(8,128)S(1)} %bitcast.12, f32[3,128,512]{2,1,0:T(8,128)S(1)} %bitcast.14, f32[128,128]{1,0:T(8,128)S(1)} %get-tuple-element.44.refs_3_, bf16[256,256]{1,0:T(8,128)(2,1)S(1)} %copy-done.6, bf16[128,256]{1,0:T(8,128)(2,1)S(1)} %copy-done.8, ...), custom_call_target="tpu_custom_call" | custom-call | flops 1600000000 | bytes 5000000 | tf_op jit(solution)/shard_map/inner/pallas_call | solution.py:430
  21.4 0.0 collective-permute-done.4.across
  21.4 0.0 collective-permute-done.5.inside
  21.4 0.0 copy-done.3
  21.4 0.0 copy-done.4
  21.4 1.9 %outer.1 = f32[5,128,512]{2,1,0:T(8,128)} custom-call(bf16[320,128]{1,0:T(8,128)(2,1)S(1)} %collective-permute-done.a, bf16[320,128]{1,0:T(8,128)(2,1)S(1)} %collective-permute-done.1.b, f32[320,128]{1,0:T(8,128)S(1)} %get-tuple-element.36.own, bf16[320,128]{1,0:T(8,128)(2,1)S(1)} %collective-permute-done.2.c.c2, ...), custom_call_target="tpu_custom_call" | custom-call | tf_op jit(solution)/shard_map/outer/pallas_call | solution.py:563
Async XLA Ops:
  2.9 0.9 %copy-start.1 = (f32[160,384]{1,0:T(8,128)S(1)}, f32[160,384]{1,0:T(8,128)}, u32[]{:S(2)}) copy-start(f32[160,384]{1,0:T(8,128)} %fold.1.both) | copy-start | bytes 737284
  3.9 8.5 %copy-start = (f32[128,5,512]{2,0,1:T(8,128)S(1)}, f32[128,5,512]{2,0,1:T(8,128)}, u32[]{:S(2)}) copy-start(f32[128,5,512]{2,0,1:T(8,128)} %param.15) | copy-start | bytes 3932164
  3.9 8.5 %copy-start.5 = (bf16[256,256]{1,0:T(8,128)(2,1)S(1)}, bf16[256,256]{1,0:T(8,128)(2,1)}, u32[]{:S(2)}) copy-start(bf16[256,256]{1,0:T(8,128)(2,1)} %constant.19.clone.refs_6_.wb1) | copy-start | bytes 393220
  3.9 8.5 %copy-start.6 = (bf16[256,256]{1,0:T(8,128)(2,1)S(1)}, bf16[256,256]{1,0:T(8,128)(2,1)}, u32[]{:S(2)}) copy-start(bf16[256,256]{1,0:T(8,128)(2,1)} %constant.17.clone.refs_4_.wf1) | copy-start | bytes 393220
  3.9 8.5 %copy-start.7 = (bf16[256,128]{1,0:T(8,128)(2,1)S(1)}, bf16[256,128]{1,0:T(8,128)(2,1)}, u32[]{:S(2)}) copy-start(bf16[256,128]{1,0:T(8,128)(2,1)} %constant.20.clone.refs_7_.wb2) | copy-start | bytes 196612
  3.9 8.5 %copy-start.8 = (bf16[128,256]{1,0:T(8,128)(2,1)S(1)}, bf16[128,256]{1,0:T(8,128)(2,1)}, u32[]{:S(2)}) copy-start(bf16[128,256]{1,0:T(8,128)(2,1)} %constant.18.clone.refs_5_.wf2) | copy-start | bytes 196612
  3.9 8.5 %copy-start.9 = (f32[128,3,512]{2,0,1:T(8,128)S(1)}, f32[128,3,512]{2,0,1:T(8,128)}, u32[]{:S(2)}) copy-start(f32[128,3,512]{2,0,1:T(8,128)} %param.16) | copy-start | bytes 2359300
  3.9 8.4 %copy-start.10 = (f32[128,3,512]{2,0,1:T(8,128)S(1)}, f32[128,3,512]{2,0,1:T(8,128)}, u32[]{:S(2)}) copy-start(f32[128,3,512]{2,0,1:T(8,128)} %param.17) | copy-start | bytes 2359300
  3.9 8.4 %copy-start.11 = (f32[48,128]{1,0:T(8,128)S(1)}, f32[48,128]{1,0:T(8,128)}, u32[]{:S(2)}) copy-start(f32[48,128]{1,0:T(8,128)} %constant.21.clone.refs_8_) | copy-start | bytes 73732
  4.2 11.1 %collective-permute-start = (bf16[320,128]{1,0:T(8,128)(2,1)S(1)}, bf16[320,128]{1,0:T(8,128)(2,1)S(1)}, u32[]{:S(2)}, u32[]{:S(2)}) collective-permute-start(bf16[320,128]{1,0:T(8,128)(2,1)S(1)} %get-tuple-element.27), channel_id=1, source_target_pairs={{0,8},{4,12},{8,16},{12,20},{16,24},{20,28},{24,0},{28,4},{1,9},{5... | collective-permute-start | bytes 245768 | tf_op jit(solution)/shard_map/ppermute | solution.py:590
  7.3 8.1 %collective-permute-start.1 = (bf16[320,128]{1,0:T(8,128)(2,1)S(1)}, bf16[320,128]{1,0:T(8,128)(2,1)S(1)}, u32[]{:S(2)}, u32[]{:S(2)}) collective-permute-start(bf16[320,128]{1,0:T(8,128)(2,1)S(1)} %get-tuple-element.28), channel_id=1, source_target_pairs={{0,4},{4,8},{8,12},{12,16},{16,20},{20,24},{24,28},{28,0},{1,5},{5... | collective-permute-start | bytes 245768 | tf_op jit(solution)/shard_map/ppermute | solution.py:590
  8.8 6.6 %collective-permute-start.2 = (bf16[320,128]{1,0:T(8,128)(2,1)S(1)}, bf16[320,128]{1,0:T(8,128)(2,1)S(1)}, u32[]{:S(2)}, u32[]{:S(2)}) collective-permute-start(bf16[320,128]{1,0:T(8,128)(2,1)S(1)} %get-tuple-element.30), channel_id=1, source_target_pairs={{0,24},{4,28},{8,0},{12,4},{16,8},{20,12},{24,16},{28,20},{1,25},{... | collective-permute-start | bytes 245768 | tf_op jit(solution)/shard_map/ppermute | solution.py:590
  11.1 4.9 %collective-permute-start.3 = (bf16[320,128]{1,0:T(8,128)(2,1)S(1)}, bf16[320,128]{1,0:T(8,128)(2,1)S(1)}, u32[]{:S(2)}, u32[]{:S(2)}) collective-permute-start(bf16[320,128]{1,0:T(8,128)(2,1)S(1)} %get-tuple-element.31), channel_id=1, source_target_pairs={{0,28},{4,0},{8,4},{12,8},{16,12},{20,16},{24,20},{28,24},{1,29},{... | collective-permute-start | bytes 245768 | tf_op jit(solution)/shard_map/ppermute | solution.py:590
  12.4 3.6 %copy-start.2 = (f32[160,384]{1,0:T(8,128)S(1)}, f32[160,384]{1,0:T(8,128)}, u32[]{:S(2)}) copy-start(f32[160,384]{1,0:T(8,128)} %fold.1.both) | copy-start | bytes 737284
  16.1 5.2 %copy-start.3 = (bf16[256,1024]{1,0:T(8,128)(2,1)S(1)}, bf16[256,1024]{1,0:T(8,128)(2,1)}, u32[]{:S(2)}) copy-start(bf16[256,1024]{1,0:T(8,128)(2,1)} %constant.23.clone.place) | copy-start | bytes 1572868
  16.2 5.2 %copy-start.4 = (bf16[256,1024]{1,0:T(8,128)(2,1)S(1)}, bf16[256,1024]{1,0:T(8,128)(2,1)}, u32[]{:S(2)}) copy-start(bf16[256,1024]{1,0:T(8,128)(2,1)} %constant.22.clone.spread) | copy-start | bytes 1572868
  16.2 5.2 %collective-permute-start.4 = (f32[8,128]{1,0:T(8,128)S(1)}, f32[8,128]{1,0:T(8,128)S(1)}, u32[]{:S(2)}, u32[]{:S(2)}) collective-permute-start(f32[8,128]{1,0:T(8,128)S(1)} %get-tuple-element.41), channel_id=1, source_target_pairs={{1,2},{2,1},{3,4},{4,3},{5,6},{6,5},{7,8},{8,7},{9,10},{10,9},{11,... | collective-permute-start | bytes 12296 | tf_op jit(solution)/shard_map/ppermute | solution.py:599
  16.9 4.4 %collective-permute-start.5 = (f32[8,128]{1,0:T(8,128)S(1)}, f32[8,128]{1,0:T(8,128)S(1)}, u32[]{:S(2)}, u32[]{:S(2)}) collective-permute-start(f32[8,128]{1,0:T(8,128)S(1)} %get-tuple-element.42), channel_id=1, source_target_pairs={{0,1},{1,0},{2,3},{3,2},{4,5},{5,4},{6,7},{7,6},{8,9},{9,8},{10,11... | collective-permute-start | bytes 12296 | tf_op jit(solution)/shard_map/ppermute | solution.py:600

commit v14 on v10

--- a/solution.py
+++ b/solution.py
@@ -199,7 +199,7 @@
     route_hbm, target_hbm, code_hbm, hang_hbm, adj_hbm, fold_hbm, *refs
 ):
     out, ints, x, fold, wide, sems = refs
-    faces_out, edges_out = out.at[0:E], out.at[E : E + 32, 0:128]
+    edges_out = out.at[320:352]
     peers = lax.axis_size("dom")
     copies = fetch(
         [(ref, ints.at[n]) for n, ref in enumerate((route_hbm, target_hbm, code_hbm, hang_hbm))]
@@ -239,9 +239,9 @@
                 marked == 2.0 * q, mapped[E * f : E * f + E, 128 * q : 128 * q + 128], 0.0
             )
         faces.append(total + pltpu.roll(total, 64, 1))
-    faces_out[:, 0:128] = jnp.where(left, faces[0], faces[1])
-    faces_out[:, 128:256] = jnp.where(left, faces[2], faces[3])
-    faces_out[:, 256:384] = faces[4]
+    out[0:128] = jnp.where(left, faces[0], faces[1])
+    out[128:256] = jnp.where(left, faces[2], faces[3])
+    out[256:320] = jnp.where(left[:64], faces[4][:64], faces[4][64:])
 
     edges_out[...] = jnp.zeros((32, 128), F32)
     edges_out[16:17] = (slot * E + target).astype(F32)
@@ -265,7 +265,7 @@
 def folded_of(route, target, code, hang, adjoint, fold):
     return pl.pallas_call(
         fold_kernel,
-        out_shape=jax.ShapeDtypeStruct((E + 32, 384), F32),
+        out_shape=jax.ShapeDtypeStruct((352, 128), F32),
         in_specs=[HBM] * 6,
         out_specs=VM,
         scratch_shapes=[
@@ -391,13 +391,17 @@
 
 
 def sum_kernel(both, *outs):
-    faces, edges = both.at[0:E], both.at[E : E + 32, 0:128]
+    edges = both.at[320:352]
+    last = both[256:320]
+    last = jnp.concatenate([last, swap(last)], 0)
+    last = jnp.where(iota(1) < 64, last, swap(last))
+    faces = jnp.concatenate([both[0:128], both[128:256], last], 1).astype(BF16)
     column = jnp.where(iota(0) == iota(1), edges[17:18], 0.0).astype(BF16)
     column = dot(column, jnp.ones((E, 128), BF16))
     outs[5][...] = jnp.where(iota(1) % 64 >= 56, column, 1.0)
     spot = edges[16:17].astype(jnp.int32)
     hit = (iota(0, (5 * E, E)) == spot).astype(F32).astype(BF16)
-    sums = dot(hit, faces[...].astype(BF16))
+    sums = dot(hit, faces)
     left = iota(1, (64, 128)) < 64
     for ref, o in zip(outs, ORDER):
         mine = sums[o * E : o * E + E]
@@ -453,7 +457,7 @@
 
 
 def line_kernel(a, b, own, c, d, both, across, inside):
-    edges = both.at[E : E + 32, 0:128]
+    edges = both.at[320:352]
     def rows(start):
         return sum(ref[start : start + 16].astype(F32) for ref in (a, b, own, c, d))
 

time: 23.2 us -> 23.3 us (level)
  no operation moved by 1% of the time
where the time goes in v14:
time: 23.3 us; the launch traced here: 22.9 us
  starting transfers between devices  11.9 us (51%)
  Pallas kernels  9.74 us (42%)
  local copies, waits for them, and re-layouts  0.97 us (4%)
    ppermute x4, starting transfers between devices, shards(): parts[n] = lax.ppermute(parts[n], 'dom', pairs)  8.12 us
    pallas_call x2, Pallas kernels, main_of(): pl.pallas_call(body, out_shape=[jax.ShapeDtypeStruct(shape, F32) for shap...  4.4 us
    ppermute x1, starting transfers between devices, shards(): inward = lax.ppermute(out_b, axes, inside)  3.01 us
    pallas_call x1, Pallas kernels, folded_of(): pl.pallas_call(fold_kernel, out_shape=jax.ShapeDtypeStruct((352, 128), F3...  2.91 us
    pallas_call x1, Pallas kernels, post_of(): pl.pallas_call(post_kernel, out_shape=jax.ShapeDtypeStruct((5, E, 512), F...  1.93 us
    unnamed x24, local copies, waits for them, and re-layouts  0.97 us
    ppermute x1, starting transfers between devices, shards(): outward = lax.ppermute(out_a, axes, across)  0.78 us
  transfers between devices with their start and end apart: 6, of which 1 were waited for; matrix products, arithmetic and copies ran while one was open for 0% of the time, Pallas kernels for 19%

profile of v14, /device:TPU:0, one launch (start us, length us, event | category | flops | bytes accessed | tf_op | source)
XLA Modules:
  0.0 22.9 jit_solution(15232193800869955229)
XLA Ops:
  0.0 2.9 %fold.1.both = f32[352,128]{1,0:T(8,128)} custom-call(s32[1,128]{1,0:T(1,128)} %bitcast.15, s32[1,128]{1,0:T(1,128)} %bitcast.16, s32[1,128]{1,0:T(1,128)} %bitcast.17, s32[1,128]{1,0:T(1,128)} %bitcast.18, f32[5,128,512]{2,1,0:T(8,128)} %bitcast.8, bf16[256,512]{1,0:T(8,128)(2,1)} %constant.16.clone.fold_hbm), custom_call_target="tpu_custom_call" | custom-call | tf_op jit(solution)/shard_map/fold/pallas_call | solution.py:266
  2.9 0.0 copy-start.1
  2.9 0.9 %copy-done.1 = f32[352,128]{1,0:T(8,128)S(1)} copy-done((f32[352,128]{1,0:T(8,128)S(1)}, f32[352,128]{1,0:T(8,128)}, u32[]{:S(2)}) %copy-start.1) | copy-done | bytes 180248
  3.8 0.0 copy-start
  3.8 0.0 copy-start.5
  3.9 0.0 copy-start.6
  3.9 0.0 copy-start.7
  3.9 0.0 copy-start.8
  3.9 0.0 copy-start.9
  3.9 0.0 copy-start.10
  3.9 0.0 copy-start.11
  3.9 0.4 %sums.1 = (bf16[320,128]{1,0:T(8,128)(2,1)S(1)}, bf16[320,128]{1,0:T(8,128)(2,1)S(1)}, f32[320,128]{1,0:T(8,128)S(1)}, bf16[320,128]{1,0:T(8,128)(2,1)S(1)}, bf1...) custom-call(f32[352,128]{1,0:T(8,128)S(1)} %copy-done.1), custom_call_target="tpu_custom_call" | custom-call | flops 8000000000 | bytes 30000000 | tf_op jit(solution)/shard_map/sums/pallas_call | solution.py:414
  4.3 3.0 %collective-permute-start = (bf16[320,128]{1,0:T(8,128)(2,1)S(1)}, bf16[320,128]{1,0:T(8,128)(2,1)S(1)}, u32[]{:S(2)}, u32[]{:S(2)}) collective-permute-start(bf16[320,128]{1,0:T(8,128)(2,1)S(1)} %get-tuple-element.27), channel_id=1, source_target_pairs={{0,4},{4,8},{8,12},{12,16},{16,20},{20,24},{24,28},{28,0},{1,5},{5... | collective-permute-start | bytes 245768 | tf_op jit(solution)/shard_map/ppermute | solution.py:594
  7.3 1.6 %collective-permute-start.1 = (bf16[320,128]{1,0:T(8,128)(2,1)S(1)}, bf16[320,128]{1,0:T(8,128)(2,1)S(1)}, u32[]{:S(2)}, u32[]{:S(2)}) collective-permute-start(bf16[320,128]{1,0:T(8,128)(2,1)S(1)} %get-tuple-element.28), channel_id=1, source_target_pairs={{0,8},{4,12},{8,16},{12,20},{16,24},{20,28},{24,0},{28,4},{1,9},{5... | collective-permute-start | bytes 245768 | tf_op jit(solution)/shard_map/ppermute | solution.py:594
  8.8 2.2 %collective-permute-start.2 = (bf16[320,128]{1,0:T(8,128)(2,1)S(1)}, bf16[320,128]{1,0:T(8,128)(2,1)S(1)}, u32[]{:S(2)}, u32[]{:S(2)}) collective-permute-start(bf16[320,128]{1,0:T(8,128)(2,1)S(1)} %get-tuple-element.30), channel_id=1, source_target_pairs={{0,24},{4,28},{8,0},{12,4},{16,8},{20,12},{24,16},{28,20},{1,25},{... | collective-permute-start | bytes 245768 | tf_op jit(solution)/shard_map/ppermute | solution.py:594
  11.1 1.3 %collective-permute-start.3 = (bf16[320,128]{1,0:T(8,128)(2,1)S(1)}, bf16[320,128]{1,0:T(8,128)(2,1)S(1)}, u32[]{:S(2)}, u32[]{:S(2)}) collective-permute-start(bf16[320,128]{1,0:T(8,128)(2,1)S(1)} %get-tuple-element.31), channel_id=1, source_target_pairs={{0,28},{4,0},{8,4},{12,8},{16,12},{20,16},{24,20},{28,24},{1,29},{... | collective-permute-start | bytes 245768 | tf_op jit(solution)/shard_map/ppermute | solution.py:594
  12.4 0.0 copy-done
  12.4 0.0 copy-done.5
  12.4 0.0 copy-done.6
  12.4 0.0 copy-done.7
  12.4 0.0 copy-done.8
  12.4 0.0 copy-done.9
  12.4 0.0 copy-done.10
  12.4 0.0 copy-done.11
  12.4 0.0 copy-start.2
  12.5 2.9 %inner.2 = (f32[3,128,512]{2,1,0:T(8,128)S(1)}, f32[128,512]{1,0:T(8,128)S(1)}, f32[4,128,128]{2,1,0:T(8,128)S(1)}, f32[2,4,8,128]{3,2,1,0:T(8,128)S(1)}, f32[2,4,8,128]{3,2,1,0:T(8,128)S(1)}) custom-call(f32[5,128,512]{2,1,0:T(8,128)S(1)} %bitcast.9, f32[3,128,512]{2,1,0:T(8,128)S(1)} %bitcast.11, f32[3,128,512]{2,1,0:T(8,128)S(1)} %bitcast.13, ...), custom_call_target="tpu_custom_call" | custom-call | flops 2400000000 | bytes 5000000 | tf_op jit(solution)/shard_map/inner/pallas_call | solution.py:434
  15.4 0.0 collective-permute-done.a
  15.4 0.0 collective-permute-done.1.b
  15.4 0.0 collective-permute-done.2.c.c2
  15.4 0.1 collective-permute-done.3.d
  15.5 0.0 copy-done.2
  15.5 0.1 lines.1
  15.7 0.0 copy-start.3
  15.7 0.0 copy-start.4
  15.7 0.8 %collective-permute-start.4 = (f32[8,128]{1,0:T(8,128)S(1)}, f32[8,128]{1,0:T(8,128)S(1)}, u32[]{:S(2)}, u32[]{:S(2)}) collective-permute-start(f32[8,128]{1,0:T(8,128)S(1)} %get-tuple-element.41), channel_id=1, source_target_pairs={{1,2},{2,1},{3,4},{4,3},{5,6},{6,5},{7,8},{8,7},{9,10},{10,9},{11,... | collective-permute-start | bytes 12296 | tf_op jit(solution)/shard_map/ppermute | solution.py:603
  16.5 3.0 %collective-permute-start.5 = (f32[8,128]{1,0:T(8,128)S(1)}, f32[8,128]{1,0:T(8,128)S(1)}, u32[]{:S(2)}, u32[]{:S(2)}) collective-permute-start(f32[8,128]{1,0:T(8,128)S(1)} %get-tuple-element.42), channel_id=1, source_target_pairs={{0,1},{1,0},{2,3},{3,2},{4,5},{5,4},{6,7},{7,6},{8,9},{9,8},{10,11... | collective-permute-start | bytes 12296 | tf_op jit(solution)/shard_map/ppermute | solution.py:604
  19.5 1.5 %inner.3.base_b = f32[2,128,512]{2,1,0:T(8,128)S(1)} custom-call(f32[5,128,512]{2,1,0:T(8,128)S(1)} %bitcast.10, f32[3,128,512]{2,1,0:T(8,128)S(1)} %bitcast.12, f32[3,128,512]{2,1,0:T(8,128)S(1)} %bitcast.14, f32[128,128]{1,0:T(8,128)S(1)} %get-tuple-element.44.refs_3_, bf16[256,256]{1,0:T(8,128)(2,1)S(1)} %copy-done.6, bf16[128,256]{1,0:T(8,128)(2,1)S(1)} %copy-done.8, ...), custom_call_target="tpu_custom_call" | custom-call | flops 1600000000 | bytes 5000000 | tf_op jit(solution)/shard_map/inner/pallas_call | solution.py:434
  20.9 0.0 collective-permute-done.4.across
  21.0 0.0 collective-permute-done.5.inside
  21.0 0.0 copy-done.3
  21.0 0.0 copy-done.4
  21.0 1.9 %outer.1 = f32[5,128,512]{2,1,0:T(8,128)} custom-call(bf16[320,128]{1,0:T(8,128)(2,1)S(1)} %collective-permute-done.a, bf16[320,128]{1,0:T(8,128)(2,1)S(1)} %collective-permute-done.1.b, f32[320,128]{1,0:T(8,128)S(1)} %get-tuple-element.36.own, bf16[320,128]{1,0:T(8,128)(2,1)S(1)} %collective-permute-done.2.c.c2, ...), custom_call_target="tpu_custom_call" | custom-call | tf_op jit(solution)/shard_map/outer/pallas_call | solution.py:567
Async XLA Ops:
  2.9 0.9 %copy-start.1 = (f32[352,128]{1,0:T(8,128)S(1)}, f32[352,128]{1,0:T(8,128)}, u32[]{:S(2)}) copy-start(f32[352,128]{1,0:T(8,128)} %fold.1.both) | copy-start | bytes 540676
  3.8 8.6 %copy-start = (f32[128,5,512]{2,0,1:T(8,128)S(1)}, f32[128,5,512]{2,0,1:T(8,128)}, u32[]{:S(2)}) copy-start(f32[128,5,512]{2,0,1:T(8,128)} %param.15) | copy-start | bytes 3932164
  3.8 8.6 %copy-start.5 = (bf16[256,256]{1,0:T(8,128)(2,1)S(1)}, bf16[256,256]{1,0:T(8,128)(2,1)}, u32[]{:S(2)}) copy-start(bf16[256,256]{1,0:T(8,128)(2,1)} %constant.19.clone.refs_6_.wb1) | copy-start | bytes 393220
  3.9 8.6 %copy-start.6 = (bf16[256,256]{1,0:T(8,128)(2,1)S(1)}, bf16[256,256]{1,0:T(8,128)(2,1)}, u32[]{:S(2)}) copy-start(bf16[256,256]{1,0:T(8,128)(2,1)} %constant.17.clone.refs_4_.wf1) | copy-start | bytes 393220
  3.9 8.6 %copy-start.7 = (bf16[256,128]{1,0:T(8,128)(2,1)S(1)}, bf16[256,128]{1,0:T(8,128)(2,1)}, u32[]{:S(2)}) copy-start(bf16[256,128]{1,0:T(8,128)(2,1)} %constant.20.clone.refs_7_.wb2) | copy-start | bytes 196612
  3.9 8.6 %copy-start.8 = (bf16[128,256]{1,0:T(8,128)(2,1)S(1)}, bf16[128,256]{1,0:T(8,128)(2,1)}, u32[]{:S(2)}) copy-start(bf16[128,256]{1,0:T(8,128)(2,1)} %constant.18.clone.refs_5_.wf2) | copy-start | bytes 196612
  3.9 8.6 %copy-start.9 = (f32[128,3,512]{2,0,1:T(8,128)S(1)}, f32[128,3,512]{2,0,1:T(8,128)}, u32[]{:S(2)}) copy-start(f32[128,3,512]{2,0,1:T(8,128)} %param.16) | copy-start | bytes 2359300
  3.9 8.5 %copy-start.10 = (f32[128,3,512]{2,0,1:T(8,128)S(1)}, f32[128,3,512]{2,0,1:T(8,128)}, u32[]{:S(2)}) copy-start(f32[128,3,512]{2,0,1:T(8,128)} %param.17) | copy-start | bytes 2359300
  3.9 8.5 %copy-start.11 = (f32[48,128]{1,0:T(8,128)S(1)}, f32[48,128]{1,0:T(8,128)}, u32[]{:S(2)}) copy-start(f32[48,128]{1,0:T(8,128)} %constant.21.clone.refs_8_) | copy-start | bytes 73732
  4.3 11.1 %collective-permute-start = (bf16[320,128]{1,0:T(8,128)(2,1)S(1)}, bf16[320,128]{1,0:T(8,128)(2,1)S(1)}, u32[]{:S(2)}, u32[]{:S(2)}) collective-permute-start(bf16[320,128]{1,0:T(8,128)(2,1)S(1)} %get-tuple-element.27), channel_id=1, source_target_pairs={{0,4},{4,8},{8,12},{12,16},{16,20},{20,24},{24,28},{28,0},{1,5},{5... | collective-permute-start | bytes 245768 | tf_op jit(solution)/shard_map/ppermute | solution.py:594
  7.3 8.2 %collective-permute-start.1 = (bf16[320,128]{1,0:T(8,128)(2,1)S(1)}, bf16[320,128]{1,0:T(8,128)(2,1)S(1)}, u32[]{:S(2)}, u32[]{:S(2)}) collective-permute-start(bf16[320,128]{1,0:T(8,128)(2,1)S(1)} %get-tuple-element.28), channel_id=1, source_target_pairs={{0,8},{4,12},{8,16},{12,20},{16,24},{20,28},{24,0},{28,4},{1,9},{5... | collective-permute-start | bytes 245768 | tf_op jit(solution)/shard_map/ppermute | solution.py:594
  8.8 6.6 %collective-permute-start.2 = (bf16[320,128]{1,0:T(8,128)(2,1)S(1)}, bf16[320,128]{1,0:T(8,128)(2,1)S(1)}, u32[]{:S(2)}, u32[]{:S(2)}) collective-permute-start(bf16[320,128]{1,0:T(8,128)(2,1)S(1)} %get-tuple-element.30), channel_id=1, source_target_pairs={{0,24},{4,28},{8,0},{12,4},{16,8},{20,12},{24,16},{28,20},{1,25},{... | collective-permute-start | bytes 245768 | tf_op jit(solution)/shard_map/ppermute | solution.py:594
  11.1 4.4 %collective-permute-start.3 = (bf16[320,128]{1,0:T(8,128)(2,1)S(1)}, bf16[320,128]{1,0:T(8,128)(2,1)S(1)}, u32[]{:S(2)}, u32[]{:S(2)}) collective-permute-start(bf16[320,128]{1,0:T(8,128)(2,1)S(1)} %get-tuple-element.31), channel_id=1, source_target_pairs={{0,28},{4,0},{8,4},{12,8},{16,12},{20,16},{24,20},{28,24},{1,29},{... | collective-permute-start | bytes 245768 | tf_op jit(solution)/shard_map/ppermute | solution.py:594
  12.4 3.1 %copy-start.2 = (f32[352,128]{1,0:T(8,128)S(1)}, f32[352,128]{1,0:T(8,128)}, u32[]{:S(2)}) copy-start(f32[352,128]{1,0:T(8,128)} %fold.1.both) | copy-start | bytes 540676
  15.7 5.3 %copy-start.3 = (bf16[256,1024]{1,0:T(8,128)(2,1)S(1)}, bf16[256,1024]{1,0:T(8,128)(2,1)}, u32[]{:S(2)}) copy-start(bf16[256,1024]{1,0:T(8,128)(2,1)} %constant.23.clone.place) | copy-start | bytes 1572868
  15.7 5.3 %copy-start.4 = (bf16[256,1024]{1,0:T(8,128)(2,1)S(1)}, bf16[256,1024]{1,0:T(8,128)(2,1)}, u32[]{:S(2)}) copy-start(bf16[256,1024]{1,0:T(8,128)(2,1)} %constant.22.clone.spread) | copy-start | bytes 1572868
  15.7 5.3 %collective-permute-start.4 = (f32[8,128]{1,0:T(8,128)S(1)}, f32[8,128]{1,0:T(8,128)S(1)}, u32[]{:S(2)}, u32[]{:S(2)}) collective-permute-start(f32[8,128]{1,0:T(8,128)S(1)} %get-tuple-element.41), channel_id=1, source_target_pairs={{1,2},{2,1},{3,4},{4,3},{5,6},{6,5},{7,8},{8,7},{9,10},{10,9},{11,... | collective-permute-start | bytes 12296 | tf_op jit(solution)/shard_map/ppermute | solution.py:603
  16.5 4.5 %collective-permute-start.5 = (f32[8,128]{1,0:T(8,128)S(1)}, f32[8,128]{1,0:T(8,128)S(1)}, u32[]{:S(2)}, u32[]{:S(2)}) collective-permute-start(f32[8,128]{1,0:T(8,128)S(1)} %get-tuple-element.42), channel_id=1, source_target_pairs={{0,1},{1,0},{2,3},{3,2},{4,5},{5,4},{6,7},{7,6},{8,9},{9,8},{10,11... | collective-permute-start | bytes 12296 | tf_op jit(solution)/shard_map/ppermute | solution.py:604

commit v15 on v14

--- a/solution.py
+++ b/solution.py
@@ -202,12 +202,11 @@
     edges_out = out.at[320:352]
     peers = lax.axis_size("dom")
     copies = fetch(
-        [(ref, ints.at[n]) for n, ref in enumerate((route_hbm, target_hbm, code_hbm, hang_hbm))]
-        + [(adj_hbm.at[f], x.at[f]) for f in range(5)]
-        + [(fold_hbm, fold)],
+        [(adj_hbm, x), (fold_hbm, fold)]
+        + [(ref, ints.at[n]) for n, ref in enumerate((route_hbm, target_hbm, code_hbm, hang_hbm))],
         sems,
     )
-    for copy in copies[:4]:
+    for copy in copies[2:]:
         copy.wait()
     route, target, code, hang = (ints[n] for n in range(4))
     lane = iota(1)
@@ -216,7 +215,7 @@
     marked = down(jnp.where(hang == 1, code, -2)) - (lane // 64).astype(F32)
     odd = lane % 16 >= 8
     group = (lane // 16 + 1) % 4
-    for copy in copies[4:]:
+    for copy in copies[:2]:
         copy.wait()
     for f in range(5):
         packed = jnp.zeros((E, 128), F32)

time: 23.3 us -> 23.2 us (level)
  no operation moved by 1% of the time
where the time goes in v15:
time: 23.2 us; the launch traced here: 22.9 us
  starting transfers between devices  11.9 us (51%)
  Pallas kernels  9.73 us (42%)
  local copies, waits for them, and re-layouts  0.97 us (4%)
    ppermute x4, starting transfers between devices, shards(): parts[n] = lax.ppermute(parts[n], 'dom', pairs)  8.12 us
    pallas_call x2, Pallas kernels, main_of(): pl.pallas_call(body, out_shape=[jax.ShapeDtypeStruct(shape, F32) for shap...  4.4 us
    ppermute x1, starting transfers between devices, shards(): inward = lax.ppermute(out_b, axes, inside)  3.01 us
    pallas_call x1, Pallas kernels, folded_of(): pl.pallas_call(fold_kernel, out_shape=jax.ShapeDtypeStruct((352, 128), F3...  2.89 us
    pallas_call x1, Pallas kernels, post_of(): pl.pallas_call(post_kernel, out_shape=jax.ShapeDtypeStruct((5, E, 512), F...  1.93 us
    unnamed x24, local copies, waits for them, and re-layouts  0.97 us
    ppermute x1, starting transfers between devices, shards(): outward = lax.ppermute(out_a, axes, across)  0.78 us
  transfers between devices with their start and end apart: 6, of which 1 were waited for; matrix products, arithmetic and copies ran while one was open for 0% of the time, Pallas kernels for 19%

profile of v15, /device:TPU:0, one launch (start us, length us, event | category | flops | bytes accessed | tf_op | source)
XLA Modules:
  0.0 22.9 jit_solution(3708757899026818129)
XLA Ops:
  0.0 2.9 %fold.1.both = f32[352,128]{1,0:T(8,128)} custom-call(s32[1,128]{1,0:T(1,128)} %bitcast.15, s32[1,128]{1,0:T(1,128)} %bitcast.16, s32[1,128]{1,0:T(1,128)} %bitcast.17, s32[1,128]{1,0:T(1,128)} %bitcast.18, f32[5,128,512]{2,1,0:T(8,128)} %bitcast.8, bf16[256,512]{1,0:T(8,128)(2,1)} %constant.16.clone.fold_hbm), custom_call_target="tpu_custom_call" | custom-call | tf_op jit(solution)/shard_map/fold/pallas_call | solution.py:265
  2.9 0.0 copy-start.1
  2.9 0.9 %copy-done.1 = f32[352,128]{1,0:T(8,128)S(1)} copy-done((f32[352,128]{1,0:T(8,128)S(1)}, f32[352,128]{1,0:T(8,128)}, u32[]{:S(2)}) %copy-start.1) | copy-done | bytes 180248
  3.8 0.0 copy-start
  3.8 0.0 copy-start.5
  3.8 0.0 copy-start.6
  3.8 0.0 copy-start.7
  3.8 0.0 copy-start.8
  3.9 0.0 copy-start.9
  3.9 0.0 copy-start.10
  3.9 0.0 copy-start.11
  3.9 0.4 %sums.1 = (bf16[320,128]{1,0:T(8,128)(2,1)S(1)}, bf16[320,128]{1,0:T(8,128)(2,1)S(1)}, f32[320,128]{1,0:T(8,128)S(1)}, bf16[320,128]{1,0:T(8,128)(2,1)S(1)}, bf1...) custom-call(f32[352,128]{1,0:T(8,128)S(1)} %copy-done.1), custom_call_target="tpu_custom_call" | custom-call | flops 8000000000 | bytes 30000000 | tf_op jit(solution)/shard_map/sums/pallas_call | solution.py:413
  4.3 3.0 %collective-permute-start = (bf16[320,128]{1,0:T(8,128)(2,1)S(1)}, bf16[320,128]{1,0:T(8,128)(2,1)S(1)}, u32[]{:S(2)}, u32[]{:S(2)}) collective-permute-start(bf16[320,128]{1,0:T(8,128)(2,1)S(1)} %get-tuple-element.27), channel_id=1, source_target_pairs={{0,4},{4,8},{8,12},{12,16},{16,20},{20,24},{24,28},{28,0},{1,5},{5... | collective-permute-start | bytes 245768 | tf_op jit(solution)/shard_map/ppermute | solution.py:593
  7.2 1.6 %collective-permute-start.1 = (bf16[320,128]{1,0:T(8,128)(2,1)S(1)}, bf16[320,128]{1,0:T(8,128)(2,1)S(1)}, u32[]{:S(2)}, u32[]{:S(2)}) collective-permute-start(bf16[320,128]{1,0:T(8,128)(2,1)S(1)} %get-tuple-element.28), channel_id=1, source_target_pairs={{0,8},{4,12},{8,16},{12,20},{16,24},{20,28},{24,0},{28,4},{1,9},{5... | collective-permute-start | bytes 245768 | tf_op jit(solution)/shard_map/ppermute | solution.py:593
  8.8 2.2 %collective-permute-start.2 = (bf16[320,128]{1,0:T(8,128)(2,1)S(1)}, bf16[320,128]{1,0:T(8,128)(2,1)S(1)}, u32[]{:S(2)}, u32[]{:S(2)}) collective-permute-start(bf16[320,128]{1,0:T(8,128)(2,1)S(1)} %get-tuple-element.30), channel_id=1, source_target_pairs={{0,24},{4,28},{8,0},{12,4},{16,8},{20,12},{24,16},{28,20},{1,25},{... | collective-permute-start | bytes 245768 | tf_op jit(solution)/shard_map/ppermute | solution.py:593
  11.1 1.3 %collective-permute-start.3 = (bf16[320,128]{1,0:T(8,128)(2,1)S(1)}, bf16[320,128]{1,0:T(8,128)(2,1)S(1)}, u32[]{:S(2)}, u32[]{:S(2)}) collective-permute-start(bf16[320,128]{1,0:T(8,128)(2,1)S(1)} %get-tuple-element.31), channel_id=1, source_target_pairs={{0,28},{4,0},{8,4},{12,8},{16,12},{20,16},{24,20},{28,24},{1,29},{... | collective-permute-start | bytes 245768 | tf_op jit(solution)/shard_map/ppermute | solution.py:593
  12.4 0.0 copy-done
  12.4 0.0 copy-done.5
  12.4 0.0 copy-done.6
  12.4 0.0 copy-done.7
  12.4 0.0 copy-done.8
  12.4 0.0 copy-done.9
  12.4 0.0 copy-done.10
  12.4 0.0 copy-done.11
  12.4 0.0 copy-start.2
  12.4 2.9 %inner.2 = (f32[3,128,512]{2,1,0:T(8,128)S(1)}, f32[128,512]{1,0:T(8,128)S(1)}, f32[4,128,128]{2,1,0:T(8,128)S(1)}, f32[2,4,8,128]{3,2,1,0:T(8,128)S(1)}, f32[2,4,8,128]{3,2,1,0:T(8,128)S(1)}) custom-call(f32[5,128,512]{2,1,0:T(8,128)S(1)} %bitcast.9, f32[3,128,512]{2,1,0:T(8,128)S(1)} %bitcast.11, f32[3,128,512]{2,1,0:T(8,128)S(1)} %bitcast.13, ...), custom_call_target="tpu_custom_call" | custom-call | flops 2400000000 | bytes 5000000 | tf_op jit(solution)/shard_map/inner/pallas_call | solution.py:433
  15.4 0.0 collective-permute-done.a
  15.4 0.0 collective-permute-done.1.b
  15.4 0.0 collective-permute-done.2.c.c2
  15.4 0.1 collective-permute-done.3.d
  15.5 0.0 copy-done.2
  15.5 0.1 lines.1
  15.7 0.0 copy-start.3
  15.7 0.0 copy-start.4
  15.7 0.8 %collective-permute-start.4 = (f32[8,128]{1,0:T(8,128)S(1)}, f32[8,128]{1,0:T(8,128)S(1)}, u32[]{:S(2)}, u32[]{:S(2)}) collective-permute-start(f32[8,128]{1,0:T(8,128)S(1)} %get-tuple-element.41), channel_id=1, source_target_pairs={{1,2},{2,1},{3,4},{4,3},{5,6},{6,5},{7,8},{8,7},{9,10},{10,9},{11,... | collective-permute-start | bytes 12296 | tf_op jit(solution)/shard_map/ppermute | solution.py:602
  16.5 3.0 %collective-permute-start.5 = (f32[8,128]{1,0:T(8,128)S(1)}, f32[8,128]{1,0:T(8,128)S(1)}, u32[]{:S(2)}, u32[]{:S(2)}) collective-permute-start(f32[8,128]{1,0:T(8,128)S(1)} %get-tuple-element.42), channel_id=1, source_target_pairs={{0,1},{1,0},{2,3},{3,2},{4,5},{5,4},{6,7},{7,6},{8,9},{9,8},{10,11... | collective-permute-start | bytes 12296 | tf_op jit(solution)/shard_map/ppermute | solution.py:603
  19.5 1.5 %inner.3.base_b = f32[2,128,512]{2,1,0:T(8,128)S(1)} custom-call(f32[5,128,512]{2,1,0:T(8,128)S(1)} %bitcast.10, f32[3,128,512]{2,1,0:T(8,128)S(1)} %bitcast.12, f32[3,128,512]{2,1,0:T(8,128)S(1)} %bitcast.14, f32[128,128]{1,0:T(8,128)S(1)} %get-tuple-element.44.refs_3_, bf16[256,256]{1,0:T(8,128)(2,1)S(1)} %copy-done.6, bf16[128,256]{1,0:T(8,128)(2,1)S(1)} %copy-done.8, ...), custom_call_target="tpu_custom_call" | custom-call | flops 1600000000 | bytes 5000000 | tf_op jit(solution)/shard_map/inner/pallas_call | solution.py:433
  20.9 0.0 collective-permute-done.4.across
  20.9 0.0 collective-permute-done.5.inside
  20.9 0.0 copy-done.3
  21.0 0.0 copy-done.4
  21.0 1.9 %outer.1 = f32[5,128,512]{2,1,0:T(8,128)} custom-call(bf16[320,128]{1,0:T(8,128)(2,1)S(1)} %collective-permute-done.a, bf16[320,128]{1,0:T(8,128)(2,1)S(1)} %collective-permute-done.1.b, f32[320,128]{1,0:T(8,128)S(1)} %get-tuple-element.36.own, bf16[320,128]{1,0:T(8,128)(2,1)S(1)} %collective-permute-done.2.c.c2, ...), custom_call_target="tpu_custom_call" | custom-call | tf_op jit(solution)/shard_map/outer/pallas_call | solution.py:566
Async XLA Ops:
  2.9 0.9 %copy-start.1 = (f32[352,128]{1,0:T(8,128)S(1)}, f32[352,128]{1,0:T(8,128)}, u32[]{:S(2)}) copy-start(f32[352,128]{1,0:T(8,128)} %fold.1.both) | copy-start | bytes 540676
  3.8 8.6 %copy-start = (f32[128,5,512]{2,0,1:T(8,128)S(1)}, f32[128,5,512]{2,0,1:T(8,128)}, u32[]{:S(2)}) copy-start(f32[128,5,512]{2,0,1:T(8,128)} %param.15) | copy-start | bytes 3932164
  3.8 8.6 %copy-start.5 = (bf16[256,256]{1,0:T(8,128)(2,1)S(1)}, bf16[256,256]{1,0:T(8,128)(2,1)}, u32[]{:S(2)}) copy-start(bf16[256,256]{1,0:T(8,128)(2,1)} %constant.19.clone.refs_6_.wb1) | copy-start | bytes 393220
  3.8 8.6 %copy-start.6 = (bf16[256,256]{1,0:T(8,128)(2,1)S(1)}, bf16[256,256]{1,0:T(8,128)(2,1)}, u32[]{:S(2)}) copy-start(bf16[256,256]{1,0:T(8,128)(2,1)} %constant.17.clone.refs_4_.wf1) | copy-start | bytes 393220
  3.8 8.6 %copy-start.7 = (bf16[256,128]{1,0:T(8,128)(2,1)S(1)}, bf16[256,128]{1,0:T(8,128)(2,1)}, u32[]{:S(2)}) copy-start(bf16[256,128]{1,0:T(8,128)(2,1)} %constant.20.clone.refs_7_.wb2) | copy-start | bytes 196612
  3.8 8.6 %copy-start.8 = (bf16[128,256]{1,0:T(8,128)(2,1)S(1)}, bf16[128,256]{1,0:T(8,128)(2,1)}, u32[]{:S(2)}) copy-start(bf16[128,256]{1,0:T(8,128)(2,1)} %constant.18.clone.refs_5_.wf2) | copy-start | bytes 196612
  3.9 8.6 %copy-start.9 = (f32[128,3,512]{2,0,1:T(8,128)S(1)}, f32[128,3,512]{2,0,1:T(8,128)}, u32[]{:S(2)}) copy-start(f32[128,3,512]{2,0,1:T(8,128)} %param.16) | copy-start | bytes 2359300
  3.9 8.5 %copy-start.10 = (f32[128,3,512]{2,0,1:T(8,128)S(1)}, f32[128,3,512]{2,0,1:T(8,128)}, u32[]{:S(2)}) copy-start(f32[128,3,512]{2,0,1:T(8,128)} %param.17) | copy-start | bytes 2359300
  3.9 8.5 %copy-start.11 = (f32[48,128]{1,0:T(8,128)S(1)}, f32[48,128]{1,0:T(8,128)}, u32[]{:S(2)}) copy-start(f32[48,128]{1,0:T(8,128)} %constant.21.clone.refs_8_) | copy-start | bytes 73732
  4.3 11.1 %collective-permute-start = (bf16[320,128]{1,0:T(8,128)(2,1)S(1)}, bf16[320,128]{1,0:T(8,128)(2,1)S(1)}, u32[]{:S(2)}, u32[]{:S(2)}) collective-permute-start(bf16[320,128]{1,0:T(8,128)(2,1)S(1)} %get-tuple-element.27), channel_id=1, source_target_pairs={{0,4},{4,8},{8,12},{12,16},{16,20},{20,24},{24,28},{28,0},{1,5},{5... | collective-permute-start | bytes 245768 | tf_op jit(solution)/shard_map/ppermute | solution.py:593
  7.2 8.2 %collective-permute-start.1 = (bf16[320,128]{1,0:T(8,128)(2,1)S(1)}, bf16[320,128]{1,0:T(8,128)(2,1)S(1)}, u32[]{:S(2)}, u32[]{:S(2)}) collective-permute-start(bf16[320,128]{1,0:T(8,128)(2,1)S(1)} %get-tuple-element.28), channel_id=1, source_target_pairs={{0,8},{4,12},{8,16},{12,20},{16,24},{20,28},{24,0},{28,4},{1,9},{5... | collective-permute-start | bytes 245768 | tf_op jit(solution)/shard_map/ppermute | solution.py:593
  8.8 6.6 %collective-permute-start.2 = (bf16[320,128]{1,0:T(8,128)(2,1)S(1)}, bf16[320,128]{1,0:T(8,128)(2,1)S(1)}, u32[]{:S(2)}, u32[]{:S(2)}) collective-permute-start(bf16[320,128]{1,0:T(8,128)(2,1)S(1)} %get-tuple-element.30), channel_id=1, source_target_pairs={{0,24},{4,28},{8,0},{12,4},{16,8},{20,12},{24,16},{28,20},{1,25},{... | collective-permute-start | bytes 245768 | tf_op jit(solution)/shard_map/ppermute | solution.py:593
  11.1 4.4 %collective-permute-start.3 = (bf16[320,128]{1,0:T(8,128)(2,1)S(1)}, bf16[320,128]{1,0:T(8,128)(2,1)S(1)}, u32[]{:S(2)}, u32[]{:S(2)}) collective-permute-start(bf16[320,128]{1,0:T(8,128)(2,1)S(1)} %get-tuple-element.31), channel_id=1, source_target_pairs={{0,28},{4,0},{8,4},{12,8},{16,12},{20,16},{24,20},{28,24},{1,29},{... | collective-permute-start | bytes 245768 | tf_op jit(solution)/shard_map/ppermute | solution.py:593
  12.4 3.1 %copy-start.2 = (f32[352,128]{1,0:T(8,128)S(1)}, f32[352,128]{1,0:T(8,128)}, u32[]{:S(2)}) copy-start(f32[352,128]{1,0:T(8,128)} %fold.1.both) | copy-start | bytes 540676
  15.7 5.3 %copy-start.3 = (bf16[256,1024]{1,0:T(8,128)(2,1)S(1)}, bf16[256,1024]{1,0:T(8,128)(2,1)}, u32[]{:S(2)}) copy-start(bf16[256,1024]{1,0:T(8,128)(2,1)} %constant.23.clone.place) | copy-start | bytes 1572868
  15.7 5.3 %copy-start.4 = (bf16[256,1024]{1,0:T(8,128)(2,1)S(1)}, bf16[256,1024]{1,0:T(8,128)(2,1)}, u32[]{:S(2)}) copy-start(bf16[256,1024]{1,0:T(8,128)(2,1)} %constant.22.clone.spread) | copy-start | bytes 1572868
  15.7 5.3 %collective-permute-start.4 = (f32[8,128]{1,0:T(8,128)S(1)}, f32[8,128]{1,0:T(8,128)S(1)}, u32[]{:S(2)}, u32[]{:S(2)}) collective-permute-start(f32[8,128]{1,0:T(8,128)S(1)} %get-tuple-element.41), channel_id=1, source_target_pairs={{1,2},{2,1},{3,4},{4,3},{5,6},{6,5},{7,8},{8,7},{9,10},{10,9},{11,... | collective-permute-start | bytes 12296 | tf_op jit(solution)/shard_map/ppermute | solution.py:602
  16.5 4.5 %collective-permute-start.5 = (f32[8,128]{1,0:T(8,128)S(1)}, f32[8,128]{1,0:T(8,128)S(1)}, u32[]{:S(2)}, u32[]{:S(2)}) collective-permute-start(f32[8,128]{1,0:T(8,128)S(1)} %get-tuple-element.42), channel_id=1, source_target_pairs={{0,1},{1,0},{2,3},{3,2},{4,5},{5,4},{6,7},{7,6},{8,9},{9,8},{10,11... | collective-permute-start | bytes 12296 | tf_op jit(solution)/shard_map/ppermute | solution.py:603
